TPU v7x, 32 devices: a whole 2x2x4 slice. The times are simulated.
32 devices in a mesh: groups: 2 (over y), blk: 4 (over z), sub: 2 (over x), pair: 2 (over core).
Axes of the slice: x: 2, y: 2, z: 4, core: 2. Of those that a mesh axis runs over, the one named last changes fastest.
Arguments:
- resid: bfloat16 [512, 8192], P(('groups', 'blk'), ('sub', 'pair')), parts along dimension 0, may hold values from -6 to 6
- context: bfloat16 [512, 8192], P('groups', 'blk'), parts along dimension 0, may hold values from -6 to 6
- w_out: bfloat16 [8192, 8192], P('blk', ('sub', 'pair')), may hold values from -0.0625 to 0.0625
- w_in: bfloat16 [8192, 14336], P(('sub', 'pair'), 'blk'), may hold values from -0.0625 to 0.0625
- w_down: bfloat16 [14336, 8192], P('blk', ('sub', 'pair')), may hold values from -0.046875 to 0.046875
- scales: float32 [3], replicated, may hold values from 0.5 to 2
Outputs:
- result: bfloat16 [512, 8192], P(('groups', 'blk'), ('sub', 'pair')), parts along dimension 0
There are 2 independent parts, one for each index of `groups`. A program takes and returns all parts, laid end to end along the dimension named above; an argument that names none is the same for every part. Nothing has to cross between parts.
All inputs are finite; a program needn't handle non-finite values.
Results may differ from a plain program's by a relative error of at most 0.025.
Values may be sent and summed in bfloat16 or wider, within the bound.
No kernel may reach another device: no remote copies, remote signals or barrier semaphores. Data moves between devices by JAX's collectives and lax.ppermute only.
A program may use at most 128 MiB of HBM per device.

v0:
```python
import jax
import jax.numpy as jnp
from jax import lax
from jax.sharding import PartitionSpec as P


def local(resid, context, w_out, w_in, w_down, scales):
    picked = context
    attn = lax.psum_scatter(
        jnp.dot(picked, w_out, preferred_element_type=jnp.float32).astype(jnp.bfloat16),
        "blk",
        scatter_dimension=0,
        tiled=True,
    ).astype(jnp.float32)
    mixed = (resid.astype(jnp.float32) + scales[0] * attn).astype(jnp.bfloat16)
    pre_terms = jnp.dot(
        lax.all_gather(mixed, "blk", axis=0, tiled=True), w_in, preferred_element_type=jnp.float32
    )
    pre_part = lax.psum_scatter(
        pre_terms.astype(jnp.bfloat16), ("sub", "pair"), scatter_dimension=0, tiled=True
    ).astype(jnp.float32)
    hidden_part = jax.nn.gelu(scales[1] * pre_part, approximate=False).astype(jnp.bfloat16)
    hidden = lax.all_gather(hidden_part, ("sub", "pair"), axis=0, tiled=True)
    picked = hidden
    mlp = lax.psum_scatter(
        jnp.dot(picked, w_down, preferred_element_type=jnp.float32).astype(jnp.bfloat16),
        "blk",
        scatter_dimension=0,
        tiled=True,
    ).astype(jnp.float32)
    return (mixed.astype(jnp.float32) + scales[2] * mlp).astype(jnp.bfloat16)


def solution(mesh):
    in_specs = (
        P(("groups", "blk"), ("sub", "pair")),
        P("groups", "blk"),
        P("blk", ("sub", "pair")),
        P(("sub", "pair"), "blk"),
        P("blk", ("sub", "pair")),
        P(),
    )
    out_specs = P(("groups", "blk"), ("sub", "pair"))
    return jax.shard_map(local, mesh=mesh, in_specs=in_specs, out_specs=out_specs, check_vma=False)
```

profile of v0, /device:TPU:0, one launch (start us, length us, event | category | flops | bytes accessed | tf_op | source)
XLA Modules:
  0.0 186.4 jit_solution(3682344931177785495)
XLA Ops:
  6.5 0.0 copy-start
  6.5 1.2 copy-done
  7.8 6.7 %convolution_convert_fusion.2 = bf16[256,2048]{1,0:T(8,128)(2,1)} fusion(bf16[256,2048]{1,0:T(8,128)(2,1)S(1)} %copy-done, bf16[2048,2048]{1,0:T(8,128)(2,1)} %param.8), kind=kOutput, calls=%fused_computation.2 | convolution fusion | flops 2148007936 | bytes 10485760 | tf_op jit(solution)/shard_map/dot_general | solution.py:10
  14.4 0.0 reduce-scatter.4.cloned.1.call-update
  14.5 0.0 all-gather.3.cloned.1.call-start
  14.5 0.7 fusion.13
  15.2 29.3 %reduce-scatter.4.cloned.1.call-done = bf16[64,2048]{1,0:T(8,128)(2,1)} async-done(((bf16[256,2048]{1,0:T(8,128)(2,1)}), bf16[64,2048]{1,0:T(8,128)(2,1)}) %reduce-scatter.4.cloned.1.call-update) | async-done | bytes 262160 | tf_op jit(solution)/shard_map/reduce_scatter | solution.py:9
  44.5 2.4 %add_convert_fusion.1 = bf16[64,2048]{1,0:T(8,128)(2,1)} fusion(bf16[64,2048]{1,0:T(8,128)(2,1)} %reduce-scatter.4.cloned.1.call-done, bf16[64,2048]{1,0:T(8,128)(2,1)S(1)} %copy-done.2, f32[]{:T(128)} %bitcast), kind=kLoop, calls=%fused_computation.26 | loop fusion | flops 655360 | bytes 786436 | tf_op jit(solution)/shard_map/convert_element_type | solution.py:15
  46.8 0.0 all-gather.3.cloned.1.call-update
  46.8 0.0 reduce-scatter.6.cloned.1.call-start
  46.9 26.7 %all-gather.3.cloned.1.call-done = bf16[256,2048]{1,0:T(8,128)(2,1)} async-done(((bf16[64,2048]{1,0:T(8,128)(2,1)}), bf16[256,2048]{1,0:T(8,128)(2,1)}) %all-gather.3.cloned.1.call-update) | async-done | bytes 1048592 | tf_op jit(solution)/shard_map/all_gather | solution.py:17
  73.6 10.7 %convolution_convert_fusion = bf16[256,3584]{1,0:T(8,128)(2,1)} fusion(bf16[256,2048]{1,0:T(8,128)(2,1)} %all-gather.3.cloned.1.call-done, bf16[2048,3584]{1,0:T(8,128)(2,1)} %param.9), kind=kOutput, calls=%fused_computation | convolution fusion | flops 3759013888 | bytes 17563648 | tf_op jit(solution)/shard_map/dot_general | solution.py:16
  84.3 0.0 reduce-scatter.6.cloned.1.call-update
  84.3 0.0 all-gather.5.cloned.1.call-start
  84.4 29.4 %reduce-scatter.6.cloned.1.call-done = bf16[64,3584]{1,0:T(8,128)(2,1)} async-done(((bf16[256,3584]{1,0:T(8,128)(2,1)}), bf16[64,3584]{1,0:T(8,128)(2,1)}) %reduce-scatter.6.cloned.1.call-update) | async-done | bytes 458768 | tf_op jit(solution)/shard_map/reduce_scatter | solution.py:19
  113.8 4.5 %fusion.2 = bf16[64,3584]{1,0:T(8,128)(2,1)} fusion(bf16[64,3584]{1,0:T(8,128)(2,1)} %reduce-scatter.6.cloned.1.call-done, f32[]{:T(128)} %bitcast.2), kind=kLoop, calls=%fused_computation.6 | loop fusion | flops 15368192 | bytes 917508 | tf_op jit(solution)/shard_map/convert_element_type | solution.py:22
  118.3 0.0 all-gather.5.cloned.1.call-update
  118.3 0.0 copy-start.1
  118.3 0.0 reduce-scatter.8.cloned.1.call-start
  118.3 21.2 %all-gather.5.cloned.1.call-done = bf16[256,3584]{1,0:T(8,128)(2,1)} async-done(((bf16[64,3584]{1,0:T(8,128)(2,1)}), bf16[256,3584]{1,0:T(8,128)(2,1)}) %all-gather.5.cloned.1.call-update) | async-done | bytes 1835024 | tf_op jit(solution)/shard_map/all_gather | solution.py:23
  139.6 10.7 %convolution_convert_fusion.1 = bf16[256,2048]{1,0:T(8,128)(2,1)} fusion(bf16[256,3584]{1,0:T(8,128)(2,1)} %all-gather.5.cloned.1.call-done, bf16[3584,2048]{1,0:T(8,128)(2,1)} %param.10), kind=kOutput, calls=%fused_computation.1 | convolution fusion | flops 3758620672 | bytes 17563648 | tf_op jit(solution)/shard_map/dot_general | solution.py:26
  150.2 0.0 reduce-scatter.8.cloned.1.call-update
  150.3 27.3 %reduce-scatter.8.cloned.1.call-done = bf16[64,2048]{1,0:T(8,128)(2,1)} async-done(((bf16[256,2048]{1,0:T(8,128)(2,1)}), bf16[64,2048]{1,0:T(8,128)(2,1)}) %reduce-scatter.8.cloned.1.call-update) | async-done | bytes 262160 | tf_op jit(solution)/shard_map/reduce_scatter | solution.py:25
  177.6 2.3 %add_convert_fusion = bf16[64,2048]{1,0:T(8,128)(2,1)} fusion(bf16[64,2048]{1,0:T(8,128)(2,1)} %reduce-scatter.8.cloned.1.call-done, bf16[64,2048]{1,0:T(8,128)(2,1)S(1)} %copy-done.1, f32[]{:T(128)} %bitcast.1), kind=kLoop, calls=%fused_computation.25 | loop fusion | flops 655360 | bytes 786436 | tf_op jit(solution)/shard_map/convert_element_type | solution.py:31
  (6 shorter events, 0.0 us)
Async XLA Ops:
  6.5 1.2 copy-start
  6.5 8.0 %copy-start.3 = (f32[3]{0:T(128)S(1)}, f32[3]{0:T(128)}, u32[]{:S(2)}) copy-start(f32[3]{0:T(128)} %param.11) | copy-start | bytes 40
  6.5 37.9 %copy-start.2 = (bf16[64,2048]{1,0:T(8,128)(2,1)S(1)}, bf16[64,2048]{1,0:T(8,128)(2,1)}, u32[]{:S(2)}) copy-start(bf16[64,2048]{1,0:T(8,128)(2,1)} %param.6) | copy-start | bytes 786436
  6.5 37.9 %reduce-scatter.4.cloned.1.call-start = ((), (), s32[]{:S(2)}) async-start(), calls=%async_computation.3 | async-start | bytes 1310720 | tf_op jit(solution)/shard_map/reduce_scatter | solution.py:9
  14.5 59.1 %all-gather.3.cloned.1.call-start = ((), (), s32[]{:S(2)}) async-start(), calls=%async_computation.4 | async-start | bytes 1310720 | tf_op jit(solution)/shard_map/all_gather | solution.py:17
  46.8 67.0 %reduce-scatter.6.cloned.1.call-start = ((), (), s32[]{:S(2)}) async-start(), calls=%async_computation.5 | async-start | bytes 2293760 | tf_op jit(solution)/shard_map/reduce_scatter | solution.py:19
  84.3 55.2 %all-gather.5.cloned.1.call-start = ((), (), s32[]{:S(2)}) async-start(), calls=%async_computation.6 | async-start | bytes 2293760 | tf_op jit(solution)/shard_map/all_gather | solution.py:23
  118.3 59.3 %copy-start.1 = (bf16[64,2048]{1,0:T(8,128)(2,1)S(1)}, bf16[64,2048]{1,0:T(8,128)(2,1)}, u32[]{:S(2)}) copy-start(bf16[64,2048]{1,0:T(8,128)(2,1)} %add_convert_fusion.1) | copy-start | bytes 786436
  118.3 59.3 %reduce-scatter.8.cloned.1.call-start = ((), (), s32[]{:S(2)}) async-start(), calls=%async_computation.7 | async-start | bytes 1310720 | tf_op jit(solution)/shard_map/reduce_scatter | solution.py:25
Sparse Core Ops, SparseCore 0:
  14.6 29.8 reduce-scatter.3
  47.0 26.5 all-gather.2
  84.4 29.3 reduce-scatter.5
  118.4 21.1 all-gather.4
  150.4 27.1 reduce-scatter.7
where the time goes:
time: 187 us; the launch traced here: 186 us
  waiting for transfers between devices  134 us (72%)
  matrix products  28.1 us (15%)
  between operations  13.2 us (7%)
  other arithmetic  9.12 us (5%)
  local copies, waits for them, and re-layouts  1.89 us (1%)
    reduce_scatter x1, waiting for transfers between devices, local(): lax.psum_scatter(pre_terms.astype(jnp.bfloat16), ('sub', 'pair'), scatter...  29.4 us
    reduce_scatter x1, waiting for transfers between devices, local(): lax.psum_scatter(jnp.dot(picked, w_out, preferred_element_type=jnp.float3...  29.3 us
    reduce_scatter x1, waiting for transfers between devices, local(): lax.psum_scatter(jnp.dot(picked, w_down, preferred_element_type=jnp.float...  27.3 us
    all_gather x1, waiting for transfers between devices, local(): lax.all_gather(mixed, 'blk', axis=0, tiled=True)  26.7 us
    all_gather x1, waiting for transfers between devices, local(): hidden = lax.all_gather(hidden_part, ('sub', 'pair'), axis=0, tiled=True)  21.2 us
    dot_general x1, matrix products, local(): jnp.dot(lax.all_gather(mixed, 'blk', axis=0, tiled=True), w_in, preferred...  10.7 us
    dot_general x1, matrix products, local(): jnp.dot(picked, w_down, preferred_element_type=jnp.float32)  10.7 us
    dot_general x1, matrix products, local(): jnp.dot(picked, w_out, preferred_element_type=jnp.float32)  6.68 us
  transfers between devices with their start and end apart: 5, of which 5 were waited for; matrix products, arithmetic and copies ran while one was open for 0% of the time, Pallas kernels for 0%

commit v1 on v0

v1 whole, which is shorter than its diff:
```python
import jax
import jax.numpy as jnp
from jax import lax
from jax.sharding import PartitionSpec as P

F32 = jnp.float32
BF16 = jnp.bfloat16


def general(resid, context, w_out, w_in, w_down, scales):
    attn = lax.psum_scatter(
        jnp.dot(context, w_out, preferred_element_type=F32).astype(BF16), "blk", scatter_dimension=0, tiled=True
    ).astype(F32)
    mixed = (resid.astype(F32) + scales[0] * attn).astype(BF16)
    pre_terms = jnp.dot(lax.all_gather(mixed, "blk", axis=0, tiled=True), w_in, preferred_element_type=F32)
    pre_part = lax.psum_scatter(
        pre_terms.astype(BF16), ("sub", "pair"), scatter_dimension=0, tiled=True
    ).astype(F32)
    hidden_part = jax.nn.gelu(scales[1] * pre_part, approximate=False).astype(BF16)
    hidden = lax.all_gather(hidden_part, ("sub", "pair"), axis=0, tiled=True)
    mlp = lax.psum_scatter(
        jnp.dot(hidden, w_down, preferred_element_type=F32).astype(BF16), "blk", scatter_dimension=0, tiled=True
    ).astype(F32)
    return (mixed.astype(F32) + scales[2] * mlp).astype(BF16)


def swap(x, axis, size, flip):
    return lax.ppermute(x, axis, [(i, i ^ flip) for i in range(size)])


def halves(x, which):
    width = x.shape[1] // 2
    return (
        lax.dynamic_slice_in_dim(x, which * width, width, 1),
        lax.dynamic_slice_in_dim(x, (1 - which) * width, width, 1),
    )


def joined(own, other, which):
    first = which == 0
    return jnp.concatenate([jnp.where(first, own, other), jnp.where(first, other, own)], axis=1)


def add(a, b):
    return a.astype(F32) + b.astype(F32)


def swapped(resid, context, w_out, w_in, w_down, scales):
    n = 4
    z, core = lax.axis_index("blk"), lax.axis_index("pair")
    odd = z & 1
    rows = resid.shape[0] // 2
    width = w_out.shape[1]
    results = []
    for half in range(2):
        ctx = context.reshape(n, 2, rows, -1)[:, half].reshape(n * rows, -1)
        res = resid[half * rows:(half + 1) * rows].astype(F32)
        attn = scales[0] * jnp.dot(ctx, w_out, preferred_element_type=F32)
        mine = (jnp.arange(n) == z)[:, None, None]
        part = (attn.reshape(n, rows, width) + jnp.where(mine, res[None], 0.0)).reshape(n * rows, width).astype(BF16)
        own, other = halves(part, odd)
        own = add(own, swap(other, "blk", n, 1)).astype(BF16)
        own = add(own, swap(own, "blk", n, 2)).astype(BF16)
        mixed = joined(own, swap(own, "blk", n, 1), odd)
        pre = jnp.dot(mixed, w_in, preferred_element_type=F32).astype(BF16)
        own, other = halves(pre, core)
        own = add(own, swap(other, "pair", 2, 1)).astype(BF16)
        own = add(own, swap(own, "sub", 2, 1))
        own = jax.nn.gelu(scales[1] * own, approximate=False).astype(BF16)
        hidden = joined(own, swap(own, "pair", 2, 1), core)
        mlp = jnp.dot(hidden, w_down, preferred_element_type=F32).astype(BF16).reshape(n, rows, width)

        def of(owner):
            return lax.dynamic_index_in_dim(mlp, owner, 0, keepdims=False)

        total = of(z).astype(F32)
        for flip in (3, 2, 1):
            total = add(total, swap(of(z ^ flip), "blk", n, flip))
        kept = lax.dynamic_slice_in_dim(mixed, z * rows, rows, 0)
        results.append((kept.astype(F32) + scales[2] * total).astype(BF16))
    return jnp.concatenate(results, axis=0)


def solution(mesh):
    shape = dict(mesh.shape)
    fast = shape["blk"] == 4 and shape["sub"] == 2 and shape["pair"] == 2
    in_specs = (
        P(("groups", "blk"), ("sub", "pair")),
        P("groups", "blk"),
        P("blk", ("sub", "pair")),
        P(("sub", "pair"), "blk"),
        P("blk", ("sub", "pair")),
        P(),
    )
    out_specs = P(("groups", "blk"), ("sub", "pair"))
    local = swapped if fast else general
    return jax.shard_map(local, mesh=mesh, in_specs=in_specs, out_specs=out_specs, check_vma=False)
```

time: 187 us -> 118 us (0.63)
  waiting for transfers between devices: 134 us -> 56.9 us
  starting transfers between devices: 0.17 us -> 25 us
  between operations: 13.2 us -> 0.39 us
  matrix products: 28.1 us -> 21.5 us
  local copies, waits for them, and re-layouts: 1.89 us -> 4.22 us
    reduce_scatter x3 -> x0, waiting for transfers between devices: 86 us -> none  [the longest x1 29.4 us: local(): lax.psum_scatter(pre_terms.astype(jnp.bfloat16), ('sub', 'pair'), scatter...]
    ppermute x0 -> x18, waiting for transfers between devices: none -> 56.9 us  [swap(): return lax.ppermute(x, axis, [(i, i ^ flip) for i in range(size)])]
    all_gather x2 -> x0, waiting for transfers between devices: 47.9 us -> none  [the longest x1 26.7 us: local(): lax.all_gather(mixed, 'blk', axis=0, tiled=True)]
    ppermute x0 -> x18, starting transfers between devices: none -> 25 us  [swap(): return lax.ppermute(x, axis, [(i, i ^ flip) for i in range(size)])]
    dot_general x3 -> x6, matrix products: 28.1 us -> 21.5 us  [the longest x2 9.51 us: swapped(): pre = jnp.dot(mixed, w_in, preferred_element_type=F32).astype(BF16)]
    slice x1 -> x2, local copies, waits for them, and re-layouts: 0.66 us -> 2.63 us  [the longest x1 1.35 us: swapped(): results.append((kept.astype(F32) + scales[2] * total).astype(BF16))]
    convert_element_type x3 -> x11, other arithmetic: 9.12 us -> 8.41 us  [the longest x2 5.42 us: swapped(): own = jax.nn.gelu(scales[1] * own, approximate=False).astype(BF16)]
  transfers between devices with their start and end apart: 5 -> 18, of which waited for: 5 -> 11; matrix products, arithmetic and copies ran while one was open for 0% -> 19% of each run, Pallas kernels for 0% -> 0%
where the time goes in v1:
time: 118 us
  waiting for transfers between devices  56.9 us (48%)
  starting transfers between devices  25 us (21%)
  matrix products  21.5 us (18%)
  other arithmetic  9.68 us (8%)
  local copies, waits for them, and re-layouts  4.22 us (4%)
    ppermute x18, waiting for transfers between devices, swap(): return lax.ppermute(x, axis, [(i, i ^ flip) for i in range(size)])  56.9 us
    ppermute x18, starting transfers between devices, swap(): return lax.ppermute(x, axis, [(i, i ^ flip) for i in range(size)])  25 us
    dot_general x2, matrix products, swapped(): pre = jnp.dot(mixed, w_in, preferred_element_type=F32).astype(BF16)  9.51 us
    dot_general x2, matrix products, swapped(): attn = scales[0] * jnp.dot(ctx, w_out, preferred_element_type=F32)  7.82 us
    convert_element_type x2, other arithmetic, swapped(): own = jax.nn.gelu(scales[1] * own, approximate=False).astype(BF16)  5.42 us
    dot_general x2, matrix products, swapped(): jnp.dot(hidden, w_down, preferred_element_type=F32).astype(BF16)  4.13 us
  transfers between devices with their start and end apart: 18, of which 11 were waited for; matrix products, arithmetic and copies ran while one was open for 19% of the time, Pallas kernels for 0%

profile of v1, /device:TPU:0, one launch (start us, length us, event | category | flops | bytes accessed | tf_op | source)
XLA Modules:
  0.0 117.6 jit_solution(7272038086949197104)
XLA Ops:
  4.1 5.9 %fusion.2 = bf16[128,2048]{1,0:T(8,128)(2,1)S(1)} fusion(f32[128,2048]{1,0:T(8,128)S(1)} %get-tuple-element.24, bf16[128,2048]{1,0:T(8,128)(2,1)S(1)} %bitcast.45, bf16[2048,2048]{1,0:T(8,128)(2,1)} %param.8, f32[]{:T(128)} %bitcast), kind=kOutput, calls=%fused_computation.8 | convolution fusion | flops 1074528256 | bytes 10485764 | tf_op jit(solution)/shard_map/dot_general | solution.py:58
  10.0 3.1 %collective-permute-start.9 = (bf16[128,1024]{1,0:T(8,128)(2,1)S(1)}, bf16[128,1024]{1,0:T(8,128)(2,1)S(1)}, u32[]{:S(2)}, u32[]{:S(2)}) collective-permute-start(bf16[128,1024]{1,0:T(8,128)(2,1)S(1)} %constant_dynamic-slice_fusion.1), channel_id=1, source_target_pairs={{0,4},{4,0},{8,12},{12,8},{1,5},{5,1},{9,13},{13,9},{2,6},{6,2},{1... | collective-permute-start | bytes 786440 | tf_op jit(solution)/shard_map/ppermute | solution.py:28
  13.1 2.0 %fusion.3 = bf16[128,2048]{1,0:T(8,128)(2,1)S(1)} fusion(f32[128,2048]{1,0:T(8,128)S(1)} %get-tuple-element.23, bf16[128,2048]{1,0:T(8,128)(2,1)S(1)} %bitcast.44, bf16[2048,2048]{1,0:T(8,128)(2,1)S(1)} %bitcast.43, f32[]{:T(128)} %bitcast), kind=kOutput, calls=%fused_computation.9 | convolution fusion | flops 1074528256 | bytes 10485764 | tf_op jit(solution)/shard_map/dot_general | solution.py:58
  15.2 5.0 %collective-permute-done.9 = bf16[128,1024]{1,0:T(8,128)(2,1)S(1)} collective-permute-done((bf16[128,1024]{1,0:T(8,128)(2,1)S(1)}, bf16[128,1024]{1,0:T(8,128)(2,1)S(1)}, u32[]{:S(2)}, u32[]{:S(2)}) %collective-permute-start.9) | collective-permute-done | bytes 262176 | tf_op jit(solution)/shard_map/ppermute | solution.py:28
  20.3 3.1 %collective-permute-start.10 = (bf16[128,1024]{1,0:T(8,128)(2,1)S(1)}, bf16[128,1024]{1,0:T(8,128)(2,1)S(1)}, u32[]{:S(2)}, u32[]{:S(2)}) collective-permute-start(bf16[128,1024]{1,0:T(8,128)(2,1)S(1)} %add_convert_fusion.3), channel_id=1, source_target_pairs={{0,8},{4,12},{8,0},{12,4},{1,9},{5,13},{9,1},{13,5},{2,10},{6,14},... | collective-permute-start | bytes 786440 | tf_op jit(solution)/shard_map/ppermute | solution.py:28
  23.5 6.5 %collective-permute-done = bf16[128,1024]{1,0:T(8,128)(2,1)S(1)} collective-permute-done((bf16[128,1024]{1,0:T(8,128)(2,1)S(1)}, bf16[128,1024]{1,0:T(8,128)(2,1)S(1)}, u32[]{:S(2)}, u32[]{:S(2)}) %collective-permute-start) | collective-permute-done | bytes 262176 | tf_op jit(solution)/shard_map/ppermute | solution.py:28
  30.1 9.7 %collective-permute-done.10 = bf16[128,1024]{1,0:T(8,128)(2,1)S(1)} collective-permute-done((bf16[128,1024]{1,0:T(8,128)(2,1)S(1)}, bf16[128,1024]{1,0:T(8,128)(2,1)S(1)}, u32[]{:S(2)}, u32[]{:S(2)}) %collective-permute-start.10) | collective-permute-done | bytes 262176 | tf_op jit(solution)/shard_map/ppermute | solution.py:28
  39.9 2.6 %collective-permute-start.11 = (bf16[128,1024]{1,0:T(8,128)(2,1)S(1)}, bf16[128,1024]{1,0:T(8,128)(2,1)S(1)}, u32[]{:S(2)}, u32[]{:S(2)}) collective-permute-start(bf16[128,1024]{1,0:T(8,128)(2,1)S(1)} %add_convert_fusion.2), channel_id=1, source_target_pairs={{0,4},{4,0},{8,12},{12,8},{1,5},{5,1},{9,13},{13,9},{2,6},{6,2},{1... | collective-permute-start | bytes 786440 | tf_op jit(solution)/shard_map/ppermute | solution.py:28
  42.5 2.5 %collective-permute-done.1 = bf16[128,1024]{1,0:T(8,128)(2,1)S(1)} collective-permute-done((bf16[128,1024]{1,0:T(8,128)(2,1)S(1)}, bf16[128,1024]{1,0:T(8,128)(2,1)S(1)}, u32[]{:S(2)}, u32[]{:S(2)}) %collective-permute-start.1) | collective-permute-done | bytes 262176 | tf_op jit(solution)/shard_map/ppermute | solution.py:28
  45.7 2.5 %collective-permute-done.11 = bf16[128,1024]{1,0:T(8,128)(2,1)S(1)} collective-permute-done((bf16[128,1024]{1,0:T(8,128)(2,1)S(1)}, bf16[128,1024]{1,0:T(8,128)(2,1)S(1)}, u32[]{:S(2)}, u32[]{:S(2)}) %collective-permute-start.11) | collective-permute-done | bytes 262176 | tf_op jit(solution)/shard_map/ppermute | solution.py:28
  48.2 7.4 %convolution_convert_fusion = bf16[128,3584]{1,0:T(8,128)(2,1)S(1)} fusion(bf16[2048,3584]{1,0:T(8,128)(2,1)} %param.9, bf16[128,1024]{1,0:T(8,128)(2,1)S(1)} %get-tuple-element.20, bf16[128,1024]{1,0:T(8,128)(2,1)S(1)} %get-tuple-element.19), kind=kOutput, calls=%fused_computation | convolution fusion | flops 1880555520 | bytes 16121856 | tf_op jit(solution)/shard_map/dot_general | solution.py:65
  57.0 2.1 %convolution_convert_fusion.1 = bf16[128,3584]{1,0:T(8,128)(2,1)S(1)} fusion(bf16[2048,3584]{1,0:T(8,128)(2,1)S(1)} %bitcast.41, bf16[128,1024]{1,0:T(8,128)(2,1)S(1)} %get-tuple-element.15, bf16[128,1024]{1,0:T(8,128)(2,1)S(1)} %get-tuple-element.14), kind=kOutput, calls=%fused_computation.1 | convolution fusion | flops 1880555520 | bytes 16121856 | tf_op jit(solution)/shard_map/dot_general | solution.py:65
  59.4 1.9 %collective-permute-start.13 = (bf16[128,1792]{1,0:T(8,128)(2,1)S(1)}, bf16[128,1792]{1,0:T(8,128)(2,1)S(1)}, u32[]{:S(2)}, u32[]{:S(2)}) collective-permute-start(bf16[128,1792]{1,0:T(8,128)(2,1)S(1)} %add_convert_fusion), channel_id=1, source_target_pairs={{0,2},{2,0},{1,3},{3,1},{4,6},{6,4},{5,7},{7,5},{8,10},{10,8},{9,1... | collective-permute-start | bytes 1376264 | tf_op jit(solution)/shard_map/ppermute | solution.py:28
  61.4 1.7 %collective-permute-start.4 = (bf16[128,1792]{1,0:T(8,128)(2,1)S(1)}, bf16[128,1792]{1,0:T(8,128)(2,1)S(1)}, u32[]{:S(2)}, u32[]{:S(2)}) collective-permute-start(bf16[128,1792]{1,0:T(8,128)(2,1)S(1)} %add_convert_fusion.1), channel_id=1, source_target_pairs={{0,2},{2,0},{1,3},{3,1},{4,6},{6,4},{5,7},{7,5},{8,10},{10,8},{9,1... | collective-permute-start | bytes 1376264 | tf_op jit(solution)/shard_map/ppermute | solution.py:28
  63.1 9.7 %collective-permute-done.13 = bf16[128,1792]{1,0:T(8,128)(2,1)S(1)} collective-permute-done((bf16[128,1792]{1,0:T(8,128)(2,1)S(1)}, bf16[128,1792]{1,0:T(8,128)(2,1)S(1)}, u32[]{:S(2)}, u32[]{:S(2)}) %collective-permute-start.13) | collective-permute-done | bytes 458784 | tf_op jit(solution)/shard_map/ppermute | solution.py:28
  72.8 2.6 %fusion.9 = bf16[128,1792]{1,0:T(8,128)(2,1)S(1)} fusion(bf16[128,1792]{1,0:T(8,128)(2,1)S(1)} %collective-permute-done.13, bf16[128,1792]{1,0:T(8,128)(2,1)S(1)} %add_convert_fusion, f32[]{:T(128)} %bitcast.5), kind=kLoop, calls=%fused_computation.19 | loop fusion | flops 15826944 | bytes 1376260 | tf_op jit(solution)/shard_map/convert_element_type | solution.py:69
  75.5 6.8 %collective-permute-done.4 = bf16[128,1792]{1,0:T(8,128)(2,1)S(1)} collective-permute-done((bf16[128,1792]{1,0:T(8,128)(2,1)S(1)}, bf16[128,1792]{1,0:T(8,128)(2,1)S(1)}, u32[]{:S(2)}, u32[]{:S(2)}) %collective-permute-start.4) | collective-permute-done | bytes 458784 | tf_op jit(solution)/shard_map/ppermute | solution.py:28
  82.3 2.8 %fusion.6 = bf16[128,1792]{1,0:T(8,128)(2,1)S(1)} fusion(bf16[128,1792]{1,0:T(8,128)(2,1)S(1)} %collective-permute-done.4, bf16[128,1792]{1,0:T(8,128)(2,1)S(1)} %add_convert_fusion.1, f32[]{:T(128)} %bitcast.5), kind=kLoop, calls=%fused_computation.16 | loop fusion | flops 15826944 | bytes 1376260 | tf_op jit(solution)/shard_map/convert_element_type | solution.py:69
  85.4 2.1 %convolution_convert_fusion.2 = bf16[128,2048]{1,0:T(8,128)(2,1)S(1)} fusion(bf16[3584,2048]{1,0:T(8,128)(2,1)S(1)} %bitcast.39, bf16[128,1792]{1,0:T(8,128)(2,1)S(1)} %get-tuple-element.10, bf16[128,1792]{1,0:T(8,128)(2,1)S(1)} %get-tuple-element.9), kind=kOutput, calls=%fused_computation.6 | convolution fusion | flops 1881145344 | bytes 16121856 | tf_op jit(solution)/shard_map/dot_general | solution.py:71
  87.5 6.4 %collective-permute-start.15 = (bf16[32,2048]{1,0:T(8,128)(2,1)S(1)}, bf16[32,2048]{1,0:T(8,128)(2,1)S(1)}, u32[]{:S(2)}, u32[]{:S(2)}) collective-permute-start(bf16[32,2048]{1,0:T(8,128)(2,1)S(1)} %get-tuple-element.16), channel_id=1, source_target_pairs={{0,12},{4,8},{8,4},{12,0},{1,13},{5,9},{9,5},{13,1},{2,14},{6,10},... | collective-permute-start | bytes 393224 | tf_op jit(solution)/shard_map/ppermute | solution.py:28
  94.6 2.1 %convolution_convert_fusion.3 = bf16[128,2048]{1,0:T(8,128)(2,1)S(1)} fusion(bf16[3584,2048]{1,0:T(8,128)(2,1)S(1)} %bitcast.39, bf16[128,1792]{1,0:T(8,128)(2,1)S(1)} %get-tuple-element.8, bf16[128,1792]{1,0:T(8,128)(2,1)S(1)} %get-tuple-element.7), kind=kOutput, calls=%fused_computation.7 | convolution fusion | flops 1881145344 | bytes 16121856 | tf_op jit(solution)/shard_map/dot_general | solution.py:71
  96.7 3.8 %collective-permute-start.6 = (bf16[32,2048]{1,0:T(8,128)(2,1)S(1)}, bf16[32,2048]{1,0:T(8,128)(2,1)S(1)}, u32[]{:S(2)}, u32[]{:S(2)}) collective-permute-start(bf16[32,2048]{1,0:T(8,128)(2,1)S(1)} %get-tuple-element.11), channel_id=1, source_target_pairs={{0,12},{4,8},{8,4},{12,0},{1,13},{5,9},{9,5},{13,1},{2,14},{6,10},... | collective-permute-start | bytes 393224 | tf_op jit(solution)/shard_map/ppermute | solution.py:28
  102.8 5.1 %collective-permute-done.16 = bf16[32,2048]{1,0:T(8,128)(2,1)S(1)} collective-permute-done((bf16[32,2048]{1,0:T(8,128)(2,1)S(1)}, bf16[32,2048]{1,0:T(8,128)(2,1)S(1)}, u32[]{:S(2)}, u32[]{:S(2)}) %collective-permute-start.16) | collective-permute-done | bytes 131104 | tf_op jit(solution)/shard_map/ppermute | solution.py:28
  109.4 6.7 %collective-permute-done.7 = bf16[32,2048]{1,0:T(8,128)(2,1)S(1)} collective-permute-done((bf16[32,2048]{1,0:T(8,128)(2,1)S(1)}, bf16[32,2048]{1,0:T(8,128)(2,1)S(1)}, u32[]{:S(2)}, u32[]{:S(2)}) %collective-permute-start.7) | collective-permute-done | bytes 131104 | tf_op jit(solution)/shard_map/ppermute | solution.py:28
  (69 shorter events, 13.2 us)
Async XLA Ops:
  4.1 9.0 %slice-start.8 = ((s8[8388608]{0:T(1024)(128)(4,1)}), s8[4194304]{0:T(1024)(128)(4,1)S(1)}, s32[]{:S(2)}) async-start(s8[8388608]{0:T(1024)(128)(4,1)} %bitcast.42), calls=%async_computation.8 | async-start | bytes 8388608
  10.0 10.2 %collective-permute-start.9 = (bf16[128,1024]{1,0:T(8,128)(2,1)S(1)}, bf16[128,1024]{1,0:T(8,128)(2,1)S(1)}, u32[]{:S(2)}, u32[]{:S(2)}) collective-permute-start(bf16[128,1024]{1,0:T(8,128)(2,1)S(1)} %constant_dynamic-slice_fusion.1), channel_id=1, source_target_pairs={{0,4},{4,0},{8,12},{12,8},{1,5},{5,1},{9,13},{13,9},{2,6},{6,2},{1... | collective-permute-start | bytes 786440 | tf_op jit(solution)/shard_map/ppermute | solution.py:28
  15.1 14.9 %collective-permute-start = (bf16[128,1024]{1,0:T(8,128)(2,1)S(1)}, bf16[128,1024]{1,0:T(8,128)(2,1)S(1)}, u32[]{:S(2)}, u32[]{:S(2)}) collective-permute-start(bf16[128,1024]{1,0:T(8,128)(2,1)S(1)} %constant_dynamic-slice_fusion.3), channel_id=1, source_target_pairs={{0,4},{4,0},{8,12},{12,8},{1,5},{5,1},{9,13},{13,9},{2,6},{6,2},{1... | collective-permute-start | bytes 786440 | tf_op jit(solution)/shard_map/ppermute | solution.py:28
  20.3 19.5 %collective-permute-start.10 = (bf16[128,1024]{1,0:T(8,128)(2,1)S(1)}, bf16[128,1024]{1,0:T(8,128)(2,1)S(1)}, u32[]{:S(2)}, u32[]{:S(2)}) collective-permute-start(bf16[128,1024]{1,0:T(8,128)(2,1)S(1)} %add_convert_fusion.3), channel_id=1, source_target_pairs={{0,8},{4,12},{8,0},{12,4},{1,9},{5,13},{9,1},{13,5},{2,10},{6,14},... | collective-permute-start | bytes 786440 | tf_op jit(solution)/shard_map/ppermute | solution.py:28
  30.0 25.8 %slice-start.4 = ((s8[14680064]{0:T(1024)(128)(4,1)}), s8[2097152]{0:T(1024)(128)(4,1)S(1)}, s32[]{:S(2)}) async-start(s8[14680064]{0:T(1024)(128)(4,1)} %bitcast.40), calls=%async_computation.4 | async-start | bytes 4194304
  30.1 14.9 %collective-permute-start.1 = (bf16[128,1024]{1,0:T(8,128)(2,1)S(1)}, bf16[128,1024]{1,0:T(8,128)(2,1)S(1)}, u32[]{:S(2)}, u32[]{:S(2)}) collective-permute-start(bf16[128,1024]{1,0:T(8,128)(2,1)S(1)} %add_convert_fusion.5), channel_id=1, source_target_pairs={{0,8},{4,12},{8,0},{12,4},{1,9},{5,13},{9,1},{13,5},{2,10},{6,14},... | collective-permute-start | bytes 786440 | tf_op jit(solution)/shard_map/ppermute | solution.py:28
  39.9 8.3 %collective-permute-start.11 = (bf16[128,1024]{1,0:T(8,128)(2,1)S(1)}, bf16[128,1024]{1,0:T(8,128)(2,1)S(1)}, u32[]{:S(2)}, u32[]{:S(2)}) collective-permute-start(bf16[128,1024]{1,0:T(8,128)(2,1)S(1)} %add_convert_fusion.2), channel_id=1, source_target_pairs={{0,4},{4,0},{8,12},{12,8},{1,5},{5,1},{9,13},{13,9},{2,6},{6,2},{1... | collective-permute-start | bytes 786440 | tf_op jit(solution)/shard_map/ppermute | solution.py:28
  45.0 10.8 %collective-permute-start.2 = (bf16[128,1024]{1,0:T(8,128)(2,1)S(1)}, bf16[128,1024]{1,0:T(8,128)(2,1)S(1)}, u32[]{:S(2)}, u32[]{:S(2)}) collective-permute-start(bf16[128,1024]{1,0:T(8,128)(2,1)S(1)} %add_convert_fusion.4), channel_id=1, source_target_pairs={{0,4},{4,0},{8,12},{12,8},{1,5},{5,1},{9,13},{13,9},{2,6},{6,2},{1... | collective-permute-start | bytes 786440 | tf_op jit(solution)/shard_map/ppermute | solution.py:28
  55.7 3.6 %collective-permute-start.12 = (bf16[128,1792]{1,0:T(8,128)(2,1)S(1)}, bf16[128,1792]{1,0:T(8,128)(2,1)S(1)}, u32[]{:S(2)}, u32[]{:S(2)}) collective-permute-start(bf16[128,1792]{1,0:T(8,128)(2,1)S(1)} %constant_dynamic-slice_fusion), channel_id=1, source_target_pairs={{0,1},{1,0},{2,3},{3,2},{4,5},{5,4},{6,7},{7,6},{8,9},{9,8},{10,11... | collective-permute-start | bytes 1376264 | tf_op jit(solution)/shard_map/ppermute | solution.py:28
  57.0 28.3 %slice-start = ((s8[14680064]{0:T(1024)(128)(4,1)}), s8[4194304]{0:T(1024)(128)(4,1)S(1)}, s32[]{:S(2)}) async-start(s8[14680064]{0:T(1024)(128)(4,1)} %bitcast.38), calls=%async_computation | async-start | bytes 8388608
  57.0 28.3 %slice-start.1 = ((s8[14680064]{0:T(1024)(128)(4,1)}), s8[4194304]{0:T(1024)(128)(4,1)S(1)}, s32[]{:S(2)}) async-start(s8[14680064]{0:T(1024)(128)(4,1)} %bitcast.38), calls=%async_computation.1 | async-start | bytes 8388608
  57.0 28.3 %slice-start.2 = ((s8[14680064]{0:T(1024)(128)(4,1)}), s8[2097152]{0:T(1024)(128)(4,1)S(1)}, s32[]{:S(2)}) async-start(s8[14680064]{0:T(1024)(128)(4,1)} %bitcast.38), calls=%async_computation.2 | async-start | bytes 4194304
  59.1 26.2 %slice-start.3 = ((s8[14680064]{0:T(1024)(128)(4,1)}), s8[4194304]{0:T(1024)(128)(4,1)S(1)}, s32[]{:S(2)}) async-start(s8[14680064]{0:T(1024)(128)(4,1)} %bitcast.38), calls=%async_computation.3 | async-start | bytes 8388608
  59.2 2.1 %collective-permute-start.3 = (bf16[128,1792]{1,0:T(8,128)(2,1)S(1)}, bf16[128,1792]{1,0:T(8,128)(2,1)S(1)}, u32[]{:S(2)}, u32[]{:S(2)}) collective-permute-start(bf16[128,1792]{1,0:T(8,128)(2,1)S(1)} %constant_dynamic-slice_fusion.2), channel_id=1, source_target_pairs={{0,1},{1,0},{2,3},{3,2},{4,5},{5,4},{6,7},{7,6},{8,9},{9,8},{10,11... | collective-permute-start | bytes 1376264 | tf_op jit(solution)/shard_map/ppermute | solution.py:28
  59.4 13.4 %collective-permute-start.13 = (bf16[128,1792]{1,0:T(8,128)(2,1)S(1)}, bf16[128,1792]{1,0:T(8,128)(2,1)S(1)}, u32[]{:S(2)}, u32[]{:S(2)}) collective-permute-start(bf16[128,1792]{1,0:T(8,128)(2,1)S(1)} %add_convert_fusion), channel_id=1, source_target_pairs={{0,2},{2,0},{1,3},{3,1},{4,6},{6,4},{5,7},{7,5},{8,10},{10,8},{9,1... | collective-permute-start | bytes 1376264 | tf_op jit(solution)/shard_map/ppermute | solution.py:28
  61.4 20.9 %collective-permute-start.4 = (bf16[128,1792]{1,0:T(8,128)(2,1)S(1)}, bf16[128,1792]{1,0:T(8,128)(2,1)S(1)}, u32[]{:S(2)}, u32[]{:S(2)}) collective-permute-start(bf16[128,1792]{1,0:T(8,128)(2,1)S(1)} %add_convert_fusion.1), channel_id=1, source_target_pairs={{0,2},{2,0},{1,3},{3,1},{4,6},{6,4},{5,7},{7,5},{8,10},{10,8},{9,1... | collective-permute-start | bytes 1376264 | tf_op jit(solution)/shard_map/ppermute | solution.py:28
  75.4 9.8 %collective-permute-start.14 = (bf16[128,1792]{1,0:T(8,128)(2,1)S(1)}, bf16[128,1792]{1,0:T(8,128)(2,1)S(1)}, u32[]{:S(2)}, u32[]{:S(2)}) collective-permute-start(bf16[128,1792]{1,0:T(8,128)(2,1)S(1)} %fusion.9), channel_id=1, source_target_pairs={{0,1},{1,0},{2,3},{3,2},{4,5},{5,4},{6,7},{7,6},{8,9},{9,8},{10,11... | collective-permute-start | bytes 1376264 | tf_op jit(solution)/shard_map/ppermute | solution.py:28
  85.1 9.4 %collective-permute-start.5 = (bf16[128,1792]{1,0:T(8,128)(2,1)S(1)}, bf16[128,1792]{1,0:T(8,128)(2,1)S(1)}, u32[]{:S(2)}, u32[]{:S(2)}) collective-permute-start(bf16[128,1792]{1,0:T(8,128)(2,1)S(1)} %fusion.6), channel_id=1, source_target_pairs={{0,1},{1,0},{2,3},{3,2},{4,5},{5,4},{6,7},{7,6},{8,9},{9,8},{10,11... | collective-permute-start | bytes 1376264 | tf_op jit(solution)/shard_map/ppermute | solution.py:28
  87.5 13.1 %collective-permute-start.15 = (bf16[32,2048]{1,0:T(8,128)(2,1)S(1)}, bf16[32,2048]{1,0:T(8,128)(2,1)S(1)}, u32[]{:S(2)}, u32[]{:S(2)}) collective-permute-start(bf16[32,2048]{1,0:T(8,128)(2,1)S(1)} %get-tuple-element.16), channel_id=1, source_target_pairs={{0,12},{4,8},{8,4},{12,0},{1,13},{5,9},{9,5},{13,1},{2,14},{6,10},... | collective-permute-start | bytes 393224 | tf_op jit(solution)/shard_map/ppermute | solution.py:28
  93.9 8.9 %collective-permute-start.17 = (bf16[32,2048]{1,0:T(8,128)(2,1)S(1)}, bf16[32,2048]{1,0:T(8,128)(2,1)S(1)}, u32[]{:S(2)}, u32[]{:S(2)}) collective-permute-start(bf16[32,2048]{1,0:T(8,128)(2,1)S(1)} %get-tuple-element.17), channel_id=1, source_target_pairs={{0,4},{4,0},{8,12},{12,8},{1,5},{5,1},{9,13},{13,9},{2,6},{6,2},{1... | collective-permute-start | bytes 393224 | tf_op jit(solution)/shard_map/ppermute | solution.py:28
  93.9 14.0 %collective-permute-start.16 = (bf16[32,2048]{1,0:T(8,128)(2,1)S(1)}, bf16[32,2048]{1,0:T(8,128)(2,1)S(1)}, u32[]{:S(2)}, u32[]{:S(2)}) collective-permute-start(bf16[32,2048]{1,0:T(8,128)(2,1)S(1)} %get-tuple-element.18), channel_id=1, source_target_pairs={{0,8},{4,12},{8,0},{12,4},{1,9},{5,13},{9,1},{13,5},{2,10},{6,14},... | collective-permute-start | bytes 393224 | tf_op jit(solution)/shard_map/ppermute | solution.py:28
  96.7 11.9 %collective-permute-start.6 = (bf16[32,2048]{1,0:T(8,128)(2,1)S(1)}, bf16[32,2048]{1,0:T(8,128)(2,1)S(1)}, u32[]{:S(2)}, u32[]{:S(2)}) collective-permute-start(bf16[32,2048]{1,0:T(8,128)(2,1)S(1)} %get-tuple-element.11), channel_id=1, source_target_pairs={{0,12},{4,8},{8,4},{12,0},{1,13},{5,9},{9,5},{13,1},{2,14},{6,10},... | collective-permute-start | bytes 393224 | tf_op jit(solution)/shard_map/ppermute | solution.py:28
  100.5 8.8 %collective-permute-start.8 = (bf16[32,2048]{1,0:T(8,128)(2,1)S(1)}, bf16[32,2048]{1,0:T(8,128)(2,1)S(1)}, u32[]{:S(2)}, u32[]{:S(2)}) collective-permute-start(bf16[32,2048]{1,0:T(8,128)(2,1)S(1)} %get-tuple-element.12), channel_id=1, source_target_pairs={{0,4},{4,0},{8,12},{12,8},{1,5},{5,1},{9,13},{13,9},{2,6},{6,2},{1... | collective-permute-start | bytes 393224 | tf_op jit(solution)/shard_map/ppermute | solution.py:28
  100.5 15.6 %collective-permute-start.7 = (bf16[32,2048]{1,0:T(8,128)(2,1)S(1)}, bf16[32,2048]{1,0:T(8,128)(2,1)S(1)}, u32[]{:S(2)}, u32[]{:S(2)}) collective-permute-start(bf16[32,2048]{1,0:T(8,128)(2,1)S(1)} %get-tuple-element.13), channel_id=1, source_target_pairs={{0,8},{4,12},{8,0},{12,4},{1,9},{5,13},{9,1},{13,5},{2,10},{6,14},... | collective-permute-start | bytes 393224 | tf_op jit(solution)/shard_map/ppermute | solution.py:28
  (4 other events, 33.1 us)

commit v2 on v1

--- a/solution.py
+++ b/solution.py
@@ -1,6 +1,10 @@
+import functools
+
 import jax
 import jax.numpy as jnp
 from jax import lax
+from jax.experimental import pallas as pl
+from jax.experimental.pallas import tpu as pltpu
 from jax.sharding import PartitionSpec as P
 
 F32 = jnp.float32
@@ -45,30 +49,151 @@
     return a.astype(F32) + b.astype(F32)
 
 
+def after(x, *done):
+    return lax.optimization_barrier((x,) + done)[0]
+
+
+def in_hbm(x):
+    return pltpu.with_memory_space_constraint(x, pltpu.HBM)
+
+
+ANY = pl.BlockSpec(memory_space=pl.ANY)
+SMEM = pl.BlockSpec(memory_space=pltpu.SMEM)
+VMEM = pl.BlockSpec(memory_space=pltpu.VMEM)
+
+
+def out_kernel(n, tile, where, scales, ctx_hbm, w_hbm, res_hbm, first, second, ctx, w, res, sems):
+    rows, width = first.shape[1:]
+    steps = width // tile
+    start = where[1] * width
+    loads = [
+        pltpu.make_async_copy(ctx_hbm, ctx, sems.at[0]),
+        pltpu.make_async_copy(
+            res_hbm.at[:, pl.ds(pl.multiple_of(start, width), width)], res, sems.at[1]
+        ),
+    ]
+    for j in range(steps):
+        columns = pl.ds(pl.multiple_of(start + j * tile, tile), tile)
+        loads.append(pltpu.make_async_copy(w_hbm.at[:, columns], w.at[j], sems.at[2 + j]))
+    for load in loads:
+        load.start()
+    loads[0].wait()
+    loads[1].wait()
+    for j in range(steps):
+        loads[2 + j].wait()
+        at = slice(j * tile, (j + 1) * tile)
+        term = jnp.dot(ctx[...], w[j], preferred_element_type=F32) * scales[0]
+        term = term.reshape(n, 2 * rows, tile)
+        mine = lax.broadcasted_iota(jnp.int32, term.shape, 0) == where[0]
+        term = (term + jnp.where(mine, res[:, at].astype(F32)[None], 0.0)).astype(BF16)
+        first[:, :, at] = term[:, :rows]
+        second[:, :, at] = term[:, rows:]
+
+
+def out_projection(context, w_out, resid, scales, z, which, n):
+    depth, width = w_out.shape[0], w_out.shape[1] // 2
+    rows = resid.shape[0] // 2
+    tile = min(256, width)
+    part = jax.ShapeDtypeStruct((n, rows, width), BF16)
+    first, second = pl.pallas_call(
+        functools.partial(out_kernel, n, tile),
+        out_shape=(part, part),
+        in_specs=[SMEM, SMEM, ANY, ANY, ANY],
+        out_specs=[VMEM, VMEM],
+        scratch_shapes=[
+            pltpu.VMEM(context.shape, BF16),
+            pltpu.VMEM((width // tile, depth, tile), BF16),
+            pltpu.VMEM((2 * rows, width), BF16),
+            pltpu.SemaphoreType.DMA((2 + width // tile,)),
+        ],
+        compiler_params=pltpu.CompilerParams(vmem_limit_bytes=16 << 20),
+        cost_estimate=pl.CostEstimate(
+            flops=2 * context.shape[0] * depth * width, bytes_accessed=2 * depth * width, transcendentals=0
+        ),
+    )(jnp.stack([z, which]).astype(jnp.int32), scales, in_hbm(context), in_hbm(w_out), in_hbm(resid))
+    return first.reshape(n * rows, -1), second.reshape(n * rows, -1)
+
+
+def fetch_kernel(blocks, which, w_hbm, *rest):
+    parts, sems = rest[:-1], rest[-1]
+    loads = []
+    for index, ((row, column), part) in enumerate(zip(blocks, parts)):
+        height, width = part.shape
+        at_row = pl.ds(pl.multiple_of(which[row] * height, height), height)
+        if column is None:
+            source = w_hbm.at[at_row, :]
+        else:
+            source = w_hbm.at[at_row, pl.ds(pl.multiple_of(which[column] * width, width), width)]
+        loads.append(pltpu.make_async_copy(source, part, sems.at[index]))
+    for load in loads:
+        load.start()
+    for load in loads:
+        load.wait()
+
+
+def fetch(w, which, blocks):
+    height = w.shape[0] // 2
+    parts = [
+        pltpu.VMEM((height, w.shape[1] if column is None else w.shape[1] // 2), BF16) for _, column in blocks
+    ]
+    return pl.pallas_call(
+        functools.partial(fetch_kernel, blocks),
+        out_shape=parts,
+        in_specs=[SMEM, ANY],
+        out_specs=[VMEM] * len(blocks),
+        scratch_shapes=[pltpu.SemaphoreType.DMA((len(blocks),))],
+        compiler_params=pltpu.CompilerParams(vmem_limit_bytes=2 << 20),
+        cost_estimate=pl.CostEstimate(flops=0, bytes_accessed=4 * w.size, transcendentals=0),
+    )(jnp.stack(which).astype(jnp.int32), in_hbm(w))
+
+
+def dot(x, w):
+    return jnp.dot(x, w, preferred_element_type=F32)
+
+
 def swapped(resid, context, w_out, w_in, w_down, scales):
     n = 4
     z, core = lax.axis_index("blk"), lax.axis_index("pair")
     odd = z & 1
     rows = resid.shape[0] // 2
     width = w_out.shape[1]
+    others = out_projection(context, w_out, resid, scales, z, 1 - odd, n)
+    owns = out_projection(context, w_out, resid, scales, z, odd, n)
     results = []
+    crossed = moved = down = None
+    others = others[0], after(others[1], owns[1])
+    summed = [add(owns[half], swap(others[half], "blk", n, 1)).astype(BF16) for half in range(2)]
+    near_far, near_near, far_far, far_near = fetch(
+        after(w_in, summed[0]), [odd, 1 - odd, core, 1 - core], [(0, 3), (0, 2), (1, 3), (1, 2)]
+    )
+    down_near, down_far = fetch(after(w_down, near_near), [core, 1 - core], [(0, None), (1, None)])
+    results = []
+    begun = (near_near, down_near)
+    moved = down = None
     for half in range(2):
-        ctx = context.reshape(n, 2, rows, -1)[:, half].reshape(n * rows, -1)
-        res = resid[half * rows:(half + 1) * rows].astype(F32)
-        attn = scales[0] * jnp.dot(ctx, w_out, preferred_element_type=F32)
-        mine = (jnp.arange(n) == z)[:, None, None]
-        part = (attn.reshape(n, rows, width) + jnp.where(mine, res[None], 0.0)).reshape(n * rows, width).astype(BF16)
-        own, other = halves(part, odd)
-        own = add(own, swap(other, "blk", n, 1)).astype(BF16)
-        own = add(own, swap(own, "blk", n, 2)).astype(BF16)
-        mixed = joined(own, swap(own, "blk", n, 1), odd)
-        pre = jnp.dot(mixed, w_in, preferred_element_type=F32).astype(BF16)
-        own, other = halves(pre, core)
-        own = add(own, swap(other, "pair", 2, 1)).astype(BF16)
-        own = add(own, swap(own, "sub", 2, 1))
+        crossed = after(swap(summed[half], "blk", n, 2), *begun)
+        own = add(summed[half], crossed).astype(BF16)
+        first = dot(own, near_far)
+        if not half:
+            summed[1] = after(summed[1], first)
+        far = swap(own, "blk", n, 1)
+        mixed = joined(own, far, odd)
+        other = (first + dot(far, far_far)).astype(BF16)
+        there = swap(other, "pair", 2, 1)
+        own = dot(own, near_near) + dot(far, far_near)
+        own = add(own, there).astype(BF16)
+        if half:
+            own = after(own, moved)
+        else:
+            begun = (own,)
+        moved = swap(own, "sub", 2, 1)
+        if half:
+            moved = after(moved, down)
+        own = add(own, moved)
         own = jax.nn.gelu(scales[1] * own, approximate=False).astype(BF16)
-        hidden = joined(own, swap(own, "pair", 2, 1), core)
-        mlp = jnp.dot(hidden, w_down, preferred_element_type=F32).astype(BF16).reshape(n, rows, width)
+        there = swap(own, "pair", 2, 1)
+        down = (dot(own, down_near) + dot(there, down_far)).astype(BF16)
+        mlp = down.reshape(n, rows, width)
 
         def of(owner):
             return lax.dynamic_index_in_dim(mlp, owner, 0, keepdims=False)

time: 118 us -> 104 us (0.88)
  Pallas kernels: 0 us -> 21.4 us
  waiting for transfers between devices: 56.9 us -> 40.7 us
  matrix products: 21.5 us -> 9.98 us
  starting transfers between devices: 25 us -> 21.9 us
  local copies, waits for them, and re-layouts: 4.22 us -> 1.39 us
  other arithmetic: 9.68 us -> 8.08 us
    pallas_call x0 -> x4, Pallas kernels: none -> 21.4 us  [the longest x2 11.6 us: fetch(): pl.pallas_call(functools.partial(fetch_kernel, blocks), out_shape=parts,...]
    ppermute x18, waiting for transfers between devices: 56.9 us -> 40.7 us  [swap(): return lax.ppermute(x, axis, [(i, i ^ flip) for i in range(size)])]
    dot_general x6 -> x12, matrix products: 21.5 us -> 9.98 us  [dot(): return jnp.dot(x, w, preferred_element_type=F32)]
    ppermute x18, starting transfers between devices: 25 us -> 21.9 us  [swap(): return lax.ppermute(x, axis, [(i, i ^ flip) for i in range(size)])]
    slice x1 -> x0, local copies, waits for them, and re-layouts: 1.28 us -> none  [swapped(): ctx = context.reshape(n, 2, rows, -1)[:, half].reshape(n * rows, -1)]
    convert_element_type x7 -> x4, other arithmetic: 1.5 us -> 0.3 us  [the longest x2 0.17 us: swapped(): add(owns[half], swap(others[half], 'blk', n, 1)).astype(BF16)]
  transfers between devices with their start and end apart: 18 -> 18, of which waited for: 11 -> 11; matrix products, arithmetic and copies ran while one was open for 19% -> 16% of each run, Pallas kernels for 0% -> 16%
where the time goes in v2:
time: 104 us
  waiting for transfers between devices  40.7 us (39%)
  starting transfers between devices  21.9 us (21%)
  Pallas kernels  21.4 us (21%)
  matrix products  9.98 us (10%)
  other arithmetic  8.08 us (8%)
  local copies, waits for them, and re-layouts  1.39 us (1%)
    ppermute x18, waiting for transfers between devices, swap(): return lax.ppermute(x, axis, [(i, i ^ flip) for i in range(size)])  40.7 us
    ppermute x18, starting transfers between devices, swap(): return lax.ppermute(x, axis, [(i, i ^ flip) for i in range(size)])  21.9 us
    pallas_call x2, Pallas kernels, fetch(): pl.pallas_call(functools.partial(fetch_kernel, blocks), out_shape=parts,...  11.6 us
    dot_general x12, matrix products, dot(): return jnp.dot(x, w, preferred_element_type=F32)  9.98 us
    pallas_call x2, Pallas kernels, out_projection(): pl.pallas_call(functools.partial(out_kernel, n, tile), out_shape=(part, p...  9.88 us
    convert_element_type x2, other arithmetic, swapped(): own = jax.nn.gelu(scales[1] * own, approximate=False).astype(BF16)  5.42 us
  transfers between devices with their start and end apart: 18, of which 11 were waited for; matrix products, arithmetic and copies ran while one was open for 16% of the time, Pallas kernels for 16%

profile of v2, /device:TPU:0, one launch (start us, length us, event | category | flops | bytes accessed | tf_op | source)
XLA Modules:
  0.0 103.8 jit_solution(12163052654738283492)
XLA Ops:
  0.7 4.9 %shard_map.65 = (bf16[4,32,1024]{2,1,0:T(8,128)(2,1)S(1)}, bf16[4,32,1024]{2,1,0:T(8,128)(2,1)S(1)}) custom-call(s32[2]{0:T(128)S(1)} %get-tuple-element.54.where, f32[3]{0:T(128)S(1)} %copy-done, bf16[256,2048]{1,0:T(8,128)(2,1)} %ctx_hbm.3, bf16[2048,2048]{1,0:T(8,128)(2,1)} %w_hbm.3, bf16[64,2048]{1,0:T(8,128)(2,1)} %res_hbm.3), custom_call_target="tpu_custom_call" | custom-call | flops 1073741824 | bytes 4194304 | tf_op jit(solution)/shard_map/pallas_call | solution.py:98
  5.7 3.1 %collective-permute-start.9 = (bf16[128,1024]{1,0:T(8,128)(2,1)S(1)}, bf16[128,1024]{1,0:T(8,128)(2,1)S(1)}, u32[]{:S(2)}, u32[]{:S(2)}) collective-permute-start(bf16[128,1024]{1,0:T(8,128)(2,1)S(1)} %bitcast.58), channel_id=1, source_target_pairs={{0,4},{4,0},{8,12},{12,8},{1,5},{5,1},{9,13},{13,9},{2,6},{6,2},{1... | collective-permute-start | bytes 786440 | tf_op jit(solution)/shard_map/ppermute | solution.py:32
  8.9 4.9 %shard_map.64 = (bf16[4,32,1024]{2,1,0:T(8,128)(2,1)S(1)}, bf16[4,32,1024]{2,1,0:T(8,128)(2,1)S(1)}) custom-call(s32[2]{0:T(128)S(1)} %get-tuple-element.53.where, f32[3]{0:T(128)S(1)} %copy-done.1, bf16[256,2048]{1,0:T(8,128)(2,1)} %ctx_hbm.3, bf16[2048,2048]{1,0:T(8,128)(2,1)} %w_hbm.3, bf16[64,2048]{1,0:T(8,128)(2,1)} %res_hbm.3), custom_call_target="tpu_custom_call" | custom-call | flops 1073741824 | bytes 4194304 | tf_op jit(solution)/shard_map/pallas_call | solution.py:98
  14.5 6.2 %collective-permute-done = bf16[128,1024]{1,0:T(8,128)(2,1)S(1)} collective-permute-done((bf16[128,1024]{1,0:T(8,128)(2,1)S(1)}, bf16[128,1024]{1,0:T(8,128)(2,1)S(1)}, u32[]{:S(2)}, u32[]{:S(2)}) %collective-permute-start) | collective-permute-done | bytes 262176 | tf_op jit(solution)/shard_map/ppermute | solution.py:32
  20.8 2.8 %collective-permute-start.1 = (bf16[128,1024]{1,0:T(8,128)(2,1)S(1)}, bf16[128,1024]{1,0:T(8,128)(2,1)S(1)}, u32[]{:S(2)}, u32[]{:S(2)}) collective-permute-start(bf16[128,1024]{1,0:T(8,128)(2,1)S(1)} %fusion.28), channel_id=1, source_target_pairs={{0,8},{4,12},{8,0},{12,4},{1,9},{5,13},{9,1},{13,5},{2,10},{6,14},... | collective-permute-start | bytes 786440 | tf_op jit(solution)/shard_map/ppermute | solution.py:32
  23.7 5.8 %shard_map.66 = (bf16[1024,1792]{1,0:T(8,128)(2,1)S(1)}, bf16[1024,1792]{1,0:T(8,128)(2,1)S(1)}, bf16[1024,1792]{1,0:T(8,128)(2,1)S(1)}, bf16[1024,1792]{1,0:T(8,128)(2,1)S(1)}) custom-call(s32[4]{0:T(128)S(1)} %pad_add_fusion.2.which, bf16[2048,3584]{1,0:T(8,128)(2,1)} %w_hbm.4), custom_call_target="tpu_custom_call" | custom-call | bytes 29360128 | tf_op jit(solution)/shard_map/pallas_call | solution.py:139
  29.5 5.7 %shard_map.67 = (bf16[1792,2048]{1,0:T(8,128)(2,1)S(1)}, bf16[1792,2048]{1,0:T(8,128)(2,1)S(1)}) custom-call(s32[2]{0:T(128)S(1)} %pad_add_fusion.3.which, bf16[3584,2048]{1,0:T(8,128)(2,1)} %w_hbm.5), custom_call_target="tpu_custom_call" | custom-call | bytes 29360128 | tf_op jit(solution)/shard_map/pallas_call | solution.py:139
  35.4 1.6 %collective-permute-start.2 = (bf16[128,1024]{1,0:T(8,128)(2,1)S(1)}, bf16[128,1024]{1,0:T(8,128)(2,1)S(1)}, u32[]{:S(2)}, u32[]{:S(2)}) collective-permute-start(bf16[128,1024]{1,0:T(8,128)(2,1)S(1)} %add_convert_fusion.2), channel_id=1, source_target_pairs={{0,4},{4,0},{8,12},{12,8},{1,5},{5,1},{9,13},{13,9},{2,6},{6,2},{1... | collective-permute-start | bytes 786440 | tf_op jit(solution)/shard_map/ppermute | solution.py:32
  37.7 1.9 %collective-permute-start.10 = (bf16[128,1024]{1,0:T(8,128)(2,1)S(1)}, bf16[128,1024]{1,0:T(8,128)(2,1)S(1)}, u32[]{:S(2)}, u32[]{:S(2)}) collective-permute-start(bf16[128,1024]{1,0:T(8,128)(2,1)S(1)} %add_convert_fusion.1), channel_id=1, source_target_pairs={{0,8},{4,12},{8,0},{12,4},{1,9},{5,13},{9,1},{13,5},{2,10},{6,14},... | collective-permute-start | bytes 786440 | tf_op jit(solution)/shard_map/ppermute | solution.py:32
  39.6 7.5 %collective-permute-done.2 = bf16[128,1024]{1,0:T(8,128)(2,1)S(1)} collective-permute-done((bf16[128,1024]{1,0:T(8,128)(2,1)S(1)}, bf16[128,1024]{1,0:T(8,128)(2,1)S(1)}, u32[]{:S(2)}, u32[]{:S(2)}) %collective-permute-start.2) | collective-permute-done | bytes 262176 | tf_op jit(solution)/shard_map/ppermute | solution.py:32
  50.3 1.2 %collective-permute-done.10 = bf16[128,1024]{1,0:T(8,128)(2,1)S(1)} collective-permute-done((bf16[128,1024]{1,0:T(8,128)(2,1)S(1)}, bf16[128,1024]{1,0:T(8,128)(2,1)S(1)}, u32[]{:S(2)}, u32[]{:S(2)}) %collective-permute-start.10) | collective-permute-done | bytes 262176 | tf_op jit(solution)/shard_map/ppermute | solution.py:32
  52.3 1.6 %collective-permute-start.4 = (bf16[128,1792]{1,0:T(8,128)(2,1)S(1)}, bf16[128,1792]{1,0:T(8,128)(2,1)S(1)}, u32[]{:S(2)}, u32[]{:S(2)}) collective-permute-start(bf16[128,1792]{1,0:T(8,128)(2,1)S(1)} %fusion.7), channel_id=1, source_target_pairs={{0,2},{2,0},{1,3},{3,1},{4,6},{6,4},{5,7},{7,5},{8,10},{10,8},{9,1... | collective-permute-start | bytes 1376264 | tf_op jit(solution)/shard_map/ppermute | solution.py:32
  54.5 5.0 %collective-permute-done.11 = bf16[128,1024]{1,0:T(8,128)(2,1)S(1)} collective-permute-done((bf16[128,1024]{1,0:T(8,128)(2,1)S(1)}, bf16[128,1024]{1,0:T(8,128)(2,1)S(1)}, u32[]{:S(2)}, u32[]{:S(2)}) %collective-permute-start.11) | collective-permute-done | bytes 262176 | tf_op jit(solution)/shard_map/ppermute | solution.py:32
  60.3 3.5 %collective-permute-done.4 = bf16[128,1792]{1,0:T(8,128)(2,1)S(1)} collective-permute-done((bf16[128,1792]{1,0:T(8,128)(2,1)S(1)}, bf16[128,1792]{1,0:T(8,128)(2,1)S(1)}, u32[]{:S(2)}, u32[]{:S(2)}) %collective-permute-start.4) | collective-permute-done | bytes 458784 | tf_op jit(solution)/shard_map/ppermute | solution.py:32
  63.8 2.7 %fusion.10 = bf16[128,1792]{1,0:T(8,128)(2,1)S(1)} fusion(bf16[128,1792]{1,0:T(8,128)(2,1)S(1)} %collective-permute-done.4, bf16[128,1792]{1,0:T(8,128)(2,1)S(1)} %fusion.7, f32[]{:T(128)} %bitcast.8), kind=kLoop, calls=%fused_computation.18 | loop fusion | flops 15826944 | bytes 1376260 | tf_op jit(solution)/shard_map/convert_element_type | solution.py:193
  68.4 1.6 %collective-permute-start.13 = (bf16[128,1792]{1,0:T(8,128)(2,1)S(1)}, bf16[128,1792]{1,0:T(8,128)(2,1)S(1)}, u32[]{:S(2)}, u32[]{:S(2)}) collective-permute-start(bf16[128,1792]{1,0:T(8,128)(2,1)S(1)} %fusion.6), channel_id=1, source_target_pairs={{0,2},{2,0},{1,3},{3,1},{4,6},{6,4},{5,7},{7,5},{8,10},{10,8},{9,1... | collective-permute-start | bytes 1376264 | tf_op jit(solution)/shard_map/ppermute | solution.py:32
  69.9 1.3 %fusion.2 = bf16[128,2048]{1,0:T(8,128)(2,1)S(1)} fusion(f32[128,2048]{1,0:T(8,128)S(1)} %fusion.44, bf16[128,1792]{1,0:T(8,128)(2,1)S(1)} %collective-permute-done.5, bf16[1792,2048]{1,0:T(8,128)(2,1)S(1)} %get-tuple-element.33), kind=kOutput, calls=%fused_computation.8 | convolution fusion | flops 940048384 | bytes 9371648 | tf_op jit(solution)/shard_map/dot_general | solution.py:151
  71.3 2.8 %collective-permute-start.6 = (bf16[32,2048]{1,0:T(8,128)(2,1)S(1)}, bf16[32,2048]{1,0:T(8,128)(2,1)S(1)}, u32[]{:S(2)}, u32[]{:S(2)}) collective-permute-start(bf16[32,2048]{1,0:T(8,128)(2,1)S(1)} %get-tuple-element.43), channel_id=1, source_target_pairs={{0,12},{4,8},{8,4},{12,0},{1,13},{5,9},{9,5},{13,1},{2,14},{6,10},... | collective-permute-start | bytes 393224 | tf_op jit(solution)/shard_map/ppermute | solution.py:32
  75.8 5.6 %collective-permute-done.13 = bf16[128,1792]{1,0:T(8,128)(2,1)S(1)} collective-permute-done((bf16[128,1792]{1,0:T(8,128)(2,1)S(1)}, bf16[128,1792]{1,0:T(8,128)(2,1)S(1)}, u32[]{:S(2)}, u32[]{:S(2)}) %collective-permute-start.13) | collective-permute-done | bytes 458784 | tf_op jit(solution)/shard_map/ppermute | solution.py:32
  81.4 2.7 %fusion.13 = bf16[128,1792]{1,0:T(8,128)(2,1)S(1)} fusion(bf16[128,1792]{1,0:T(8,128)(2,1)S(1)} %collective-permute-done.13, bf16[128,1792]{1,0:T(8,128)(2,1)S(1)} %fusion.6, f32[]{:T(128)} %bitcast.8), kind=kLoop, calls=%fused_computation.21 | loop fusion | flops 15826944 | bytes 1376260 | tf_op jit(solution)/shard_map/convert_element_type | solution.py:193
  87.1 2.8 %collective-permute-start.15 = (bf16[32,2048]{1,0:T(8,128)(2,1)S(1)}, bf16[32,2048]{1,0:T(8,128)(2,1)S(1)}, u32[]{:S(2)}, u32[]{:S(2)}) collective-permute-start(bf16[32,2048]{1,0:T(8,128)(2,1)S(1)} %get-tuple-element.48), channel_id=1, source_target_pairs={{0,12},{4,8},{8,4},{12,0},{1,13},{5,9},{9,5},{13,1},{2,14},{6,10},... | collective-permute-start | bytes 393224 | tf_op jit(solution)/shard_map/ppermute | solution.py:32
  92.3 3.1 %collective-permute-done.15 = bf16[32,2048]{1,0:T(8,128)(2,1)S(1)} collective-permute-done((bf16[32,2048]{1,0:T(8,128)(2,1)S(1)}, bf16[32,2048]{1,0:T(8,128)(2,1)S(1)}, u32[]{:S(2)}, u32[]{:S(2)}) %collective-permute-start.15) | collective-permute-done | bytes 131104 | tf_op jit(solution)/shard_map/ppermute | solution.py:32
  95.4 2.7 %collective-permute-done.17 = bf16[32,2048]{1,0:T(8,128)(2,1)S(1)} collective-permute-done((bf16[32,2048]{1,0:T(8,128)(2,1)S(1)}, bf16[32,2048]{1,0:T(8,128)(2,1)S(1)}, u32[]{:S(2)}, u32[]{:S(2)}) %collective-permute-start.17) | collective-permute-done | bytes 131104 | tf_op jit(solution)/shard_map/ppermute | solution.py:32
  98.1 4.3 %collective-permute-done.16 = bf16[32,2048]{1,0:T(8,128)(2,1)S(1)} collective-permute-done((bf16[32,2048]{1,0:T(8,128)(2,1)S(1)}, bf16[32,2048]{1,0:T(8,128)(2,1)S(1)}, u32[]{:S(2)}, u32[]{:S(2)}) %collective-permute-start.16) | collective-permute-done | bytes 131104 | tf_op jit(solution)/shard_map/ppermute | solution.py:32
  (49 shorter events, 18.2 us)
Async XLA Ops:
  0.1 0.7 copy-start
  0.7 8.1 %copy-start.1 = (f32[3]{0:T(128)S(1)}, f32[3]{0:T(128)}, u32[]{:S(2)}) copy-start(f32[3]{0:T(128)} %scales.3) | copy-start | bytes 40
  5.7 29.6 %collective-permute-start.9 = (bf16[128,1024]{1,0:T(8,128)(2,1)S(1)}, bf16[128,1024]{1,0:T(8,128)(2,1)S(1)}, u32[]{:S(2)}, u32[]{:S(2)}) collective-permute-start(bf16[128,1024]{1,0:T(8,128)(2,1)S(1)} %bitcast.58), channel_id=1, source_target_pairs={{0,4},{4,0},{8,12},{12,8},{1,5},{5,1},{9,13},{13,9},{2,6},{6,2},{1... | collective-permute-start | bytes 786440 | tf_op jit(solution)/shard_map/ppermute | solution.py:32
  8.8 11.9 %collective-permute-start = (bf16[128,1024]{1,0:T(8,128)(2,1)S(1)}, bf16[128,1024]{1,0:T(8,128)(2,1)S(1)}, u32[]{:S(2)}, u32[]{:S(2)}) collective-permute-start(bf16[128,1024]{1,0:T(8,128)(2,1)S(1)} %bitcast.59), channel_id=1, source_target_pairs={{0,4},{4,0},{8,12},{12,8},{1,5},{5,1},{9,13},{13,9},{2,6},{6,2},{1... | collective-permute-start | bytes 786440 | tf_op jit(solution)/shard_map/ppermute | solution.py:32
  20.8 14.6 %collective-permute-start.1 = (bf16[128,1024]{1,0:T(8,128)(2,1)S(1)}, bf16[128,1024]{1,0:T(8,128)(2,1)S(1)}, u32[]{:S(2)}, u32[]{:S(2)}) collective-permute-start(bf16[128,1024]{1,0:T(8,128)(2,1)S(1)} %fusion.28), channel_id=1, source_target_pairs={{0,8},{4,12},{8,0},{12,4},{1,9},{5,13},{9,1},{13,5},{2,10},{6,14},... | collective-permute-start | bytes 786440 | tf_op jit(solution)/shard_map/ppermute | solution.py:32
  35.4 11.6 %collective-permute-start.2 = (bf16[128,1024]{1,0:T(8,128)(2,1)S(1)}, bf16[128,1024]{1,0:T(8,128)(2,1)S(1)}, u32[]{:S(2)}, u32[]{:S(2)}) collective-permute-start(bf16[128,1024]{1,0:T(8,128)(2,1)S(1)} %add_convert_fusion.2), channel_id=1, source_target_pairs={{0,4},{4,0},{8,12},{12,8},{1,5},{5,1},{9,13},{13,9},{2,6},{6,2},{1... | collective-permute-start | bytes 786440 | tf_op jit(solution)/shard_map/ppermute | solution.py:32
  37.7 13.7 %collective-permute-start.10 = (bf16[128,1024]{1,0:T(8,128)(2,1)S(1)}, bf16[128,1024]{1,0:T(8,128)(2,1)S(1)}, u32[]{:S(2)}, u32[]{:S(2)}) collective-permute-start(bf16[128,1024]{1,0:T(8,128)(2,1)S(1)} %add_convert_fusion.1), channel_id=1, source_target_pairs={{0,8},{4,12},{8,0},{12,4},{1,9},{5,13},{9,1},{13,5},{2,10},{6,14},... | collective-permute-start | bytes 786440 | tf_op jit(solution)/shard_map/ppermute | solution.py:32
  47.7 1.9 %collective-permute-start.3 = (bf16[128,1792]{1,0:T(8,128)(2,1)S(1)}, bf16[128,1792]{1,0:T(8,128)(2,1)S(1)}, u32[]{:S(2)}, u32[]{:S(2)}) collective-permute-start(bf16[128,1792]{1,0:T(8,128)(2,1)S(1)} %fusion.4), channel_id=1, source_target_pairs={{0,1},{1,0},{2,3},{3,2},{4,5},{5,4},{6,7},{7,6},{8,9},{9,8},{10,11... | collective-permute-start | bytes 1376264 | tf_op jit(solution)/shard_map/ppermute | solution.py:32
  52.2 7.2 %collective-permute-start.11 = (bf16[128,1024]{1,0:T(8,128)(2,1)S(1)}, bf16[128,1024]{1,0:T(8,128)(2,1)S(1)}, u32[]{:S(2)}, u32[]{:S(2)}) collective-permute-start(bf16[128,1024]{1,0:T(8,128)(2,1)S(1)} %add_convert_fusion), channel_id=1, source_target_pairs={{0,4},{4,0},{8,12},{12,8},{1,5},{5,1},{9,13},{13,9},{2,6},{6,2},{1... | collective-permute-start | bytes 786440 | tf_op jit(solution)/shard_map/ppermute | solution.py:32
  52.3 11.5 %collective-permute-start.4 = (bf16[128,1792]{1,0:T(8,128)(2,1)S(1)}, bf16[128,1792]{1,0:T(8,128)(2,1)S(1)}, u32[]{:S(2)}, u32[]{:S(2)}) collective-permute-start(bf16[128,1792]{1,0:T(8,128)(2,1)S(1)} %fusion.7), channel_id=1, source_target_pairs={{0,2},{2,0},{1,3},{3,1},{4,6},{6,4},{5,7},{7,5},{8,10},{10,8},{9,1... | collective-permute-start | bytes 1376264 | tf_op jit(solution)/shard_map/ppermute | solution.py:32
  60.1 7.5 %collective-permute-start.12 = (bf16[128,1792]{1,0:T(8,128)(2,1)S(1)}, bf16[128,1792]{1,0:T(8,128)(2,1)S(1)}, u32[]{:S(2)}, u32[]{:S(2)}) collective-permute-start(bf16[128,1792]{1,0:T(8,128)(2,1)S(1)} %fusion.5), channel_id=1, source_target_pairs={{0,1},{1,0},{2,3},{3,2},{4,5},{5,4},{6,7},{7,6},{8,9},{9,8},{10,11... | collective-permute-start | bytes 1376264 | tf_op jit(solution)/shard_map/ppermute | solution.py:32
  66.5 3.5 %collective-permute-start.5 = (bf16[128,1792]{1,0:T(8,128)(2,1)S(1)}, bf16[128,1792]{1,0:T(8,128)(2,1)S(1)}, u32[]{:S(2)}, u32[]{:S(2)}) collective-permute-start(bf16[128,1792]{1,0:T(8,128)(2,1)S(1)} %fusion.10), channel_id=1, source_target_pairs={{0,1},{1,0},{2,3},{3,2},{4,5},{5,4},{6,7},{7,6},{8,9},{9,8},{10,11... | collective-permute-start | bytes 1376264 | tf_op jit(solution)/shard_map/ppermute | solution.py:32
  68.4 13.0 %collective-permute-start.13 = (bf16[128,1792]{1,0:T(8,128)(2,1)S(1)}, bf16[128,1792]{1,0:T(8,128)(2,1)S(1)}, u32[]{:S(2)}, u32[]{:S(2)}) collective-permute-start(bf16[128,1792]{1,0:T(8,128)(2,1)S(1)} %fusion.6), channel_id=1, source_target_pairs={{0,2},{2,0},{1,3},{3,1},{4,6},{6,4},{5,7},{7,5},{8,10},{10,8},{9,1... | collective-permute-start | bytes 1376264 | tf_op jit(solution)/shard_map/ppermute | solution.py:32
  71.3 19.4 %collective-permute-start.6 = (bf16[32,2048]{1,0:T(8,128)(2,1)S(1)}, bf16[32,2048]{1,0:T(8,128)(2,1)S(1)}, u32[]{:S(2)}, u32[]{:S(2)}) collective-permute-start(bf16[32,2048]{1,0:T(8,128)(2,1)S(1)} %get-tuple-element.43), channel_id=1, source_target_pairs={{0,12},{4,8},{8,4},{12,0},{1,13},{5,9},{9,5},{13,1},{2,14},{6,10},... | collective-permute-start | bytes 393224 | tf_op jit(solution)/shard_map/ppermute | solution.py:32
  74.1 17.5 %collective-permute-start.8 = (bf16[32,2048]{1,0:T(8,128)(2,1)S(1)}, bf16[32,2048]{1,0:T(8,128)(2,1)S(1)}, u32[]{:S(2)}, u32[]{:S(2)}) collective-permute-start(bf16[32,2048]{1,0:T(8,128)(2,1)S(1)} %get-tuple-element.44), channel_id=1, source_target_pairs={{0,4},{4,0},{8,12},{12,8},{1,5},{5,1},{9,13},{13,9},{2,6},{6,2},{1... | collective-permute-start | bytes 393224 | tf_op jit(solution)/shard_map/ppermute | solution.py:32
  74.9 16.7 %collective-permute-start.7 = (bf16[32,2048]{1,0:T(8,128)(2,1)S(1)}, bf16[32,2048]{1,0:T(8,128)(2,1)S(1)}, u32[]{:S(2)}, u32[]{:S(2)}) collective-permute-start(bf16[32,2048]{1,0:T(8,128)(2,1)S(1)} %get-tuple-element.45), channel_id=1, source_target_pairs={{0,8},{4,12},{8,0},{12,4},{1,9},{5,13},{9,1},{13,5},{2,10},{6,14},... | collective-permute-start | bytes 393224 | tf_op jit(solution)/shard_map/ppermute | solution.py:32
  84.1 1.9 %collective-permute-start.14 = (bf16[128,1792]{1,0:T(8,128)(2,1)S(1)}, bf16[128,1792]{1,0:T(8,128)(2,1)S(1)}, u32[]{:S(2)}, u32[]{:S(2)}) collective-permute-start(bf16[128,1792]{1,0:T(8,128)(2,1)S(1)} %fusion.13), channel_id=1, source_target_pairs={{0,1},{1,0},{2,3},{3,2},{4,5},{5,4},{6,7},{7,6},{8,9},{9,8},{10,11... | collective-permute-start | bytes 1376264 | tf_op jit(solution)/shard_map/ppermute | solution.py:32
  87.1 8.3 %collective-permute-start.15 = (bf16[32,2048]{1,0:T(8,128)(2,1)S(1)}, bf16[32,2048]{1,0:T(8,128)(2,1)S(1)}, u32[]{:S(2)}, u32[]{:S(2)}) collective-permute-start(bf16[32,2048]{1,0:T(8,128)(2,1)S(1)} %get-tuple-element.48), channel_id=1, source_target_pairs={{0,12},{4,8},{8,4},{12,0},{1,13},{5,9},{9,5},{13,1},{2,14},{6,10},... | collective-permute-start | bytes 393224 | tf_op jit(solution)/shard_map/ppermute | solution.py:32
  89.9 8.1 %collective-permute-start.17 = (bf16[32,2048]{1,0:T(8,128)(2,1)S(1)}, bf16[32,2048]{1,0:T(8,128)(2,1)S(1)}, u32[]{:S(2)}, u32[]{:S(2)}) collective-permute-start(bf16[32,2048]{1,0:T(8,128)(2,1)S(1)} %get-tuple-element.49), channel_id=1, source_target_pairs={{0,4},{4,0},{8,12},{12,8},{1,5},{5,1},{9,13},{13,9},{2,6},{6,2},{1... | collective-permute-start | bytes 393224 | tf_op jit(solution)/shard_map/ppermute | solution.py:32
  90.7 11.7 %collective-permute-start.16 = (bf16[32,2048]{1,0:T(8,128)(2,1)S(1)}, bf16[32,2048]{1,0:T(8,128)(2,1)S(1)}, u32[]{:S(2)}, u32[]{:S(2)}) collective-permute-start(bf16[32,2048]{1,0:T(8,128)(2,1)S(1)} %get-tuple-element.50), channel_id=1, source_target_pairs={{0,8},{4,12},{8,0},{12,4},{1,9},{5,13},{9,1},{13,5},{2,10},{6,14},... | collective-permute-start | bytes 393224 | tf_op jit(solution)/shard_map/ppermute | solution.py:32

commit v3 on v1

v3 whole, which is shorter than its diff:
```python
import functools
import math

import jax
import jax.numpy as jnp
from jax import lax
from jax.experimental import pallas as pl
from jax.experimental.pallas import tpu as pltpu
from jax.sharding import PartitionSpec as P

F32 = jnp.float32
BF16 = jnp.bfloat16


def general(resid, context, w_out, w_in, w_down, scales):
    attn = lax.psum_scatter(
        jnp.dot(context, w_out, preferred_element_type=F32).astype(BF16), "blk", scatter_dimension=0, tiled=True
    ).astype(F32)
    mixed = (resid.astype(F32) + scales[0] * attn).astype(BF16)
    pre_terms = jnp.dot(lax.all_gather(mixed, "blk", axis=0, tiled=True), w_in, preferred_element_type=F32)
    pre_part = lax.psum_scatter(
        pre_terms.astype(BF16), ("sub", "pair"), scatter_dimension=0, tiled=True
    ).astype(F32)
    hidden_part = jax.nn.gelu(scales[1] * pre_part, approximate=False).astype(BF16)
    hidden = lax.all_gather(hidden_part, ("sub", "pair"), axis=0, tiled=True)
    mlp = lax.psum_scatter(
        jnp.dot(hidden, w_down, preferred_element_type=F32).astype(BF16), "blk", scatter_dimension=0, tiled=True
    ).astype(F32)
    return (mixed.astype(F32) + scales[2] * mlp).astype(BF16)


def swap(x, axis, size, flip):
    return lax.ppermute(x, axis, [(i, i ^ flip) for i in range(size)])


def add(a, b):
    return a.astype(F32) + b.astype(F32)


def dot(x, w):
    return jnp.dot(x, w, preferred_element_type=F32)


def in_hbm(x):
    return pltpu.with_memory_space_constraint(x, pltpu.HBM)


ANY = pl.BlockSpec(memory_space=pl.ANY)
SMEM = pl.BlockSpec(memory_space=pltpu.SMEM)
VMEM = pl.BlockSpec(memory_space=pltpu.VMEM)


def nothing(*refs):
    pass


def after(x, *done):
    return pl.pallas_call(
        nothing,
        out_shape=jax.ShapeDtypeStruct(x.shape, x.dtype),
        in_specs=[ANY] * (1 + len(done)),
        out_specs=ANY,
        input_output_aliases={0: 0},
        compiler_params=pltpu.CompilerParams(vmem_limit_bytes=1 << 20),
    )(x, *done)


def sent(mlp, n):
    z = lax.axis_index("blk")
    blocks = mlp.reshape(n, mlp.shape[0] // n, -1)
    return [swap(lax.dynamic_index_in_dim(blocks, z ^ flip, 0, keepdims=False), "blk", n, flip) for flip in (3, 2, 1)]


def out_kernel(pieces, near, scales_hbm, ctx_hbm, w_hbm, res_hbm, *rest):
    parts, (ctx, w, res, acc, scales, sems) = rest[:-6], rest[-6:]
    depth, width = w.shape
    block = depth // pieces
    tile = min(256, width)
    z = lax.axis_index("blk")
    which = (z & 1) if near else 1 - (z & 1)
    columns = pl.ds(pl.multiple_of(which * width, width), width)
    loads = []
    for k in range(pieces):
        at = pl.ds(k * block, block)
        loads.append(
            (
                pltpu.make_async_copy(ctx_hbm.at[:, at], ctx.at[:, at], sems.at[2 + 2 * k]),
                pltpu.make_async_copy(w_hbm.at[at, columns], w.at[at], sems.at[3 + 2 * k]),
            )
        )
    last = (
        pltpu.make_async_copy(res_hbm.at[:, columns], res, sems.at[0]),
        pltpu.make_async_copy(scales_hbm, scales, sems.at[1]),
    )
    for load in [load for pair in loads for load in pair] + list(last):
        load.start()
    for k in range(pieces):
        for load in loads[k] + (last if k == pieces - 1 else ()):
            load.wait()
        deep = slice(k * block, (k + 1) * block)
        for c in range(width // tile):
            at = slice(c * tile, (c + 1) * tile)
            term = dot(ctx[:, deep], w[deep, at])
            if k:
                term = acc[:, at] + term
            if k < pieces - 1:
                acc[:, at] = term
                continue
            term = (term * scales[0]).reshape(-1, res.shape[0], tile)
            mine = lax.broadcasted_iota(jnp.int32, term.shape, 0) == z
            term = (term + jnp.where(mine, res[:, at].astype(F32)[None], 0.0)).astype(BF16)
            start = 0
            for part in parts:
                part[:, :, at] = term[:, start:start + part.shape[1]]
                start += part.shape[1]


def out_projection(context, w_out, resid, scales, near, sizes):
    depth, width = w_out.shape[0], w_out.shape[1] // 2
    pieces = 8
    n = context.shape[0] // resid.shape[0]
    parts = pl.pallas_call(
        functools.partial(out_kernel, pieces, near),
        out_shape=[jax.ShapeDtypeStruct((n, size, width), BF16) for size in sizes],
        in_specs=[ANY] * 4,
        out_specs=[VMEM] * len(sizes),
        scratch_shapes=[
            pltpu.VMEM(context.shape, BF16),
            pltpu.VMEM((depth, width), BF16),
            pltpu.VMEM((resid.shape[0], width), BF16),
            pltpu.VMEM((context.shape[0], width), F32),
            pltpu.SMEM(scales.shape, F32),
            pltpu.SemaphoreType.DMA((2 + 2 * pieces,)),
        ],
        compiler_params=pltpu.CompilerParams(vmem_limit_bytes=9 << 20),
        cost_estimate=pl.CostEstimate(
            flops=2 * context.shape[0] * depth * width, bytes_accessed=2 * depth * width, transcendentals=0
        ),
    )(in_hbm(scales), in_hbm(context), in_hbm(w_out), in_hbm(resid))
    return [part.reshape(n * size, width) for part, size in zip(parts, sizes)]


def fetch_kernel(w_hbm, done, *rest):
    parts, token, sems = rest[:-2], rest[-2], rest[-1]
    token[...] = jnp.zeros_like(token)
    height, width = parts[0].shape
    odd, core = lax.axis_index("blk") & 1, lax.axis_index("pair")
    blocks = [(odd, 1 - core), (odd, core), (1 - odd, 1 - core), (1 - odd, core)]
    loads = []
    for index, ((row, column), part) in enumerate(zip(blocks, parts)):
        at_row = pl.ds(pl.multiple_of(row * height, height), height)
        at_column = pl.ds(pl.multiple_of(column * width, width), width)
        loads.append(pltpu.make_async_copy(w_hbm.at[at_row, at_column], part, sems.at[index]))
        loads[index].start()
    for load in loads:
        load.wait()


def fetch(w, done):
    part = pltpu.VMEM((w.shape[0] // 2, w.shape[1] // 2), BF16)
    return pl.pallas_call(
        fetch_kernel,
        out_shape=[part] * 4 + [jax.ShapeDtypeStruct((8, 128), F32)],
        in_specs=[ANY, ANY],
        out_specs=[VMEM] * 5,
        scratch_shapes=[pltpu.SemaphoreType.DMA((4,))],
        compiler_params=pltpu.CompilerParams(vmem_limit_bytes=2 << 20),
        cost_estimate=pl.CostEstimate(flops=0, bytes_accessed=1024, transcendentals=0),
    )(in_hbm(w), done)


def gelu_kernel(scales, own, there, out):
    tile = 256
    for start in range(0, out.shape[1], tile):
        at = slice(start, min(start + tile, out.shape[1]))
        v = scales[1] * add(own[:, at], there[:, at])
        out[:, at] = (0.5 * v * (1.0 + lax.erf(v * math.sqrt(0.5)))).astype(BF16)


def gelu(scales, own, there):
    return pl.pallas_call(
        gelu_kernel,
        out_shape=jax.ShapeDtypeStruct(own.shape, BF16),
        in_specs=[SMEM, VMEM, VMEM],
        out_specs=VMEM,
        compiler_params=pltpu.CompilerParams(vmem_limit_bytes=3 << 20),
    )(scales, own, there)


def down_kernel(pieces, hidden, w_hbm, out, w, acc, sems):
    depth, width = w.shape
    block, tile = depth // pieces, min(512, width)
    loads = []
    for k in range(pieces):
        at = pl.ds(k * block, block)
        loads.append(pltpu.make_async_copy(w_hbm.at[at], w.at[at], sems.at[k]))
        loads[k].start()
    for k in range(pieces):
        loads[k].wait()
        deep = slice(k * block, (k + 1) * block)
        for c in range(width // tile):
            at = slice(c * tile, (c + 1) * tile)
            term = dot(hidden[:, deep], w[deep, at])
            if k:
                term = acc[:, at] + term
            if k < pieces - 1:
                acc[:, at] = term
            else:
                out[:, at] = term.astype(BF16)


def down_projection(hidden, w):
    rows, width = hidden.shape[0], w.shape[1]
    pieces = 7
    return pl.pallas_call(
        functools.partial(down_kernel, pieces),
        out_shape=jax.ShapeDtypeStruct((rows, width), BF16),
        in_specs=[VMEM, ANY],
        out_specs=VMEM,
        scratch_shapes=[
            pltpu.VMEM(w.shape, BF16),
            pltpu.VMEM((rows, width), F32),
            pltpu.SemaphoreType.DMA((pieces,)),
        ],
        compiler_params=pltpu.CompilerParams(vmem_limit_bytes=18 << 20),
        cost_estimate=pl.CostEstimate(flops=2 * rows * w.size, bytes_accessed=2 * w.size, transcendentals=0),
    )(hidden, in_hbm(w))


def end_kernel(scales, done, near, far, mlp, first, second, third, out):
    z = lax.axis_index("blk")
    odd = (z & 1) == 1
    size, width = first.shape[0], out.shape[1] // 2
    rows = pl.ds(pl.multiple_of(z * size, size), size)
    head = out.shape[0] - size
    out[:head, :] = done[...]
    for part in range(2):
        at = slice(part * width, (part + 1) * width)
        total = mlp[rows, at].astype(F32)
        for term in (first, second, third):
            total = total + term[:, at].astype(F32)
        other, own = (far, near) if part == 0 else (near, far)
        mixed = jnp.where(odd, other[rows, :].astype(F32), own[rows, :].astype(F32))
        out[head:, at] = (mixed + scales[2] * total).astype(BF16)


def end(scales, done, near, far, mlp, terms):
    rows, width = done.shape[0] + terms[0].shape[0], done.shape[1]
    return pl.pallas_call(
        end_kernel,
        out_shape=jax.ShapeDtypeStruct((rows, width), BF16),
        in_specs=[SMEM] + [VMEM] * 7,
        out_specs=VMEM,
        compiler_params=pltpu.CompilerParams(vmem_limit_bytes=3 << 20),
    )(scales, done, near, far, mlp, *terms)


def swapped(resid, context, w_out, w_in, w_down, scales):
    n = 4
    z, core = lax.axis_index("blk"), lax.axis_index("pair")
    odd = (z & 1) == 1
    rows = resid.shape[0] // 2
    sizes = [rows, rows]

    other_a, other_b = out_projection(context, w_out, resid, scales, False, sizes)
    own_a, own_b = out_projection(context, w_out, resid, scales, True, sizes)
    other_b = after(other_b, own_a)
    sum_a = add(own_a, swap(other_a, "blk", n, 1)).astype(BF16)
    sum_b = add(own_b, swap(other_b, "blk", n, 1)).astype(BF16)
    near_far, near_near, far_far, far_near, fetched = fetch(w_in, sum_a)

    crossed = after(swap(sum_a, "blk", n, 2), fetched, sum_b)
    near_a = add(sum_a, crossed).astype(BF16)
    first = dot(near_a, near_far)
    sum_b = after(sum_b, first)
    far_a = swap(near_a, "blk", n, 1)
    crossed = swap(sum_b, "blk", n, 2)
    other = (first + dot(far_a, far_far)).astype(BF16)
    mine = dot(near_a, near_near) + dot(far_a, far_near)
    mine_a = add(mine, swap(other, "pair", 2, 1)).astype(BF16)

    crossed = after(crossed, other)
    near_b = add(sum_b, crossed).astype(BF16)
    width = mine_a.shape[1] // 2
    left_a = swap(mine_a[:, :width], "sub", 2, 1)
    right_a = swap(mine_a[:, width:], "sub", 2, 1)
    far_b = after(swap(near_b, "blk", n, 1), left_a)
    mine = dot(near_b, near_near)
    first = dot(near_b, near_far)
    far_b = after(far_b, mine, first)
    mine = mine + dot(far_b, far_near)
    other = (first + dot(far_b, far_far)).astype(BF16)
    there = lax.dynamic_index_in_dim(lax.all_gather(other, "pair", axis=0), 1 - core, 0, keepdims=False)
    mine_b = add(mine, there).astype(BF16)
    right_a = after(right_a, mine_b)
    mine_b = after(mine_b, right_a)
    moved_b = swap(mine_b, "sub", 2, 1)

    hidden = gelu(scales, mine_a, jnp.concatenate([left_a, right_a], axis=1))
    there = swap(hidden, "pair", 2, 1)
    first_core = core == 0
    hidden = jnp.concatenate([jnp.where(first_core, hidden, there), jnp.where(first_core, there, hidden)], axis=1)
    mlp_a = down_projection(hidden, w_down)
    terms_a = sent(mlp_a, n)
    kept = [lax.dynamic_slice_in_dim(part, z * rows, rows, 0) for part in (near_a, far_a)]
    kept = jnp.concatenate([jnp.where(odd, kept[1], kept[0]), jnp.where(odd, kept[0], kept[1])], axis=1)
    total = lax.dynamic_slice_in_dim(mlp_a, z * rows, rows, 0).astype(F32)
    for term in terms_a:
        total = total + term.astype(F32)
    done = (kept.astype(F32) + scales[2] * total).astype(BF16)

    hidden = gelu(scales, mine_b, after(moved_b, mlp_a))
    hidden = lax.all_gather(hidden, "pair", axis=0)
    mlp_b = dot(jnp.concatenate([hidden[0], hidden[1]], axis=1), w_down).astype(BF16)
    return end(scales, done, near_b, far_b, mlp_b, sent(mlp_b, n))


def solution(mesh):
    shape = dict(mesh.shape)
    fast = shape["blk"] == 4 and shape["sub"] == 2 and shape["pair"] == 2
    in_specs = (
        P(("groups", "blk"), ("sub", "pair")),
        P("groups", "blk"),
        P("blk", ("sub", "pair")),
        P(("sub", "pair"), "blk"),
        P("blk", ("sub", "pair")),
        P(),
    )
    out_specs = P(("groups", "blk"), ("sub", "pair"))
    local = swapped if fast else general
    return jax.shard_map(local, mesh=mesh, in_specs=in_specs, out_specs=out_specs, check_vma=False)
```

time: 118 us -> 90.8 us (0.77)
  waiting for transfers between devices: 56.9 us -> 31.1 us
  Pallas kernels: 0 us -> 20.7 us
  matrix products: 21.5 us -> 7.44 us
  other arithmetic: 9.68 us -> 1.28 us
  blocking collectives: 0 us -> 5.11 us
  local copies, waits for them, and re-layouts: 4.22 us -> 0.78 us
    ppermute x18 -> x17, waiting for transfers between devices: 56.9 us -> 31.1 us  [swap(): return lax.ppermute(x, axis, [(i, i ^ flip) for i in range(size)])]
    pallas_call x0 -> x16, Pallas kernels: none -> 20.7 us  [the longest x1 6.37 us: down_projection(): pl.pallas_call(functools.partial(down_kernel, pieces), out_shape=jax.Shap...]
    dot_general x6 -> x9, matrix products: 21.5 us -> 7.44 us  [dot(): return jnp.dot(x, w, preferred_element_type=F32)]
    convert_element_type x11 -> x5, other arithmetic: 8.41 us -> 1.04 us  [the longest x1 0.74 us: swapped(): done = (kept.astype(F32) + scales[2] * total).astype(BF16)]
    all_gather x0 -> x2, blocking collectives: none -> 5.11 us  [the longest x1 2.64 us: swapped(): hidden = lax.all_gather(hidden, 'pair', axis=0)]
    slice x2 -> x3, local copies, waits for them, and re-layouts: 2.63 us -> 0.68 us  [the longest x1 0.58 us: swapped(): done = (kept.astype(F32) + scales[2] * total).astype(BF16)]
    unnamed x20 -> x10, local copies, waits for them, and re-layouts: 1.22 us -> 0.03 us
    ppermute x18 -> x17, starting transfers between devices: 25 us -> 23.9 us  [swap(): return lax.ppermute(x, axis, [(i, i ^ flip) for i in range(size)])]
  transfers between devices with their start and end apart: 18 -> 17, of which waited for: 11 -> 11; matrix products, arithmetic and copies ran while one was open for 19% -> 10% of each run, Pallas kernels for 0% -> 17%
where the time goes in v3:
time: 90.8 us; the launch traced here: 90.7 us
  waiting for transfers between devices  31.1 us (34%)
  starting transfers between devices  23.9 us (26%)
  Pallas kernels  20.7 us (23%)
  matrix products  7.44 us (8%)
  blocking collectives  5.11 us (6%)
  other arithmetic  1.28 us (1%)
    ppermute x17, waiting for transfers between devices, swap(): return lax.ppermute(x, axis, [(i, i ^ flip) for i in range(size)])  31.1 us
    ppermute x17, starting transfers between devices, swap(): return lax.ppermute(x, axis, [(i, i ^ flip) for i in range(size)])  23.9 us
    dot_general x9, matrix products, dot(): return jnp.dot(x, w, preferred_element_type=F32)  7.44 us
    pallas_call x1, Pallas kernels, down_projection(): pl.pallas_call(functools.partial(down_kernel, pieces), out_shape=jax.Shap...  6.37 us
    pallas_call x2, Pallas kernels, out_projection(): pl.pallas_call(functools.partial(out_kernel, pieces, near), out_shape=[ja...  5.99 us
    pallas_call x1, Pallas kernels, fetch(): pl.pallas_call(fetch_kernel, out_shape=[part] * 4 + [jax.ShapeDtypeStruct...  5.28 us
    all_gather x1, blocking collectives, swapped(): hidden = lax.all_gather(hidden, 'pair', axis=0)  2.64 us
    all_gather x1, blocking collectives, swapped(): lax.all_gather(other, 'pair', axis=0)  2.46 us
  transfers between devices with their start and end apart: 17, of which 11 were waited for; matrix products, arithmetic and copies ran while one was open for 10% of the time, Pallas kernels for 17%

profile of v3, /device:TPU:0, one launch (start us, length us, event | category | flops | bytes accessed | tf_op | source)
XLA Modules:
  0.0 90.7 jit_solution(15239704248541338463)
XLA Ops:
  0.0 3.0 %shard_map.65 = (bf16[4,32,1024]{2,1,0:T(8,128)(2,1)S(1)}, bf16[4,32,1024]{2,1,0:T(8,128)(2,1)S(1)}) custom-call(f32[3]{0:T(128)} %scales.5, bf16[256,2048]{1,0:T(8,128)(2,1)} %ctx_hbm.3, bf16[2048,2048]{1,0:T(8,128)(2,1)} %w_hbm.5, bf16[64,2048]{1,0:T(8,128)(2,1)} %res_hbm.3), custom_call_target="tpu_custom_call" | custom-call | flops 1073741824 | bytes 4194304 | tf_op jit(solution)/shard_map/pallas_call | solution.py:122
  3.0 3.1 %collective-permute-start = (bf16[128,1024]{1,0:T(8,128)(2,1)S(1)}, bf16[128,1024]{1,0:T(8,128)(2,1)S(1)}, u32[]{:S(2)}, u32[]{:S(2)}) collective-permute-start(bf16[128,1024]{1,0:T(8,128)(2,1)S(1)} %bitcast.47), channel_id=1, source_target_pairs={{0,4},{4,0},{8,12},{12,8},{1,5},{5,1},{9,13},{13,9},{2,6},{6,2},{1... | collective-permute-start | bytes 786440 | tf_op jit(solution)/shard_map/ppermute | solution.py:33
  6.1 3.0 %shard_map.64 = (bf16[4,32,1024]{2,1,0:T(8,128)(2,1)S(1)}, bf16[4,32,1024]{2,1,0:T(8,128)(2,1)S(1)}) custom-call(f32[3]{0:T(128)} %scales.5, bf16[256,2048]{1,0:T(8,128)(2,1)} %ctx_hbm.3, bf16[2048,2048]{1,0:T(8,128)(2,1)} %w_hbm.5, bf16[64,2048]{1,0:T(8,128)(2,1)} %res_hbm.3), custom_call_target="tpu_custom_call" | custom-call | flops 1073741824 | bytes 4194304 | tf_op jit(solution)/shard_map/pallas_call | solution.py:122
  9.2 4.0 %collective-permute-done = bf16[128,1024]{1,0:T(8,128)(2,1)S(1)} collective-permute-done((bf16[128,1024]{1,0:T(8,128)(2,1)S(1)}, bf16[128,1024]{1,0:T(8,128)(2,1)S(1)}, u32[]{:S(2)}, u32[]{:S(2)}) %collective-permute-start) | collective-permute-done | bytes 262176 | tf_op jit(solution)/shard_map/ppermute | solution.py:33
  13.3 3.1 %collective-permute-start.1 = (bf16[128,1024]{1,0:T(8,128)(2,1)S(1)}, bf16[128,1024]{1,0:T(8,128)(2,1)S(1)}, u32[]{:S(2)}, u32[]{:S(2)}) collective-permute-start(bf16[128,1024]{1,0:T(8,128)(2,1)S(1)} %add_convert_fusion.2.done), channel_id=1, source_target_pairs={{0,8},{4,12},{8,0},{12,4},{1,9},{5,13},{9,1},{13,5},{2,10},{6,14},... | collective-permute-start | bytes 786440 | tf_op jit(solution)/shard_map/ppermute | solution.py:33
  16.5 5.3 %shard_map.66 = (bf16[1024,1792]{1,0:T(8,128)(2,1)S(1)}, bf16[1024,1792]{1,0:T(8,128)(2,1)S(1)}, bf16[1024,1792]{1,0:T(8,128)(2,1)S(1)}, bf16[1024,1792]{1,0:T(8,128)(2,1)S(1)}, f32[8,128]{1,0:T(8,128)S(1)}) custom-call(bf16[2048,3584]{1,0:T(8,128)(2,1)} %w_hbm.6, bf16[128,1024]{1,0:T(8,128)(2,1)S(1)} %add_convert_fusion.2.done), custom_call_target="tpu_custom_call" | custom-call | bytes 1024 | tf_op jit(solution)/shard_map/pallas_call | solution.py:161
  23.0 3.6 %collective-permute-done.1.refs_0_ = bf16[128,1024]{1,0:T(8,128)(2,1)S(1)} collective-permute-done((bf16[128,1024]{1,0:T(8,128)(2,1)S(1)}, bf16[128,1024]{1,0:T(8,128)(2,1)S(1)}, u32[]{:S(2)}, u32[]{:S(2)}) %collective-permute-start.1) | collective-permute-done | bytes 262176 | tf_op jit(solution)/shard_map/ppermute | solution.py:33
  28.0 3.4 %collective-permute-start.7 = (bf16[128,1024]{1,0:T(8,128)(2,1)S(1)}, bf16[128,1024]{1,0:T(8,128)(2,1)S(1)}, u32[]{:S(2)}, u32[]{:S(2)}) collective-permute-start(bf16[128,1024]{1,0:T(8,128)(2,1)S(1)} %shard_map.69), channel_id=1, source_target_pairs={{0,8},{4,12},{8,0},{12,4},{1,9},{5,13},{9,1},{13,5},{2,10},{6,14},... | collective-permute-start | bytes 786440 | tf_op jit(solution)/shard_map/ppermute | solution.py:33
  31.5 5.4 %collective-permute-done.3 = bf16[128,1024]{1,0:T(8,128)(2,1)S(1)} collective-permute-done((bf16[128,1024]{1,0:T(8,128)(2,1)S(1)}, bf16[128,1024]{1,0:T(8,128)(2,1)S(1)}, u32[]{:S(2)}, u32[]{:S(2)}) %collective-permute-start.3) | collective-permute-done | bytes 262176 | tf_op jit(solution)/shard_map/ppermute | solution.py:33
  37.7 3.3 %collective-permute-done.7.refs_0_ = bf16[128,1024]{1,0:T(8,128)(2,1)S(1)} collective-permute-done((bf16[128,1024]{1,0:T(8,128)(2,1)S(1)}, bf16[128,1024]{1,0:T(8,128)(2,1)S(1)}, u32[]{:S(2)}, u32[]{:S(2)}) %collective-permute-start.7) | collective-permute-done | bytes 262176 | tf_op jit(solution)/shard_map/ppermute | solution.py:33
  43.3 1.6 %collective-permute-start.5 = (bf16[128,896]{1,0:T(8,128)(2,1)S(1)}, bf16[128,896]{1,0:T(8,128)(2,1)S(1)}, u32[]{:S(2)}, u32[]{:S(2)}) collective-permute-start(bf16[128,896]{1,0:T(8,128)(2,1)S(1)} %get-tuple-element.35), channel_id=1, source_target_pairs={{0,2},{2,0},{1,3},{3,1},{4,6},{6,4},{5,7},{7,5},{8,10},{10,8},{9,1... | collective-permute-start | bytes 688136 | tf_op jit(solution)/shard_map/ppermute | solution.py:33
  46.1 2.1 %collective-permute-done.8.refs_0_ = bf16[128,1024]{1,0:T(8,128)(2,1)S(1)} collective-permute-done((bf16[128,1024]{1,0:T(8,128)(2,1)S(1)}, bf16[128,1024]{1,0:T(8,128)(2,1)S(1)}, u32[]{:S(2)}, u32[]{:S(2)}) %collective-permute-start.8) | collective-permute-done | bytes 262176 | tf_op jit(solution)/shard_map/ppermute | solution.py:33
  48.2 2.3 %collective-permute-done.5.refs_1_ = bf16[128,896]{1,0:T(8,128)(2,1)S(1)} collective-permute-done((bf16[128,896]{1,0:T(8,128)(2,1)S(1)}, bf16[128,896]{1,0:T(8,128)(2,1)S(1)}, u32[]{:S(2)}, u32[]{:S(2)}) %collective-permute-start.5) | collective-permute-done | bytes 229408 | tf_op jit(solution)/shard_map/ppermute | solution.py:33
  51.1 2.5 %all-gather = bf16[256,1792]{1,0:T(8,128)(2,1)S(1)} all-gather(bf16[128,1792]{1,0:T(8,128)(2,1)S(1)} %fusion.3), channel_id=2, replica_groups=mesh['groups'=2,'blk'=4,'sub'=2,'pair'=2] {'pair'}, dimensions={0}, use_global_device_ids=true | all-gather | bytes 1376256 | tf_op jit(solution)/shard_map/all_gather | solution.py:293
  56.0 1.6 %collective-permute-start.13 = (bf16[128,1792]{1,0:T(8,128)(2,1)S(1)}, bf16[128,1792]{1,0:T(8,128)(2,1)S(1)}, u32[]{:S(2)}, u32[]{:S(2)}) collective-permute-start(bf16[128,1792]{1,0:T(8,128)(2,1)S(1)} %shard_map.76.own), channel_id=1, source_target_pairs={{0,2},{2,0},{1,3},{3,1},{4,6},{6,4},{5,7},{7,5},{8,10},{10,8},{9,1... | collective-permute-start | bytes 1376264 | tf_op jit(solution)/shard_map/ppermute | solution.py:33
  57.8 6.4 %shard_map.75.refs_1_ = bf16[128,2048]{1,0:T(8,128)(2,1)S(1)} custom-call(bf16[128,3584]{1,0:T(8,128)(2,1)S(1)} %pad_maximum_fusion.hidden, bf16[3584,2048]{1,0:T(8,128)(2,1)} %w_hbm.7), custom_call_target="tpu_custom_call" | custom-call | flops 1879048192 | bytes 14680064 | tf_op jit(solution)/shard_map/pallas_call | solution.py:215
  64.2 3.2 %collective-permute-start.10 = (bf16[32,2048]{1,0:T(8,128)(2,1)S(1)}, bf16[32,2048]{1,0:T(8,128)(2,1)S(1)}, u32[]{:S(2)}, u32[]{:S(2)}) collective-permute-start(bf16[32,2048]{1,0:T(8,128)(2,1)S(1)} %get-tuple-element.32), channel_id=1, source_target_pairs={{0,12},{4,8},{8,4},{12,0},{1,13},{5,9},{9,5},{13,1},{2,14},{6,10},... | collective-permute-start | bytes 393224 | tf_op jit(solution)/shard_map/ppermute | solution.py:33
  69.7 2.6 %all-gather.1 = bf16[256,1792]{1,0:T(8,128)(2,1)S(1)} all-gather(bf16[128,1792]{1,0:T(8,128)(2,1)S(1)} %shard_map.78), channel_id=3, replica_groups=mesh['groups'=2,'blk'=4,'sub'=2,'pair'=2] {'pair'}, dimensions={0}, use_global_device_ids=true | all-gather | bytes 1376256 | tf_op jit(solution)/shard_map/all_gather | solution.py:313
  72.5 2.1 %convolution_convert_fusion.mlp = bf16[128,2048]{1,0:T(8,128)(2,1)S(1)} fusion(bf16[3584,2048]{1,0:T(8,128)(2,1)S(1)} %bitcast.49, bf16[128,1792]{1,0:T(8,128)(2,1)S(1)} %get-tuple-element.24, bf16[128,1792]{1,0:T(8,128)(2,1)S(1)} %get-tuple-element.23), kind=kOutput, calls=%fused_computation.8 | convolution fusion | flops 1881145344 | bytes 16121856 | tf_op jit(solution)/shard_map/dot_general | solution.py:41
  74.7 1.8 %collective-permute-start.16 = (bf16[32,2048]{1,0:T(8,128)(2,1)S(1)}, bf16[32,2048]{1,0:T(8,128)(2,1)S(1)}, u32[]{:S(2)}, u32[]{:S(2)}) collective-permute-start(bf16[32,2048]{1,0:T(8,128)(2,1)S(1)} %get-tuple-element.27), channel_id=1, source_target_pairs={{0,4},{4,0},{8,12},{12,8},{1,5},{5,1},{9,13},{13,9},{2,6},{6,2},{1... | collective-permute-start | bytes 393224 | tf_op jit(solution)/shard_map/ppermute | solution.py:33
  76.5 2.0 %collective-permute-start.15 = (bf16[32,2048]{1,0:T(8,128)(2,1)S(1)}, bf16[32,2048]{1,0:T(8,128)(2,1)S(1)}, u32[]{:S(2)}, u32[]{:S(2)}) collective-permute-start(bf16[32,2048]{1,0:T(8,128)(2,1)S(1)} %get-tuple-element.28), channel_id=1, source_target_pairs={{0,8},{4,12},{8,0},{12,4},{1,9},{5,13},{9,1},{13,5},{2,10},{6,14},... | collective-permute-start | bytes 393224 | tf_op jit(solution)/shard_map/ppermute | solution.py:33
  80.8 4.5 %collective-permute-done.16.third = bf16[32,2048]{1,0:T(8,128)(2,1)S(1)} collective-permute-done((bf16[32,2048]{1,0:T(8,128)(2,1)S(1)}, bf16[32,2048]{1,0:T(8,128)(2,1)S(1)}, u32[]{:S(2)}, u32[]{:S(2)}) %collective-permute-start.16) | collective-permute-done | bytes 131104 | tf_op jit(solution)/shard_map/ppermute | solution.py:33
  85.3 4.0 %collective-permute-done.15.second = bf16[32,2048]{1,0:T(8,128)(2,1)S(1)} collective-permute-done((bf16[32,2048]{1,0:T(8,128)(2,1)S(1)}, bf16[32,2048]{1,0:T(8,128)(2,1)S(1)}, u32[]{:S(2)}, u32[]{:S(2)}) %collective-permute-start.15) | collective-permute-done | bytes 131104 | tf_op jit(solution)/shard_map/ppermute | solution.py:33
  89.3 1.4 %shard_map.79 = bf16[64,2048]{1,0:T(8,128)(2,1)} custom-call(f32[3]{0:T(128)S(1)} %copy-done, bf16[32,2048]{1,0:T(8,128)(2,1)S(1)} %add_convert_fusion.3.done, bf16[128,1024]{1,0:T(8,128)(2,1)S(1)} %add_convert_fusion.near, bf16[128,1024]{1,0:T(8,128)(2,1)S(1)} %shard_map.72.far, bf16[128,2048]{1,0:T(8,128)(2,1)S(1)} %convolution_convert_fusion.mlp, ...), custom_call_target="tpu_custom_call" | custom-call | tf_op jit(solution)/shard_map/pallas_call | solution.py:249
  (62 shorter events, 15.0 us)
Async XLA Ops:
  3.0 10.2 %collective-permute-start = (bf16[128,1024]{1,0:T(8,128)(2,1)S(1)}, bf16[128,1024]{1,0:T(8,128)(2,1)S(1)}, u32[]{:S(2)}, u32[]{:S(2)}) collective-permute-start(bf16[128,1024]{1,0:T(8,128)(2,1)S(1)} %bitcast.47), channel_id=1, source_target_pairs={{0,4},{4,0},{8,12},{12,8},{1,5},{5,1},{9,13},{13,9},{2,6},{6,2},{1... | collective-permute-start | bytes 786440 | tf_op jit(solution)/shard_map/ppermute | solution.py:33
  9.1 13.8 %collective-permute-start.2 = (bf16[128,1024]{1,0:T(8,128)(2,1)S(1)}, bf16[128,1024]{1,0:T(8,128)(2,1)S(1)}, u32[]{:S(2)}, u32[]{:S(2)}) collective-permute-start(bf16[128,1024]{1,0:T(8,128)(2,1)S(1)} %shard_map.67), channel_id=1, source_target_pairs={{0,4},{4,0},{8,12},{12,8},{1,5},{5,1},{9,13},{13,9},{2,6},{6,2},{1... | collective-permute-start | bytes 786440 | tf_op jit(solution)/shard_map/ppermute | solution.py:33
  13.3 13.3 %collective-permute-start.1 = (bf16[128,1024]{1,0:T(8,128)(2,1)S(1)}, bf16[128,1024]{1,0:T(8,128)(2,1)S(1)}, u32[]{:S(2)}, u32[]{:S(2)}) collective-permute-start(bf16[128,1024]{1,0:T(8,128)(2,1)S(1)} %add_convert_fusion.2.done), channel_id=1, source_target_pairs={{0,8},{4,12},{8,0},{12,4},{1,9},{5,13},{9,1},{13,5},{2,10},{6,14},... | collective-permute-start | bytes 786440 | tf_op jit(solution)/shard_map/ppermute | solution.py:33
  26.7 10.2 %collective-permute-start.3 = (bf16[128,1024]{1,0:T(8,128)(2,1)S(1)}, bf16[128,1024]{1,0:T(8,128)(2,1)S(1)}, u32[]{:S(2)}, u32[]{:S(2)}) collective-permute-start(bf16[128,1024]{1,0:T(8,128)(2,1)S(1)} %add_convert_fusion.1), channel_id=1, source_target_pairs={{0,4},{4,0},{8,12},{12,8},{1,5},{5,1},{9,13},{13,9},{2,6},{6,2},{1... | collective-permute-start | bytes 786440 | tf_op jit(solution)/shard_map/ppermute | solution.py:33
  28.0 13.0 %collective-permute-start.7 = (bf16[128,1024]{1,0:T(8,128)(2,1)S(1)}, bf16[128,1024]{1,0:T(8,128)(2,1)S(1)}, u32[]{:S(2)}, u32[]{:S(2)}) collective-permute-start(bf16[128,1024]{1,0:T(8,128)(2,1)S(1)} %shard_map.69), channel_id=1, source_target_pairs={{0,8},{4,12},{8,0},{12,4},{1,9},{5,13},{9,1},{13,5},{2,10},{6,14},... | collective-permute-start | bytes 786440 | tf_op jit(solution)/shard_map/ppermute | solution.py:33
  37.6 4.9 %collective-permute-start.4 = (bf16[128,1792]{1,0:T(8,128)(2,1)S(1)}, bf16[128,1792]{1,0:T(8,128)(2,1)S(1)}, u32[]{:S(2)}, u32[]{:S(2)}) collective-permute-start(bf16[128,1792]{1,0:T(8,128)(2,1)S(1)} %fusion.2.refs_1_), channel_id=1, source_target_pairs={{0,1},{1,0},{2,3},{3,2},{4,5},{5,4},{6,7},{7,6},{8,9},{9,8},{10,11... | collective-permute-start | bytes 1376264 | tf_op jit(solution)/shard_map/ppermute | solution.py:33
  41.7 6.4 %collective-permute-start.8 = (bf16[128,1024]{1,0:T(8,128)(2,1)S(1)}, bf16[128,1024]{1,0:T(8,128)(2,1)S(1)}, u32[]{:S(2)}, u32[]{:S(2)}) collective-permute-start(bf16[128,1024]{1,0:T(8,128)(2,1)S(1)} %add_convert_fusion.near), channel_id=1, source_target_pairs={{0,4},{4,0},{8,12},{12,8},{1,5},{5,1},{9,13},{13,9},{2,6},{6,2},{1... | collective-permute-start | bytes 786440 | tf_op jit(solution)/shard_map/ppermute | solution.py:33
  43.3 7.2 %collective-permute-start.5 = (bf16[128,896]{1,0:T(8,128)(2,1)S(1)}, bf16[128,896]{1,0:T(8,128)(2,1)S(1)}, u32[]{:S(2)}, u32[]{:S(2)}) collective-permute-start(bf16[128,896]{1,0:T(8,128)(2,1)S(1)} %get-tuple-element.35), channel_id=1, source_target_pairs={{0,2},{2,0},{1,3},{3,1},{4,6},{6,4},{5,7},{7,5},{8,10},{10,8},{9,1... | collective-permute-start | bytes 688136 | tf_op jit(solution)/shard_map/ppermute | solution.py:33
  45.5 8.8 %collective-permute-start.6 = (bf16[128,896]{1,0:T(8,128)(2,1)S(1)}, bf16[128,896]{1,0:T(8,128)(2,1)S(1)}, u32[]{:S(2)}, u32[]{:S(2)}) collective-permute-start(bf16[128,896]{1,0:T(8,128)(2,1)S(1)} %get-tuple-element.36), channel_id=1, source_target_pairs={{0,2},{2,0},{1,3},{3,1},{4,6},{6,4},{5,7},{7,5},{8,10},{10,8},{9,1... | collective-permute-start | bytes 688136 | tf_op jit(solution)/shard_map/ppermute | solution.py:33
  53.6 0.8 copy-start
  55.2 2.4 %collective-permute-start.9 = (bf16[128,1792]{1,0:T(8,128)(2,1)S(1)}, bf16[128,1792]{1,0:T(8,128)(2,1)S(1)}, u32[]{:S(2)}, u32[]{:S(2)}) collective-permute-start(bf16[128,1792]{1,0:T(8,128)(2,1)S(1)} %shard_map.74), channel_id=1, source_target_pairs={{0,1},{1,0},{2,3},{3,2},{4,5},{5,4},{6,7},{7,6},{8,9},{9,8},{10,11... | collective-permute-start | bytes 1376264 | tf_op jit(solution)/shard_map/ppermute | solution.py:33
  56.0 16.4 %slice-start = ((s8[14680064]{0:T(1024)(128)(4,1)}), s8[4194304]{0:T(1024)(128)(4,1)S(1)}, s32[]{:S(2)}) async-start(s8[14680064]{0:T(1024)(128)(4,1)} %bitcast.48), calls=%async_computation | async-start | bytes 8388608
  56.0 12.9 %collective-permute-start.13 = (bf16[128,1792]{1,0:T(8,128)(2,1)S(1)}, bf16[128,1792]{1,0:T(8,128)(2,1)S(1)}, u32[]{:S(2)}, u32[]{:S(2)}) collective-permute-start(bf16[128,1792]{1,0:T(8,128)(2,1)S(1)} %shard_map.76.own), channel_id=1, source_target_pairs={{0,2},{2,0},{1,3},{3,1},{4,6},{6,4},{5,7},{7,5},{8,10},{10,8},{9,1... | collective-permute-start | bytes 1376264 | tf_op jit(solution)/shard_map/ppermute | solution.py:33
  57.8 14.7 %slice-start.1 = ((s8[14680064]{0:T(1024)(128)(4,1)}), s8[4194304]{0:T(1024)(128)(4,1)S(1)}, s32[]{:S(2)}) async-start(s8[14680064]{0:T(1024)(128)(4,1)} %bitcast.48), calls=%async_computation.1 | async-start | bytes 8388608
  57.8 14.7 %slice-start.2 = ((s8[14680064]{0:T(1024)(128)(4,1)}), s8[4194304]{0:T(1024)(128)(4,1)S(1)}, s32[]{:S(2)}) async-start(s8[14680064]{0:T(1024)(128)(4,1)} %bitcast.48), calls=%async_computation.2 | async-start | bytes 8388608
  57.8 14.7 %slice-start.3 = ((s8[14680064]{0:T(1024)(128)(4,1)}), s8[2097152]{0:T(1024)(128)(4,1)S(1)}, s32[]{:S(2)}) async-start(s8[14680064]{0:T(1024)(128)(4,1)} %bitcast.48), calls=%async_computation.3 | async-start | bytes 4194304
  64.2 14.2 %collective-permute-start.10 = (bf16[32,2048]{1,0:T(8,128)(2,1)S(1)}, bf16[32,2048]{1,0:T(8,128)(2,1)S(1)}, u32[]{:S(2)}, u32[]{:S(2)}) collective-permute-start(bf16[32,2048]{1,0:T(8,128)(2,1)S(1)} %get-tuple-element.32), channel_id=1, source_target_pairs={{0,12},{4,8},{8,4},{12,0},{1,13},{5,9},{9,5},{13,1},{2,14},{6,10},... | collective-permute-start | bytes 393224 | tf_op jit(solution)/shard_map/ppermute | solution.py:33
  67.4 12.2 %collective-permute-start.12 = (bf16[32,2048]{1,0:T(8,128)(2,1)S(1)}, bf16[32,2048]{1,0:T(8,128)(2,1)S(1)}, u32[]{:S(2)}, u32[]{:S(2)}) collective-permute-start(bf16[32,2048]{1,0:T(8,128)(2,1)S(1)} %get-tuple-element.33), channel_id=1, source_target_pairs={{0,4},{4,0},{8,12},{12,8},{1,5},{5,1},{9,13},{13,9},{2,6},{6,2},{1... | collective-permute-start | bytes 393224 | tf_op jit(solution)/shard_map/ppermute | solution.py:33
  68.3 11.7 %collective-permute-start.11 = (bf16[32,2048]{1,0:T(8,128)(2,1)S(1)}, bf16[32,2048]{1,0:T(8,128)(2,1)S(1)}, u32[]{:S(2)}, u32[]{:S(2)}) collective-permute-start(bf16[32,2048]{1,0:T(8,128)(2,1)S(1)} %get-tuple-element.34), channel_id=1, source_target_pairs={{0,8},{4,12},{8,0},{12,4},{1,9},{5,13},{9,1},{13,5},{2,10},{6,14},... | collective-permute-start | bytes 393224 | tf_op jit(solution)/shard_map/ppermute | solution.py:33
  74.7 10.6 %collective-permute-start.16 = (bf16[32,2048]{1,0:T(8,128)(2,1)S(1)}, bf16[32,2048]{1,0:T(8,128)(2,1)S(1)}, u32[]{:S(2)}, u32[]{:S(2)}) collective-permute-start(bf16[32,2048]{1,0:T(8,128)(2,1)S(1)} %get-tuple-element.27), channel_id=1, source_target_pairs={{0,4},{4,0},{8,12},{12,8},{1,5},{5,1},{9,13},{13,9},{2,6},{6,2},{1... | collective-permute-start | bytes 393224 | tf_op jit(solution)/shard_map/ppermute | solution.py:33
  76.5 12.8 %collective-permute-start.15 = (bf16[32,2048]{1,0:T(8,128)(2,1)S(1)}, bf16[32,2048]{1,0:T(8,128)(2,1)S(1)}, u32[]{:S(2)}, u32[]{:S(2)}) collective-permute-start(bf16[32,2048]{1,0:T(8,128)(2,1)S(1)} %get-tuple-element.28), channel_id=1, source_target_pairs={{0,8},{4,12},{8,0},{12,4},{1,9},{5,13},{9,1},{13,5},{2,10},{6,14},... | collective-permute-start | bytes 393224 | tf_op jit(solution)/shard_map/ppermute | solution.py:33
  78.4 10.9 %collective-permute-start.14 = (bf16[32,2048]{1,0:T(8,128)(2,1)S(1)}, bf16[32,2048]{1,0:T(8,128)(2,1)S(1)}, u32[]{:S(2)}, u32[]{:S(2)}) collective-permute-start(bf16[32,2048]{1,0:T(8,128)(2,1)S(1)} %get-tuple-element.29), channel_id=1, source_target_pairs={{0,12},{4,8},{8,4},{12,0},{1,13},{5,9},{9,5},{13,1},{2,14},{6,10},... | collective-permute-start | bytes 393224 | tf_op jit(solution)/shard_map/ppermute | solution.py:33

commit v4 on v3

--- a/solution.py
+++ b/solution.py
@@ -71,8 +71,20 @@
     return [swap(lax.dynamic_index_in_dim(blocks, z ^ flip, 0, keepdims=False), "blk", n, flip) for flip in (3, 2, 1)]
 
 
+def sent_by_two(mlp, n):
+    z = lax.axis_index("blk")
+    blocks = mlp.reshape(n, mlp.shape[0] // n, -1)
+
+    def of(flip):
+        return lax.dynamic_index_in_dim(blocks, z ^ flip, 0, keepdims=False)
+
+    joint = swap(of(3), "blk", n, 1)
+    term = swap(of(1), "blk", n, 1)
+    return [term, swap(add(of(2), joint).astype(BF16), "blk", n, 2)]
+
+
 def out_kernel(pieces, near, scales_hbm, ctx_hbm, w_hbm, res_hbm, *rest):
-    parts, (ctx, w, res, acc, scales, sems) = rest[:-6], rest[-6:]
+    parts, gains, (ctx, w, res, acc, scales, sems) = rest[:-8], rest[-8:-6], rest[-6:]
     depth, width = w.shape
     block = depth // pieces
     tile = min(256, width)
@@ -113,17 +125,20 @@
             for part in parts:
                 part[:, :, at] = term[:, start:start + part.shape[1]]
                 start += part.shape[1]
+    for index, gain in enumerate(gains):
+        gain[...] = jnp.full_like(gain, scales[1 + index])
 
 
 def out_projection(context, w_out, resid, scales, near, sizes):
     depth, width = w_out.shape[0], w_out.shape[1] // 2
     pieces = 8
     n = context.shape[0] // resid.shape[0]
-    parts = pl.pallas_call(
+    gain = jax.ShapeDtypeStruct((8, 128), F32)
+    *parts, gain_in, gain_down = pl.pallas_call(
         functools.partial(out_kernel, pieces, near),
-        out_shape=[jax.ShapeDtypeStruct((n, size, width), BF16) for size in sizes],
+        out_shape=[jax.ShapeDtypeStruct((n, size, width), BF16) for size in sizes] + [gain, gain],
         in_specs=[ANY] * 4,
-        out_specs=[VMEM] * len(sizes),
+        out_specs=[VMEM] * (len(sizes) + 2),
         scratch_shapes=[
             pltpu.VMEM(context.shape, BF16),
             pltpu.VMEM((depth, width), BF16),
@@ -137,7 +152,7 @@
             flops=2 * context.shape[0] * depth * width, bytes_accessed=2 * depth * width, transcendentals=0
         ),
     )(in_hbm(scales), in_hbm(context), in_hbm(w_out), in_hbm(resid))
-    return [part.reshape(n * size, width) for part, size in zip(parts, sizes)]
+    return [part.reshape(n * size, width) for part, size in zip(parts, sizes)] + [gain_in, gain_down]
 
 
 def fetch_kernel(w_hbm, done, *rest):
@@ -169,22 +184,22 @@
     )(in_hbm(w), done)
 
 
-def gelu_kernel(scales, own, there, out):
+def gelu_kernel(gain, own, there, out):
     tile = 256
     for start in range(0, out.shape[1], tile):
         at = slice(start, min(start + tile, out.shape[1]))
-        v = scales[1] * add(own[:, at], there[:, at])
+        v = gain[:1, :1] * add(own[:, at], there[:, at])
         out[:, at] = (0.5 * v * (1.0 + lax.erf(v * math.sqrt(0.5)))).astype(BF16)
 
 
-def gelu(scales, own, there):
+def gelu(gain, own, there):
     return pl.pallas_call(
         gelu_kernel,
         out_shape=jax.ShapeDtypeStruct(own.shape, BF16),
-        in_specs=[SMEM, VMEM, VMEM],
+        in_specs=[VMEM] * 3,
         out_specs=VMEM,
         compiler_params=pltpu.CompilerParams(vmem_limit_bytes=3 << 20),
-    )(scales, own, there)
+    )(gain, own, there)
 
 
 def down_kernel(pieces, hidden, w_hbm, out, w, acc, sems):
@@ -227,7 +242,7 @@
     )(hidden, in_hbm(w))
 
 
-def end_kernel(scales, done, near, far, mlp, first, second, third, out):
+def end_kernel(gain, done, near, far, mlp, first, second, third, out):
     z = lax.axis_index("blk")
     odd = (z & 1) == 1
     size, width = first.shape[0], out.shape[1] // 2
@@ -241,18 +256,18 @@
             total = total + term[:, at].astype(F32)
         other, own = (far, near) if part == 0 else (near, far)
         mixed = jnp.where(odd, other[rows, :].astype(F32), own[rows, :].astype(F32))
-        out[head:, at] = (mixed + scales[2] * total).astype(BF16)
-
-
-def end(scales, done, near, far, mlp, terms):
+        out[head:, at] = (mixed + gain[:1, :1] * total).astype(BF16)
+
+
+def end(gain, done, near, far, mlp, terms):
     rows, width = done.shape[0] + terms[0].shape[0], done.shape[1]
     return pl.pallas_call(
         end_kernel,
         out_shape=jax.ShapeDtypeStruct((rows, width), BF16),
-        in_specs=[SMEM] + [VMEM] * 7,
+        in_specs=[VMEM] * 8,
         out_specs=VMEM,
         compiler_params=pltpu.CompilerParams(vmem_limit_bytes=3 << 20),
-    )(scales, done, near, far, mlp, *terms)
+    )(gain, done, near, far, mlp, *terms)
 
 
 def swapped(resid, context, w_out, w_in, w_down, scales):
@@ -262,8 +277,8 @@
     rows = resid.shape[0] // 2
     sizes = [rows, rows]
 
-    other_a, other_b = out_projection(context, w_out, resid, scales, False, sizes)
-    own_a, own_b = out_projection(context, w_out, resid, scales, True, sizes)
+    other_a, other_b, _, _ = out_projection(context, w_out, resid, scales, False, sizes)
+    own_a, own_b, gain_in, gain_down = out_projection(context, w_out, resid, scales, True, sizes)
     other_b = after(other_b, own_a)
     sum_a = add(own_a, swap(other_a, "blk", n, 1)).astype(BF16)
     sum_b = add(own_b, swap(other_b, "blk", n, 1)).astype(BF16)
@@ -276,10 +291,12 @@
     far_a = swap(near_a, "blk", n, 1)
     crossed = swap(sum_b, "blk", n, 2)
     other = (first + dot(far_a, far_far)).astype(BF16)
-    mine = dot(near_a, near_near) + dot(far_a, far_near)
+    mine = dot(near_a, near_near)
+    early = mine
+    mine = mine + dot(far_a, far_near)
     mine_a = add(mine, swap(other, "pair", 2, 1)).astype(BF16)
 
-    crossed = after(crossed, other)
+    crossed = after(crossed, other, early)
     near_b = add(sum_b, crossed).astype(BF16)
     width = mine_a.shape[1] // 2
     left_a = swap(mine_a[:, :width], "sub", 2, 1)
@@ -296,7 +313,7 @@
     mine_b = after(mine_b, right_a)
     moved_b = swap(mine_b, "sub", 2, 1)
 
-    hidden = gelu(scales, mine_a, jnp.concatenate([left_a, right_a], axis=1))
+    hidden = gelu(gain_in, mine_a, jnp.concatenate([left_a, right_a], axis=1))
     there = swap(hidden, "pair", 2, 1)
     first_core = core == 0
     hidden = jnp.concatenate([jnp.where(first_core, hidden, there), jnp.where(first_core, there, hidden)], axis=1)
@@ -307,12 +324,12 @@
     total = lax.dynamic_slice_in_dim(mlp_a, z * rows, rows, 0).astype(F32)
     for term in terms_a:
         total = total + term.astype(F32)
-    done = (kept.astype(F32) + scales[2] * total).astype(BF16)
-
-    hidden = gelu(scales, mine_b, after(moved_b, mlp_a))
+    done = (kept.astype(F32) + gain_down[:1, :1] * total).astype(BF16)
+
+    hidden = gelu(gain_in, mine_b, after(moved_b, mlp_a))
     hidden = lax.all_gather(hidden, "pair", axis=0)
     mlp_b = dot(jnp.concatenate([hidden[0], hidden[1]], axis=1), w_down).astype(BF16)
-    return end(scales, done, near_b, far_b, mlp_b, sent(mlp_b, n))
+    return end(gain_down, done, near_b, far_b, mlp_b, sent(mlp_b, n))
 
 
 def solution(mesh):

time: 90.8 us -> 89.1 us (0.981)
  Pallas kernels: 20.7 us -> 19.6 us
    pallas_call x2, Pallas kernels: 1.66 us -> 0.61 us  [gelu(): pl.pallas_call(gelu_kernel, out_shape=jax.ShapeDtypeStruct(own.shape, BF1...]
where the time goes in v4:
time: 89.1 us; the launch traced here: 88.9 us
  waiting for transfers between devices  31.1 us (35%)
  starting transfers between devices  23.4 us (26%)
  Pallas kernels  19.6 us (22%)
  matrix products  7.44 us (8%)
  blocking collectives  5.11 us (6%)
  other arithmetic  1.23 us (1%)
    ppermute x17, waiting for transfers between devices, swap(): return lax.ppermute(x, axis, [(i, i ^ flip) for i in range(size)])  31.1 us
    ppermute x17, starting transfers between devices, swap(): return lax.ppermute(x, axis, [(i, i ^ flip) for i in range(size)])  23.4 us
    dot_general x9, matrix products, dot(): return jnp.dot(x, w, preferred_element_type=F32)  7.44 us
    pallas_call x2, Pallas kernels, out_projection(): pl.pallas_call(functools.partial(out_kernel, pieces, near), out_shape=[ja...  6.52 us
    pallas_call x1, Pallas kernels, down_projection(): pl.pallas_call(functools.partial(down_kernel, pieces), out_shape=jax.Shap...  6.34 us
    pallas_call x1, Pallas kernels, fetch(): pl.pallas_call(fetch_kernel, out_shape=[part] * 4 + [jax.ShapeDtypeStruct...  5.28 us
    all_gather x1, blocking collectives, swapped(): hidden = lax.all_gather(hidden, 'pair', axis=0)  2.64 us
    all_gather x1, blocking collectives, swapped(): lax.all_gather(other, 'pair', axis=0)  2.46 us
  transfers between devices with their start and end apart: 17, of which 11 were waited for; matrix products, arithmetic and copies ran while one was open for 10% of the time, Pallas kernels for 17%

profile of v4, /device:TPU:0, one launch (start us, length us, event | category | flops | bytes accessed | tf_op | source)
XLA Modules:
  0.0 88.9 jit_solution(18114225940033693854)
XLA Ops:
  0.0 3.5 %shard_map.65 = (bf16[4,32,1024]{2,1,0:T(8,128)(2,1)S(1)}, bf16[4,32,1024]{2,1,0:T(8,128)(2,1)S(1)}, f32[8,128]{1,0:T(8,128)}, f32[8,128]{1,0:T(8,128)}) custom-call(f32[3]{0:T(128)} %scales_hbm.3, bf16[256,2048]{1,0:T(8,128)(2,1)} %ctx_hbm.3, bf16[2048,2048]{1,0:T(8,128)(2,1)} %w_hbm.5, bf16[64,2048]{1,0:T(8,128)(2,1)} %res_hbm.3), custom_call_target="tpu_custom_call" | custom-call | flops 1073741824 | bytes 4194304 | tf_op jit(solution)/shard_map/pallas_call | solution.py:137
  3.5 3.1 %collective-permute-start = (bf16[128,1024]{1,0:T(8,128)(2,1)S(1)}, bf16[128,1024]{1,0:T(8,128)(2,1)S(1)}, u32[]{:S(2)}, u32[]{:S(2)}) collective-permute-start(bf16[128,1024]{1,0:T(8,128)(2,1)S(1)} %bitcast.47), channel_id=1, source_target_pairs={{0,4},{4,0},{8,12},{12,8},{1,5},{5,1},{9,13},{13,9},{2,6},{6,2},{1... | collective-permute-start | bytes 786440 | tf_op jit(solution)/shard_map/ppermute | solution.py:33
  6.6 3.0 %shard_map.64 = (bf16[4,32,1024]{2,1,0:T(8,128)(2,1)S(1)}, bf16[4,32,1024]{2,1,0:T(8,128)(2,1)S(1)}, f32[8,128]{1,0:T(8,128)S(1)}, f32[8,128]{1,0:T(8,128)S(1)}) custom-call(f32[3]{0:T(128)} %scales_hbm.3, bf16[256,2048]{1,0:T(8,128)(2,1)} %ctx_hbm.3, bf16[2048,2048]{1,0:T(8,128)(2,1)} %w_hbm.5, bf16[64,2048]{1,0:T(8,128)(2,1)} %res_hbm.3), custom_call_target="tpu_custom_call" | custom-call | flops 1073741824 | bytes 4194304 | tf_op jit(solution)/shard_map/pallas_call | solution.py:137
  9.7 4.0 %collective-permute-done = bf16[128,1024]{1,0:T(8,128)(2,1)S(1)} collective-permute-done((bf16[128,1024]{1,0:T(8,128)(2,1)S(1)}, bf16[128,1024]{1,0:T(8,128)(2,1)S(1)}, u32[]{:S(2)}, u32[]{:S(2)}) %collective-permute-start) | collective-permute-done | bytes 262176 | tf_op jit(solution)/shard_map/ppermute | solution.py:33
  13.8 3.1 %collective-permute-start.1 = (bf16[128,1024]{1,0:T(8,128)(2,1)S(1)}, bf16[128,1024]{1,0:T(8,128)(2,1)S(1)}, u32[]{:S(2)}, u32[]{:S(2)}) collective-permute-start(bf16[128,1024]{1,0:T(8,128)(2,1)S(1)} %add_convert_fusion.2.done), channel_id=1, source_target_pairs={{0,8},{4,12},{8,0},{12,4},{1,9},{5,13},{9,1},{13,5},{2,10},{6,14},... | collective-permute-start | bytes 786440 | tf_op jit(solution)/shard_map/ppermute | solution.py:33
  17.0 5.3 %shard_map.66 = (bf16[1024,1792]{1,0:T(8,128)(2,1)S(1)}, bf16[1024,1792]{1,0:T(8,128)(2,1)S(1)}, bf16[1024,1792]{1,0:T(8,128)(2,1)S(1)}, bf16[1024,1792]{1,0:T(8,128)(2,1)S(1)}, f32[8,128]{1,0:T(8,128)S(1)}) custom-call(bf16[2048,3584]{1,0:T(8,128)(2,1)} %w_hbm.6, bf16[128,1024]{1,0:T(8,128)(2,1)S(1)} %add_convert_fusion.2.done), custom_call_target="tpu_custom_call" | custom-call | bytes 1024 | tf_op jit(solution)/shard_map/pallas_call | solution.py:176
  23.6 3.6 %collective-permute-done.1.refs_0_ = bf16[128,1024]{1,0:T(8,128)(2,1)S(1)} collective-permute-done((bf16[128,1024]{1,0:T(8,128)(2,1)S(1)}, bf16[128,1024]{1,0:T(8,128)(2,1)S(1)}, u32[]{:S(2)}, u32[]{:S(2)}) %collective-permute-start.1) | collective-permute-done | bytes 262176 | tf_op jit(solution)/shard_map/ppermute | solution.py:33
  28.6 3.4 %collective-permute-start.7 = (bf16[128,1024]{1,0:T(8,128)(2,1)S(1)}, bf16[128,1024]{1,0:T(8,128)(2,1)S(1)}, u32[]{:S(2)}, u32[]{:S(2)}) collective-permute-start(bf16[128,1024]{1,0:T(8,128)(2,1)S(1)} %shard_map.69), channel_id=1, source_target_pairs={{0,8},{4,12},{8,0},{12,4},{1,9},{5,13},{9,1},{13,5},{2,10},{6,14},... | collective-permute-start | bytes 786440 | tf_op jit(solution)/shard_map/ppermute | solution.py:33
  32.7 4.8 %collective-permute-done.3 = bf16[128,1024]{1,0:T(8,128)(2,1)S(1)} collective-permute-done((bf16[128,1024]{1,0:T(8,128)(2,1)S(1)}, bf16[128,1024]{1,0:T(8,128)(2,1)S(1)}, u32[]{:S(2)}, u32[]{:S(2)}) %collective-permute-start.3) | collective-permute-done | bytes 262176 | tf_op jit(solution)/shard_map/ppermute | solution.py:33
  38.2 3.3 %collective-permute-done.7.refs_0_ = bf16[128,1024]{1,0:T(8,128)(2,1)S(1)} collective-permute-done((bf16[128,1024]{1,0:T(8,128)(2,1)S(1)}, bf16[128,1024]{1,0:T(8,128)(2,1)S(1)}, u32[]{:S(2)}, u32[]{:S(2)}) %collective-permute-start.7) | collective-permute-done | bytes 262176 | tf_op jit(solution)/shard_map/ppermute | solution.py:33
  43.1 1.6 %collective-permute-start.5 = (bf16[128,896]{1,0:T(8,128)(2,1)S(1)}, bf16[128,896]{1,0:T(8,128)(2,1)S(1)}, u32[]{:S(2)}, u32[]{:S(2)}) collective-permute-start(bf16[128,896]{1,0:T(8,128)(2,1)S(1)} %get-tuple-element.39), channel_id=1, source_target_pairs={{0,2},{2,0},{1,3},{3,1},{4,6},{6,4},{5,7},{7,5},{8,10},{10,8},{9,1... | collective-permute-start | bytes 688136 | tf_op jit(solution)/shard_map/ppermute | solution.py:33
  45.9 2.1 %collective-permute-done.8.refs_0_ = bf16[128,1024]{1,0:T(8,128)(2,1)S(1)} collective-permute-done((bf16[128,1024]{1,0:T(8,128)(2,1)S(1)}, bf16[128,1024]{1,0:T(8,128)(2,1)S(1)}, u32[]{:S(2)}, u32[]{:S(2)}) %collective-permute-start.8) | collective-permute-done | bytes 262176 | tf_op jit(solution)/shard_map/ppermute | solution.py:33
  48.0 2.9 %collective-permute-done.5.refs_1_ = bf16[128,896]{1,0:T(8,128)(2,1)S(1)} collective-permute-done((bf16[128,896]{1,0:T(8,128)(2,1)S(1)}, bf16[128,896]{1,0:T(8,128)(2,1)S(1)}, u32[]{:S(2)}, u32[]{:S(2)}) %collective-permute-start.5) | collective-permute-done | bytes 229408 | tf_op jit(solution)/shard_map/ppermute | solution.py:33
  51.6 2.5 %all-gather = bf16[256,1792]{1,0:T(8,128)(2,1)S(1)} all-gather(bf16[128,1792]{1,0:T(8,128)(2,1)S(1)} %fusion.3), channel_id=2, replica_groups=mesh['groups'=2,'blk'=4,'sub'=2,'pair'=2] {'pair'}, dimensions={0}, use_global_device_ids=true | all-gather | bytes 1376256 | tf_op jit(solution)/shard_map/all_gather | solution.py:310
  55.9 1.6 %collective-permute-start.13 = (bf16[128,1792]{1,0:T(8,128)(2,1)S(1)}, bf16[128,1792]{1,0:T(8,128)(2,1)S(1)}, u32[]{:S(2)}, u32[]{:S(2)}) collective-permute-start(bf16[128,1792]{1,0:T(8,128)(2,1)S(1)} %shard_map.76.own), channel_id=1, source_target_pairs={{0,2},{2,0},{1,3},{3,1},{4,6},{6,4},{5,7},{7,5},{8,10},{10,8},{9,1... | collective-permute-start | bytes 1376264 | tf_op jit(solution)/shard_map/ppermute | solution.py:33
  57.6 6.3 %shard_map.75.refs_1_ = bf16[128,2048]{1,0:T(8,128)(2,1)S(1)} custom-call(bf16[128,3584]{1,0:T(8,128)(2,1)S(1)} %pad_maximum_fusion.hidden, bf16[3584,2048]{1,0:T(8,128)(2,1)} %w_hbm.7), custom_call_target="tpu_custom_call" | custom-call | flops 1879048192 | bytes 14680064 | tf_op jit(solution)/shard_map/pallas_call | solution.py:230
  64.0 2.6 %collective-permute-start.10 = (bf16[32,2048]{1,0:T(8,128)(2,1)S(1)}, bf16[32,2048]{1,0:T(8,128)(2,1)S(1)}, u32[]{:S(2)}, u32[]{:S(2)}) collective-permute-start(bf16[32,2048]{1,0:T(8,128)(2,1)S(1)} %get-tuple-element.36), channel_id=1, source_target_pairs={{0,12},{4,8},{8,4},{12,0},{1,13},{5,9},{9,5},{13,1},{2,14},{6,10},... | collective-permute-start | bytes 393224 | tf_op jit(solution)/shard_map/ppermute | solution.py:33
  69.1 2.6 %all-gather.1 = bf16[256,1792]{1,0:T(8,128)(2,1)S(1)} all-gather(bf16[128,1792]{1,0:T(8,128)(2,1)S(1)} %shard_map.78), channel_id=3, replica_groups=mesh['groups'=2,'blk'=4,'sub'=2,'pair'=2] {'pair'}, dimensions={0}, use_global_device_ids=true | all-gather | bytes 1376256 | tf_op jit(solution)/shard_map/all_gather | solution.py:330
  71.8 2.1 %convolution_convert_fusion.mlp = bf16[128,2048]{1,0:T(8,128)(2,1)S(1)} fusion(bf16[3584,2048]{1,0:T(8,128)(2,1)S(1)} %bitcast.49, bf16[128,1792]{1,0:T(8,128)(2,1)S(1)} %get-tuple-element.28, bf16[128,1792]{1,0:T(8,128)(2,1)S(1)} %get-tuple-element.27), kind=kOutput, calls=%fused_computation.8 | convolution fusion | flops 1881145344 | bytes 16121856 | tf_op jit(solution)/shard_map/dot_general | solution.py:41
  75.2 2.0 %collective-permute-start.15 = (bf16[32,2048]{1,0:T(8,128)(2,1)S(1)}, bf16[32,2048]{1,0:T(8,128)(2,1)S(1)}, u32[]{:S(2)}, u32[]{:S(2)}) collective-permute-start(bf16[32,2048]{1,0:T(8,128)(2,1)S(1)} %get-tuple-element.32), channel_id=1, source_target_pairs={{0,8},{4,12},{8,0},{12,4},{1,9},{5,13},{9,1},{13,5},{2,10},{6,14},... | collective-permute-start | bytes 393224 | tf_op jit(solution)/shard_map/ppermute | solution.py:33
  77.2 1.3 %collective-permute-start.14 = (bf16[32,2048]{1,0:T(8,128)(2,1)S(1)}, bf16[32,2048]{1,0:T(8,128)(2,1)S(1)}, u32[]{:S(2)}, u32[]{:S(2)}) collective-permute-start(bf16[32,2048]{1,0:T(8,128)(2,1)S(1)} %get-tuple-element.33), channel_id=1, source_target_pairs={{0,12},{4,8},{8,4},{12,0},{1,13},{5,9},{9,5},{13,1},{2,14},{6,10},... | collective-permute-start | bytes 393224 | tf_op jit(solution)/shard_map/ppermute | solution.py:33
  78.5 1.3 %collective-permute-done.11 = bf16[32,2048]{1,0:T(8,128)(2,1)S(1)} collective-permute-done((bf16[32,2048]{1,0:T(8,128)(2,1)S(1)}, bf16[32,2048]{1,0:T(8,128)(2,1)S(1)}, u32[]{:S(2)}, u32[]{:S(2)}) %collective-permute-start.11) | collective-permute-done | bytes 131104 | tf_op jit(solution)/shard_map/ppermute | solution.py:33
  80.5 3.8 %collective-permute-done.16.third = bf16[32,2048]{1,0:T(8,128)(2,1)S(1)} collective-permute-done((bf16[32,2048]{1,0:T(8,128)(2,1)S(1)}, bf16[32,2048]{1,0:T(8,128)(2,1)S(1)}, u32[]{:S(2)}, u32[]{:S(2)}) %collective-permute-start.16) | collective-permute-done | bytes 131104 | tf_op jit(solution)/shard_map/ppermute | solution.py:33
  84.3 3.8 %collective-permute-done.15.second = bf16[32,2048]{1,0:T(8,128)(2,1)S(1)} collective-permute-done((bf16[32,2048]{1,0:T(8,128)(2,1)S(1)}, bf16[32,2048]{1,0:T(8,128)(2,1)S(1)}, u32[]{:S(2)}, u32[]{:S(2)}) %collective-permute-start.15) | collective-permute-done | bytes 131104 | tf_op jit(solution)/shard_map/ppermute | solution.py:33
  (60 shorter events, 15.0 us)
Async XLA Ops:
  3.5 10.2 %collective-permute-start = (bf16[128,1024]{1,0:T(8,128)(2,1)S(1)}, bf16[128,1024]{1,0:T(8,128)(2,1)S(1)}, u32[]{:S(2)}, u32[]{:S(2)}) collective-permute-start(bf16[128,1024]{1,0:T(8,128)(2,1)S(1)} %bitcast.47), channel_id=1, source_target_pairs={{0,4},{4,0},{8,12},{12,8},{1,5},{5,1},{9,13},{13,9},{2,6},{6,2},{1... | collective-permute-start | bytes 786440 | tf_op jit(solution)/shard_map/ppermute | solution.py:33
  9.6 13.8 %collective-permute-start.2 = (bf16[128,1024]{1,0:T(8,128)(2,1)S(1)}, bf16[128,1024]{1,0:T(8,128)(2,1)S(1)}, u32[]{:S(2)}, u32[]{:S(2)}) collective-permute-start(bf16[128,1024]{1,0:T(8,128)(2,1)S(1)} %shard_map.67), channel_id=1, source_target_pairs={{0,4},{4,0},{8,12},{12,8},{1,5},{5,1},{9,13},{13,9},{2,6},{6,2},{1... | collective-permute-start | bytes 786440 | tf_op jit(solution)/shard_map/ppermute | solution.py:33
  13.8 13.3 %collective-permute-start.1 = (bf16[128,1024]{1,0:T(8,128)(2,1)S(1)}, bf16[128,1024]{1,0:T(8,128)(2,1)S(1)}, u32[]{:S(2)}, u32[]{:S(2)}) collective-permute-start(bf16[128,1024]{1,0:T(8,128)(2,1)S(1)} %add_convert_fusion.2.done), channel_id=1, source_target_pairs={{0,8},{4,12},{8,0},{12,4},{1,9},{5,13},{9,1},{13,5},{2,10},{6,14},... | collective-permute-start | bytes 786440 | tf_op jit(solution)/shard_map/ppermute | solution.py:33
  27.2 10.2 %collective-permute-start.3 = (bf16[128,1024]{1,0:T(8,128)(2,1)S(1)}, bf16[128,1024]{1,0:T(8,128)(2,1)S(1)}, u32[]{:S(2)}, u32[]{:S(2)}) collective-permute-start(bf16[128,1024]{1,0:T(8,128)(2,1)S(1)} %add_convert_fusion.1), channel_id=1, source_target_pairs={{0,4},{4,0},{8,12},{12,8},{1,5},{5,1},{9,13},{13,9},{2,6},{6,2},{1... | collective-permute-start | bytes 786440 | tf_op jit(solution)/shard_map/ppermute | solution.py:33
  28.6 13.0 %collective-permute-start.7 = (bf16[128,1024]{1,0:T(8,128)(2,1)S(1)}, bf16[128,1024]{1,0:T(8,128)(2,1)S(1)}, u32[]{:S(2)}, u32[]{:S(2)}) collective-permute-start(bf16[128,1024]{1,0:T(8,128)(2,1)S(1)} %shard_map.69), channel_id=1, source_target_pairs={{0,8},{4,12},{8,0},{12,4},{1,9},{5,13},{9,1},{13,5},{2,10},{6,14},... | collective-permute-start | bytes 786440 | tf_op jit(solution)/shard_map/ppermute | solution.py:33
  38.1 4.2 %collective-permute-start.4 = (bf16[128,1792]{1,0:T(8,128)(2,1)S(1)}, bf16[128,1792]{1,0:T(8,128)(2,1)S(1)}, u32[]{:S(2)}, u32[]{:S(2)}) collective-permute-start(bf16[128,1792]{1,0:T(8,128)(2,1)S(1)} %fusion.2.refs_1_), channel_id=1, source_target_pairs={{0,1},{1,0},{2,3},{3,2},{4,5},{5,4},{6,7},{7,6},{8,9},{9,8},{10,11... | collective-permute-start | bytes 1376264 | tf_op jit(solution)/shard_map/ppermute | solution.py:33
  41.6 6.4 %collective-permute-start.8 = (bf16[128,1024]{1,0:T(8,128)(2,1)S(1)}, bf16[128,1024]{1,0:T(8,128)(2,1)S(1)}, u32[]{:S(2)}, u32[]{:S(2)}) collective-permute-start(bf16[128,1024]{1,0:T(8,128)(2,1)S(1)} %add_convert_fusion.near), channel_id=1, source_target_pairs={{0,4},{4,0},{8,12},{12,8},{1,5},{5,1},{9,13},{13,9},{2,6},{6,2},{1... | collective-permute-start | bytes 786440 | tf_op jit(solution)/shard_map/ppermute | solution.py:33
  43.1 7.8 %collective-permute-start.5 = (bf16[128,896]{1,0:T(8,128)(2,1)S(1)}, bf16[128,896]{1,0:T(8,128)(2,1)S(1)}, u32[]{:S(2)}, u32[]{:S(2)}) collective-permute-start(bf16[128,896]{1,0:T(8,128)(2,1)S(1)} %get-tuple-element.39), channel_id=1, source_target_pairs={{0,2},{2,0},{1,3},{3,1},{4,6},{6,4},{5,7},{7,5},{8,10},{10,8},{9,1... | collective-permute-start | bytes 688136 | tf_op jit(solution)/shard_map/ppermute | solution.py:33
  45.3 9.4 %collective-permute-start.6 = (bf16[128,896]{1,0:T(8,128)(2,1)S(1)}, bf16[128,896]{1,0:T(8,128)(2,1)S(1)}, u32[]{:S(2)}, u32[]{:S(2)}) collective-permute-start(bf16[128,896]{1,0:T(8,128)(2,1)S(1)} %get-tuple-element.40), channel_id=1, source_target_pairs={{0,2},{2,0},{1,3},{3,1},{4,6},{6,4},{5,7},{7,5},{8,10},{10,8},{9,1... | collective-permute-start | bytes 688136 | tf_op jit(solution)/shard_map/ppermute | solution.py:33
  55.1 2.3 %collective-permute-start.9 = (bf16[128,1792]{1,0:T(8,128)(2,1)S(1)}, bf16[128,1792]{1,0:T(8,128)(2,1)S(1)}, u32[]{:S(2)}, u32[]{:S(2)}) collective-permute-start(bf16[128,1792]{1,0:T(8,128)(2,1)S(1)} %shard_map.74), channel_id=1, source_target_pairs={{0,1},{1,0},{2,3},{3,2},{4,5},{5,4},{6,7},{7,6},{8,9},{9,8},{10,11... | collective-permute-start | bytes 1376264 | tf_op jit(solution)/shard_map/ppermute | solution.py:33
  55.9 15.9 %slice-start = ((s8[14680064]{0:T(1024)(128)(4,1)}), s8[4194304]{0:T(1024)(128)(4,1)S(1)}, s32[]{:S(2)}) async-start(s8[14680064]{0:T(1024)(128)(4,1)} %bitcast.48), calls=%async_computation | async-start | bytes 8388608
  55.9 12.9 %collective-permute-start.13 = (bf16[128,1792]{1,0:T(8,128)(2,1)S(1)}, bf16[128,1792]{1,0:T(8,128)(2,1)S(1)}, u32[]{:S(2)}, u32[]{:S(2)}) collective-permute-start(bf16[128,1792]{1,0:T(8,128)(2,1)S(1)} %shard_map.76.own), channel_id=1, source_target_pairs={{0,2},{2,0},{1,3},{3,1},{4,6},{6,4},{5,7},{7,5},{8,10},{10,8},{9,1... | collective-permute-start | bytes 1376264 | tf_op jit(solution)/shard_map/ppermute | solution.py:33
  57.6 14.2 %slice-start.1 = ((s8[14680064]{0:T(1024)(128)(4,1)}), s8[4194304]{0:T(1024)(128)(4,1)S(1)}, s32[]{:S(2)}) async-start(s8[14680064]{0:T(1024)(128)(4,1)} %bitcast.48), calls=%async_computation.1 | async-start | bytes 8388608
  57.6 14.2 %slice-start.2 = ((s8[14680064]{0:T(1024)(128)(4,1)}), s8[4194304]{0:T(1024)(128)(4,1)S(1)}, s32[]{:S(2)}) async-start(s8[14680064]{0:T(1024)(128)(4,1)} %bitcast.48), calls=%async_computation.2 | async-start | bytes 8388608
  57.6 14.2 %slice-start.3 = ((s8[14680064]{0:T(1024)(128)(4,1)}), s8[2097152]{0:T(1024)(128)(4,1)S(1)}, s32[]{:S(2)}) async-start(s8[14680064]{0:T(1024)(128)(4,1)} %bitcast.48), calls=%async_computation.3 | async-start | bytes 4194304
  64.0 13.1 %collective-permute-start.10 = (bf16[32,2048]{1,0:T(8,128)(2,1)S(1)}, bf16[32,2048]{1,0:T(8,128)(2,1)S(1)}, u32[]{:S(2)}, u32[]{:S(2)}) collective-permute-start(bf16[32,2048]{1,0:T(8,128)(2,1)S(1)} %get-tuple-element.36), channel_id=1, source_target_pairs={{0,12},{4,8},{8,4},{12,0},{1,13},{5,9},{9,5},{13,1},{2,14},{6,10},... | collective-permute-start | bytes 393224 | tf_op jit(solution)/shard_map/ppermute | solution.py:33
  66.6 11.8 %collective-permute-start.12 = (bf16[32,2048]{1,0:T(8,128)(2,1)S(1)}, bf16[32,2048]{1,0:T(8,128)(2,1)S(1)}, u32[]{:S(2)}, u32[]{:S(2)}) collective-permute-start(bf16[32,2048]{1,0:T(8,128)(2,1)S(1)} %get-tuple-element.37), channel_id=1, source_target_pairs={{0,4},{4,0},{8,12},{12,8},{1,5},{5,1},{9,13},{13,9},{2,6},{6,2},{1... | collective-permute-start | bytes 393224 | tf_op jit(solution)/shard_map/ppermute | solution.py:33
  67.5 12.3 %collective-permute-start.11 = (bf16[32,2048]{1,0:T(8,128)(2,1)S(1)}, bf16[32,2048]{1,0:T(8,128)(2,1)S(1)}, u32[]{:S(2)}, u32[]{:S(2)}) collective-permute-start(bf16[32,2048]{1,0:T(8,128)(2,1)S(1)} %get-tuple-element.38), channel_id=1, source_target_pairs={{0,8},{4,12},{8,0},{12,4},{1,9},{5,13},{9,1},{13,5},{2,10},{6,14},... | collective-permute-start | bytes 393224 | tf_op jit(solution)/shard_map/ppermute | solution.py:33
  74.0 10.3 %collective-permute-start.16 = (bf16[32,2048]{1,0:T(8,128)(2,1)S(1)}, bf16[32,2048]{1,0:T(8,128)(2,1)S(1)}, u32[]{:S(2)}, u32[]{:S(2)}) collective-permute-start(bf16[32,2048]{1,0:T(8,128)(2,1)S(1)} %get-tuple-element.31), channel_id=1, source_target_pairs={{0,4},{4,0},{8,12},{12,8},{1,5},{5,1},{9,13},{13,9},{2,6},{6,2},{1... | collective-permute-start | bytes 393224 | tf_op jit(solution)/shard_map/ppermute | solution.py:33
  75.2 12.9 %collective-permute-start.15 = (bf16[32,2048]{1,0:T(8,128)(2,1)S(1)}, bf16[32,2048]{1,0:T(8,128)(2,1)S(1)}, u32[]{:S(2)}, u32[]{:S(2)}) collective-permute-start(bf16[32,2048]{1,0:T(8,128)(2,1)S(1)} %get-tuple-element.32), channel_id=1, source_target_pairs={{0,8},{4,12},{8,0},{12,4},{1,9},{5,13},{9,1},{13,5},{2,10},{6,14},... | collective-permute-start | bytes 393224 | tf_op jit(solution)/shard_map/ppermute | solution.py:33
  77.2 10.9 %collective-permute-start.14 = (bf16[32,2048]{1,0:T(8,128)(2,1)S(1)}, bf16[32,2048]{1,0:T(8,128)(2,1)S(1)}, u32[]{:S(2)}, u32[]{:S(2)}) collective-permute-start(bf16[32,2048]{1,0:T(8,128)(2,1)S(1)} %get-tuple-element.33), channel_id=1, source_target_pairs={{0,12},{4,8},{8,4},{12,0},{1,13},{5,9},{9,5},{13,1},{2,14},{6,10},... | collective-permute-start | bytes 393224 | tf_op jit(solution)/shard_map/ppermute | solution.py:33

commit v5 on v4

--- a/solution.py
+++ b/solution.py
@@ -131,12 +131,12 @@
 
 def out_projection(context, w_out, resid, scales, near, sizes):
     depth, width = w_out.shape[0], w_out.shape[1] // 2
-    pieces = 8
+    pieces = depth // 256
     n = context.shape[0] // resid.shape[0]
-    gain = jax.ShapeDtypeStruct((8, 128), F32)
+    gains = [jax.ShapeDtypeStruct((1, 128), F32), jax.ShapeDtypeStruct((1, 2 * width), F32)]
     *parts, gain_in, gain_down = pl.pallas_call(
         functools.partial(out_kernel, pieces, near),
-        out_shape=[jax.ShapeDtypeStruct((n, size, width), BF16) for size in sizes] + [gain, gain],
+        out_shape=[jax.ShapeDtypeStruct((n, size, width), BF16) for size in sizes] + gains,
         in_specs=[ANY] * 4,
         out_specs=[VMEM] * (len(sizes) + 2),
         scratch_shapes=[
@@ -226,7 +226,7 @@
 
 def down_projection(hidden, w):
     rows, width = hidden.shape[0], w.shape[1]
-    pieces = 7
+    pieces = w.shape[0] // 256
     return pl.pallas_call(
         functools.partial(down_kernel, pieces),
         out_shape=jax.ShapeDtypeStruct((rows, width), BF16),
@@ -298,7 +298,7 @@
 
     crossed = after(crossed, other, early)
     near_b = add(sum_b, crossed).astype(BF16)
-    width = mine_a.shape[1] // 2
+    width = mine_a.shape[1] // 128 * 3 // 8 * 128
     left_a = swap(mine_a[:, :width], "sub", 2, 1)
     right_a = swap(mine_a[:, width:], "sub", 2, 1)
     far_b = after(swap(near_b, "blk", n, 1), left_a)
@@ -324,7 +324,7 @@
     total = lax.dynamic_slice_in_dim(mlp_a, z * rows, rows, 0).astype(F32)
     for term in terms_a:
         total = total + term.astype(F32)
-    done = (kept.astype(F32) + gain_down[:1, :1] * total).astype(BF16)
+    done = (kept.astype(F32) + gain_down * total).astype(BF16)
 
     hidden = gelu(gain_in, mine_b, after(moved_b, mlp_a))
     hidden = lax.all_gather(hidden, "pair", axis=0)

time: 89.1 us -> 88.1 us (0.989)
  transfers between devices with their start and end apart: 17 -> 17, of which waited for: 11 -> 12; matrix products, arithmetic and copies ran while one was open for 10% -> 9% of each run, Pallas kernels for 17% -> 17%
where the time goes in v5:
time: 88.1 us; the launch traced here: 87.9 us
  waiting for transfers between devices  31.4 us (36%)
  starting transfers between devices  23.4 us (27%)
  Pallas kernels  19.5 us (22%)
  matrix products  7.42 us (8%)
  blocking collectives  5.11 us (6%)
    ppermute x17, waiting for transfers between devices, swap(): return lax.ppermute(x, axis, [(i, i ^ flip) for i in range(size)])  31.4 us
    ppermute x17, starting transfers between devices, swap(): return lax.ppermute(x, axis, [(i, i ^ flip) for i in range(size)])  23.4 us
    dot_general x9, matrix products, dot(): return jnp.dot(x, w, preferred_element_type=F32)  7.42 us
    pallas_call x2, Pallas kernels, out_projection(): pl.pallas_call(functools.partial(out_kernel, pieces, near), out_shape=[ja...  6.52 us
    pallas_call x1, Pallas kernels, down_projection(): pl.pallas_call(functools.partial(down_kernel, pieces), out_shape=jax.Shap...  6.15 us
    pallas_call x1, Pallas kernels, fetch(): pl.pallas_call(fetch_kernel, out_shape=[part] * 4 + [jax.ShapeDtypeStruct...  5.28 us
    all_gather x1, blocking collectives, swapped(): hidden = lax.all_gather(hidden, 'pair', axis=0)  2.64 us
    all_gather x1, blocking collectives, swapped(): lax.all_gather(other, 'pair', axis=0)  2.46 us
  transfers between devices with their start and end apart: 17, of which 12 were waited for; matrix products, arithmetic and copies ran while one was open for 9% of the time, Pallas kernels for 17%

profile of v5, /device:TPU:0, one launch (start us, length us, event | category | flops | bytes accessed | tf_op | source)
XLA Modules:
  0.0 87.9 jit_solution(10169231356965384139)
XLA Ops:
  0.0 3.5 %shard_map.65 = (bf16[4,32,1024]{2,1,0:T(8,128)(2,1)S(1)}, bf16[4,32,1024]{2,1,0:T(8,128)(2,1)S(1)}, f32[1,128]{1,0:T(1,128)}, f32[1,2048]{1,0:T(1,128)}) custom-call(f32[3]{0:T(128)} %scales_hbm.3, bf16[256,2048]{1,0:T(8,128)(2,1)} %ctx_hbm.3, bf16[2048,2048]{1,0:T(8,128)(2,1)} %w_hbm.5, bf16[64,2048]{1,0:T(8,128)(2,1)} %res_hbm.3), custom_call_target="tpu_custom_call" | custom-call | flops 1073741824 | bytes 4194304 | tf_op jit(solution)/shard_map/pallas_call | solution.py:137
  3.5 3.1 %collective-permute-start = (bf16[128,1024]{1,0:T(8,128)(2,1)S(1)}, bf16[128,1024]{1,0:T(8,128)(2,1)S(1)}, u32[]{:S(2)}, u32[]{:S(2)}) collective-permute-start(bf16[128,1024]{1,0:T(8,128)(2,1)S(1)} %bitcast.48), channel_id=1, source_target_pairs={{0,4},{4,0},{8,12},{12,8},{1,5},{5,1},{9,13},{13,9},{2,6},{6,2},{1... | collective-permute-start | bytes 786440 | tf_op jit(solution)/shard_map/ppermute | solution.py:33
  6.6 3.0 %shard_map.64 = (bf16[4,32,1024]{2,1,0:T(8,128)(2,1)S(1)}, bf16[4,32,1024]{2,1,0:T(8,128)(2,1)S(1)}, f32[1,128]{1,0:T(1,128)S(1)}, f32[1,2048]{1,0:T(1,128)S(1)}) custom-call(f32[3]{0:T(128)} %scales_hbm.3, bf16[256,2048]{1,0:T(8,128)(2,1)} %ctx_hbm.3, bf16[2048,2048]{1,0:T(8,128)(2,1)} %w_hbm.5, bf16[64,2048]{1,0:T(8,128)(2,1)} %res_hbm.3), custom_call_target="tpu_custom_call" | custom-call | flops 1073741824 | bytes 4194304 | tf_op jit(solution)/shard_map/pallas_call | solution.py:137
  9.7 4.0 %collective-permute-done = bf16[128,1024]{1,0:T(8,128)(2,1)S(1)} collective-permute-done((bf16[128,1024]{1,0:T(8,128)(2,1)S(1)}, bf16[128,1024]{1,0:T(8,128)(2,1)S(1)}, u32[]{:S(2)}, u32[]{:S(2)}) %collective-permute-start) | collective-permute-done | bytes 262176 | tf_op jit(solution)/shard_map/ppermute | solution.py:33
  13.8 3.1 %collective-permute-start.1 = (bf16[128,1024]{1,0:T(8,128)(2,1)S(1)}, bf16[128,1024]{1,0:T(8,128)(2,1)S(1)}, u32[]{:S(2)}, u32[]{:S(2)}) collective-permute-start(bf16[128,1024]{1,0:T(8,128)(2,1)S(1)} %add_convert_fusion.2.done), channel_id=1, source_target_pairs={{0,8},{4,12},{8,0},{12,4},{1,9},{5,13},{9,1},{13,5},{2,10},{6,14},... | collective-permute-start | bytes 786440 | tf_op jit(solution)/shard_map/ppermute | solution.py:33
  17.0 5.3 %shard_map.66 = (bf16[1024,1792]{1,0:T(8,128)(2,1)S(1)}, bf16[1024,1792]{1,0:T(8,128)(2,1)S(1)}, bf16[1024,1792]{1,0:T(8,128)(2,1)S(1)}, bf16[1024,1792]{1,0:T(8,128)(2,1)S(1)}, f32[8,128]{1,0:T(8,128)S(1)}) custom-call(bf16[2048,3584]{1,0:T(8,128)(2,1)} %w_hbm.6, bf16[128,1024]{1,0:T(8,128)(2,1)S(1)} %add_convert_fusion.2.done), custom_call_target="tpu_custom_call" | custom-call | bytes 1024 | tf_op jit(solution)/shard_map/pallas_call | solution.py:176
  23.6 3.6 %collective-permute-done.1.refs_0_ = bf16[128,1024]{1,0:T(8,128)(2,1)S(1)} collective-permute-done((bf16[128,1024]{1,0:T(8,128)(2,1)S(1)}, bf16[128,1024]{1,0:T(8,128)(2,1)S(1)}, u32[]{:S(2)}, u32[]{:S(2)}) %collective-permute-start.1) | collective-permute-done | bytes 262176 | tf_op jit(solution)/shard_map/ppermute | solution.py:33
  28.6 3.4 %collective-permute-start.7 = (bf16[128,1024]{1,0:T(8,128)(2,1)S(1)}, bf16[128,1024]{1,0:T(8,128)(2,1)S(1)}, u32[]{:S(2)}, u32[]{:S(2)}) collective-permute-start(bf16[128,1024]{1,0:T(8,128)(2,1)S(1)} %shard_map.69), channel_id=1, source_target_pairs={{0,8},{4,12},{8,0},{12,4},{1,9},{5,13},{9,1},{13,5},{2,10},{6,14},... | collective-permute-start | bytes 786440 | tf_op jit(solution)/shard_map/ppermute | solution.py:33
  32.7 4.8 %collective-permute-done.3 = bf16[128,1024]{1,0:T(8,128)(2,1)S(1)} collective-permute-done((bf16[128,1024]{1,0:T(8,128)(2,1)S(1)}, bf16[128,1024]{1,0:T(8,128)(2,1)S(1)}, u32[]{:S(2)}, u32[]{:S(2)}) %collective-permute-start.3) | collective-permute-done | bytes 262176 | tf_op jit(solution)/shard_map/ppermute | solution.py:33
  38.2 3.3 %collective-permute-done.7.refs_0_ = bf16[128,1024]{1,0:T(8,128)(2,1)S(1)} collective-permute-done((bf16[128,1024]{1,0:T(8,128)(2,1)S(1)}, bf16[128,1024]{1,0:T(8,128)(2,1)S(1)}, u32[]{:S(2)}, u32[]{:S(2)}) %collective-permute-start.7) | collective-permute-done | bytes 262176 | tf_op jit(solution)/shard_map/ppermute | solution.py:33
  43.1 1.6 %collective-permute-start.5 = (bf16[128,640]{1,0:T(8,128)(2,1)S(1)}, bf16[128,640]{1,0:T(8,128)(2,1)S(1)}, u32[]{:S(2)}, u32[]{:S(2)}) collective-permute-start(bf16[128,640]{1,0:T(8,128)(2,1)S(1)} %slice.18), channel_id=1, source_target_pairs={{0,2},{2,0},{1,3},{3,1},{4,6},{6,4},{5,7},{7,5},{8,10},{10,8},{9,1... | collective-permute-start | bytes 491528 | tf_op jit(solution)/shard_map/ppermute | solution.py:33
  45.9 2.1 %collective-permute-done.8.refs_0_ = bf16[128,1024]{1,0:T(8,128)(2,1)S(1)} collective-permute-done((bf16[128,1024]{1,0:T(8,128)(2,1)S(1)}, bf16[128,1024]{1,0:T(8,128)(2,1)S(1)}, u32[]{:S(2)}, u32[]{:S(2)}) %collective-permute-start.8) | collective-permute-done | bytes 262176 | tf_op jit(solution)/shard_map/ppermute | solution.py:33
  48.0 2.2 %collective-permute-done.5.refs_1_ = bf16[128,640]{1,0:T(8,128)(2,1)S(1)} collective-permute-done((bf16[128,640]{1,0:T(8,128)(2,1)S(1)}, bf16[128,640]{1,0:T(8,128)(2,1)S(1)}, u32[]{:S(2)}, u32[]{:S(2)}) %collective-permute-start.5) | collective-permute-done | bytes 163872 | tf_op jit(solution)/shard_map/ppermute | solution.py:33
  50.9 2.5 %all-gather = bf16[256,1792]{1,0:T(8,128)(2,1)S(1)} all-gather(bf16[128,1792]{1,0:T(8,128)(2,1)S(1)} %fusion.3), channel_id=2, replica_groups=mesh['groups'=2,'blk'=4,'sub'=2,'pair'=2] {'pair'}, dimensions={0}, use_global_device_ids=true | all-gather | bytes 1376256 | tf_op jit(solution)/shard_map/all_gather | solution.py:310
  54.7 1.5 %collective-permute-start.13 = (bf16[128,1792]{1,0:T(8,128)(2,1)S(1)}, bf16[128,1792]{1,0:T(8,128)(2,1)S(1)}, u32[]{:S(2)}, u32[]{:S(2)}) collective-permute-start(bf16[128,1792]{1,0:T(8,128)(2,1)S(1)} %shard_map.76.own), channel_id=1, source_target_pairs={{0,2},{2,0},{1,3},{3,1},{4,6},{6,4},{5,7},{7,5},{8,10},{10,8},{9,1... | collective-permute-start | bytes 1376264 | tf_op jit(solution)/shard_map/ppermute | solution.py:33
  56.5 6.1 %shard_map.75.refs_1_ = bf16[128,2048]{1,0:T(8,128)(2,1)S(1)} custom-call(bf16[128,3584]{1,0:T(8,128)(2,1)S(1)} %pad_maximum_fusion.hidden, bf16[3584,2048]{1,0:T(8,128)(2,1)} %w_hbm.7), custom_call_target="tpu_custom_call" | custom-call | flops 1879048192 | bytes 14680064 | tf_op jit(solution)/shard_map/pallas_call | solution.py:230
  62.7 2.5 %collective-permute-start.10 = (bf16[32,2048]{1,0:T(8,128)(2,1)S(1)}, bf16[32,2048]{1,0:T(8,128)(2,1)S(1)}, u32[]{:S(2)}, u32[]{:S(2)}) collective-permute-start(bf16[32,2048]{1,0:T(8,128)(2,1)S(1)} %get-tuple-element.36), channel_id=1, source_target_pairs={{0,12},{4,8},{8,4},{12,0},{1,13},{5,9},{9,5},{13,1},{2,14},{6,10},... | collective-permute-start | bytes 393224 | tf_op jit(solution)/shard_map/ppermute | solution.py:33
  67.9 2.6 %all-gather.1 = bf16[256,1792]{1,0:T(8,128)(2,1)S(1)} all-gather(bf16[128,1792]{1,0:T(8,128)(2,1)S(1)} %shard_map.78), channel_id=3, replica_groups=mesh['groups'=2,'blk'=4,'sub'=2,'pair'=2] {'pair'}, dimensions={0}, use_global_device_ids=true | all-gather | bytes 1376256 | tf_op jit(solution)/shard_map/all_gather | solution.py:330
  70.7 2.1 %convolution_convert_fusion.mlp = bf16[128,2048]{1,0:T(8,128)(2,1)S(1)} fusion(bf16[3584,2048]{1,0:T(8,128)(2,1)S(1)} %bitcast.50, bf16[128,1792]{1,0:T(8,128)(2,1)S(1)} %get-tuple-element.28, bf16[128,1792]{1,0:T(8,128)(2,1)S(1)} %get-tuple-element.27), kind=kOutput, calls=%fused_computation.8 | convolution fusion | flops 1881145344 | bytes 16121856 | tf_op jit(solution)/shard_map/dot_general | solution.py:41
  72.8 1.3 %collective-permute-start.16 = (bf16[32,2048]{1,0:T(8,128)(2,1)S(1)}, bf16[32,2048]{1,0:T(8,128)(2,1)S(1)}, u32[]{:S(2)}, u32[]{:S(2)}) collective-permute-start(bf16[32,2048]{1,0:T(8,128)(2,1)S(1)} %get-tuple-element.31), channel_id=1, source_target_pairs={{0,4},{4,0},{8,12},{12,8},{1,5},{5,1},{9,13},{13,9},{2,6},{6,2},{1... | collective-permute-start | bytes 393224 | tf_op jit(solution)/shard_map/ppermute | solution.py:33
  74.2 1.8 %collective-permute-start.15 = (bf16[32,2048]{1,0:T(8,128)(2,1)S(1)}, bf16[32,2048]{1,0:T(8,128)(2,1)S(1)}, u32[]{:S(2)}, u32[]{:S(2)}) collective-permute-start(bf16[32,2048]{1,0:T(8,128)(2,1)S(1)} %get-tuple-element.32), channel_id=1, source_target_pairs={{0,8},{4,12},{8,0},{12,4},{1,9},{5,13},{9,1},{13,5},{2,10},{6,14},... | collective-permute-start | bytes 393224 | tf_op jit(solution)/shard_map/ppermute | solution.py:33
  76.0 1.4 %collective-permute-start.14 = (bf16[32,2048]{1,0:T(8,128)(2,1)S(1)}, bf16[32,2048]{1,0:T(8,128)(2,1)S(1)}, u32[]{:S(2)}, u32[]{:S(2)}) collective-permute-start(bf16[32,2048]{1,0:T(8,128)(2,1)S(1)} %get-tuple-element.33), channel_id=1, source_target_pairs={{0,12},{4,8},{8,4},{12,0},{1,13},{5,9},{9,5},{13,1},{2,14},{6,10},... | collective-permute-start | bytes 393224 | tf_op jit(solution)/shard_map/ppermute | solution.py:33
  78.6 4.6 %collective-permute-done.16.third = bf16[32,2048]{1,0:T(8,128)(2,1)S(1)} collective-permute-done((bf16[32,2048]{1,0:T(8,128)(2,1)S(1)}, bf16[32,2048]{1,0:T(8,128)(2,1)S(1)}, u32[]{:S(2)}, u32[]{:S(2)}) %collective-permute-start.16) | collective-permute-done | bytes 131104 | tf_op jit(solution)/shard_map/ppermute | solution.py:33
  83.2 3.9 %collective-permute-done.15.second = bf16[32,2048]{1,0:T(8,128)(2,1)S(1)} collective-permute-done((bf16[32,2048]{1,0:T(8,128)(2,1)S(1)}, bf16[32,2048]{1,0:T(8,128)(2,1)S(1)}, u32[]{:S(2)}, u32[]{:S(2)}) %collective-permute-start.15) | collective-permute-done | bytes 131104 | tf_op jit(solution)/shard_map/ppermute | solution.py:33
  (60 shorter events, 14.1 us)
Async XLA Ops:
  3.5 10.2 %collective-permute-start = (bf16[128,1024]{1,0:T(8,128)(2,1)S(1)}, bf16[128,1024]{1,0:T(8,128)(2,1)S(1)}, u32[]{:S(2)}, u32[]{:S(2)}) collective-permute-start(bf16[128,1024]{1,0:T(8,128)(2,1)S(1)} %bitcast.48), channel_id=1, source_target_pairs={{0,4},{4,0},{8,12},{12,8},{1,5},{5,1},{9,13},{13,9},{2,6},{6,2},{1... | collective-permute-start | bytes 786440 | tf_op jit(solution)/shard_map/ppermute | solution.py:33
  9.6 13.8 %collective-permute-start.2 = (bf16[128,1024]{1,0:T(8,128)(2,1)S(1)}, bf16[128,1024]{1,0:T(8,128)(2,1)S(1)}, u32[]{:S(2)}, u32[]{:S(2)}) collective-permute-start(bf16[128,1024]{1,0:T(8,128)(2,1)S(1)} %shard_map.67), channel_id=1, source_target_pairs={{0,4},{4,0},{8,12},{12,8},{1,5},{5,1},{9,13},{13,9},{2,6},{6,2},{1... | collective-permute-start | bytes 786440 | tf_op jit(solution)/shard_map/ppermute | solution.py:33
  13.8 13.3 %collective-permute-start.1 = (bf16[128,1024]{1,0:T(8,128)(2,1)S(1)}, bf16[128,1024]{1,0:T(8,128)(2,1)S(1)}, u32[]{:S(2)}, u32[]{:S(2)}) collective-permute-start(bf16[128,1024]{1,0:T(8,128)(2,1)S(1)} %add_convert_fusion.2.done), channel_id=1, source_target_pairs={{0,8},{4,12},{8,0},{12,4},{1,9},{5,13},{9,1},{13,5},{2,10},{6,14},... | collective-permute-start | bytes 786440 | tf_op jit(solution)/shard_map/ppermute | solution.py:33
  27.2 10.2 %collective-permute-start.3 = (bf16[128,1024]{1,0:T(8,128)(2,1)S(1)}, bf16[128,1024]{1,0:T(8,128)(2,1)S(1)}, u32[]{:S(2)}, u32[]{:S(2)}) collective-permute-start(bf16[128,1024]{1,0:T(8,128)(2,1)S(1)} %add_convert_fusion.1), channel_id=1, source_target_pairs={{0,4},{4,0},{8,12},{12,8},{1,5},{5,1},{9,13},{13,9},{2,6},{6,2},{1... | collective-permute-start | bytes 786440 | tf_op jit(solution)/shard_map/ppermute | solution.py:33
  28.6 13.0 %collective-permute-start.7 = (bf16[128,1024]{1,0:T(8,128)(2,1)S(1)}, bf16[128,1024]{1,0:T(8,128)(2,1)S(1)}, u32[]{:S(2)}, u32[]{:S(2)}) collective-permute-start(bf16[128,1024]{1,0:T(8,128)(2,1)S(1)} %shard_map.69), channel_id=1, source_target_pairs={{0,8},{4,12},{8,0},{12,4},{1,9},{5,13},{9,1},{13,5},{2,10},{6,14},... | collective-permute-start | bytes 786440 | tf_op jit(solution)/shard_map/ppermute | solution.py:33
  38.1 4.2 %collective-permute-start.4 = (bf16[128,1792]{1,0:T(8,128)(2,1)S(1)}, bf16[128,1792]{1,0:T(8,128)(2,1)S(1)}, u32[]{:S(2)}, u32[]{:S(2)}) collective-permute-start(bf16[128,1792]{1,0:T(8,128)(2,1)S(1)} %fusion.2.refs_1_), channel_id=1, source_target_pairs={{0,1},{1,0},{2,3},{3,2},{4,5},{5,4},{6,7},{7,6},{8,9},{9,8},{10,11... | collective-permute-start | bytes 1376264 | tf_op jit(solution)/shard_map/ppermute | solution.py:33
  41.6 6.4 %collective-permute-start.8 = (bf16[128,1024]{1,0:T(8,128)(2,1)S(1)}, bf16[128,1024]{1,0:T(8,128)(2,1)S(1)}, u32[]{:S(2)}, u32[]{:S(2)}) collective-permute-start(bf16[128,1024]{1,0:T(8,128)(2,1)S(1)} %add_convert_fusion.near), channel_id=1, source_target_pairs={{0,4},{4,0},{8,12},{12,8},{1,5},{5,1},{9,13},{13,9},{2,6},{6,2},{1... | collective-permute-start | bytes 786440 | tf_op jit(solution)/shard_map/ppermute | solution.py:33
  43.1 7.2 %collective-permute-start.5 = (bf16[128,640]{1,0:T(8,128)(2,1)S(1)}, bf16[128,640]{1,0:T(8,128)(2,1)S(1)}, u32[]{:S(2)}, u32[]{:S(2)}) collective-permute-start(bf16[128,640]{1,0:T(8,128)(2,1)S(1)} %slice.18), channel_id=1, source_target_pairs={{0,2},{2,0},{1,3},{3,1},{4,6},{6,4},{5,7},{7,5},{8,10},{10,8},{9,1... | collective-permute-start | bytes 491528 | tf_op jit(solution)/shard_map/ppermute | solution.py:33
  45.3 8.7 %collective-permute-start.6 = (bf16[128,1152]{1,0:T(8,128)(2,1)S(1)}, bf16[128,1152]{1,0:T(8,128)(2,1)S(1)}, u32[]{:S(2)}, u32[]{:S(2)}) collective-permute-start(bf16[128,1152]{1,0:T(8,128)(2,1)S(1)} %slice.19), channel_id=1, source_target_pairs={{0,2},{2,0},{1,3},{3,1},{4,6},{6,4},{5,7},{7,5},{8,10},{10,8},{9,1... | collective-permute-start | bytes 884744 | tf_op jit(solution)/shard_map/ppermute | solution.py:33
  54.5 1.9 %collective-permute-start.9 = (bf16[128,1792]{1,0:T(8,128)(2,1)S(1)}, bf16[128,1792]{1,0:T(8,128)(2,1)S(1)}, u32[]{:S(2)}, u32[]{:S(2)}) collective-permute-start(bf16[128,1792]{1,0:T(8,128)(2,1)S(1)} %shard_map.74), channel_id=1, source_target_pairs={{0,1},{1,0},{2,3},{3,2},{4,5},{5,4},{6,7},{7,6},{8,9},{9,8},{10,11... | collective-permute-start | bytes 1376264 | tf_op jit(solution)/shard_map/ppermute | solution.py:33
  54.7 15.9 %slice-start = ((s8[14680064]{0:T(1024)(128)(4,1)}), s8[4194304]{0:T(1024)(128)(4,1)S(1)}, s32[]{:S(2)}) async-start(s8[14680064]{0:T(1024)(128)(4,1)} %bitcast.49), calls=%async_computation | async-start | bytes 8388608
  54.7 12.9 %collective-permute-start.13 = (bf16[128,1792]{1,0:T(8,128)(2,1)S(1)}, bf16[128,1792]{1,0:T(8,128)(2,1)S(1)}, u32[]{:S(2)}, u32[]{:S(2)}) collective-permute-start(bf16[128,1792]{1,0:T(8,128)(2,1)S(1)} %shard_map.76.own), channel_id=1, source_target_pairs={{0,2},{2,0},{1,3},{3,1},{4,6},{6,4},{5,7},{7,5},{8,10},{10,8},{9,1... | collective-permute-start | bytes 1376264 | tf_op jit(solution)/shard_map/ppermute | solution.py:33
  56.5 14.1 %slice-start.1 = ((s8[14680064]{0:T(1024)(128)(4,1)}), s8[4194304]{0:T(1024)(128)(4,1)S(1)}, s32[]{:S(2)}) async-start(s8[14680064]{0:T(1024)(128)(4,1)} %bitcast.49), calls=%async_computation.1 | async-start | bytes 8388608
  56.5 14.1 %slice-start.2 = ((s8[14680064]{0:T(1024)(128)(4,1)}), s8[4194304]{0:T(1024)(128)(4,1)S(1)}, s32[]{:S(2)}) async-start(s8[14680064]{0:T(1024)(128)(4,1)} %bitcast.49), calls=%async_computation.2 | async-start | bytes 8388608
  56.5 14.1 %slice-start.3 = ((s8[14680064]{0:T(1024)(128)(4,1)}), s8[2097152]{0:T(1024)(128)(4,1)S(1)}, s32[]{:S(2)}) async-start(s8[14680064]{0:T(1024)(128)(4,1)} %bitcast.49), calls=%async_computation.3 | async-start | bytes 4194304
  62.7 13.2 %collective-permute-start.10 = (bf16[32,2048]{1,0:T(8,128)(2,1)S(1)}, bf16[32,2048]{1,0:T(8,128)(2,1)S(1)}, u32[]{:S(2)}, u32[]{:S(2)}) collective-permute-start(bf16[32,2048]{1,0:T(8,128)(2,1)S(1)} %get-tuple-element.36), channel_id=1, source_target_pairs={{0,12},{4,8},{8,4},{12,0},{1,13},{5,9},{9,5},{13,1},{2,14},{6,10},... | collective-permute-start | bytes 393224 | tf_op jit(solution)/shard_map/ppermute | solution.py:33
  65.2 12.1 %collective-permute-start.12 = (bf16[32,2048]{1,0:T(8,128)(2,1)S(1)}, bf16[32,2048]{1,0:T(8,128)(2,1)S(1)}, u32[]{:S(2)}, u32[]{:S(2)}) collective-permute-start(bf16[32,2048]{1,0:T(8,128)(2,1)S(1)} %get-tuple-element.37), channel_id=1, source_target_pairs={{0,4},{4,0},{8,12},{12,8},{1,5},{5,1},{9,13},{13,9},{2,6},{6,2},{1... | collective-permute-start | bytes 393224 | tf_op jit(solution)/shard_map/ppermute | solution.py:33
  66.3 12.2 %collective-permute-start.11 = (bf16[32,2048]{1,0:T(8,128)(2,1)S(1)}, bf16[32,2048]{1,0:T(8,128)(2,1)S(1)}, u32[]{:S(2)}, u32[]{:S(2)}) collective-permute-start(bf16[32,2048]{1,0:T(8,128)(2,1)S(1)} %get-tuple-element.38), channel_id=1, source_target_pairs={{0,8},{4,12},{8,0},{12,4},{1,9},{5,13},{9,1},{13,5},{2,10},{6,14},... | collective-permute-start | bytes 393224 | tf_op jit(solution)/shard_map/ppermute | solution.py:33
  72.8 10.3 %collective-permute-start.16 = (bf16[32,2048]{1,0:T(8,128)(2,1)S(1)}, bf16[32,2048]{1,0:T(8,128)(2,1)S(1)}, u32[]{:S(2)}, u32[]{:S(2)}) collective-permute-start(bf16[32,2048]{1,0:T(8,128)(2,1)S(1)} %get-tuple-element.31), channel_id=1, source_target_pairs={{0,4},{4,0},{8,12},{12,8},{1,5},{5,1},{9,13},{13,9},{2,6},{6,2},{1... | collective-permute-start | bytes 393224 | tf_op jit(solution)/shard_map/ppermute | solution.py:33
  74.2 12.9 %collective-permute-start.15 = (bf16[32,2048]{1,0:T(8,128)(2,1)S(1)}, bf16[32,2048]{1,0:T(8,128)(2,1)S(1)}, u32[]{:S(2)}, u32[]{:S(2)}) collective-permute-start(bf16[32,2048]{1,0:T(8,128)(2,1)S(1)} %get-tuple-element.32), channel_id=1, source_target_pairs={{0,8},{4,12},{8,0},{12,4},{1,9},{5,13},{9,1},{13,5},{2,10},{6,14},... | collective-permute-start | bytes 393224 | tf_op jit(solution)/shard_map/ppermute | solution.py:33
  76.0 11.1 %collective-permute-start.14 = (bf16[32,2048]{1,0:T(8,128)(2,1)S(1)}, bf16[32,2048]{1,0:T(8,128)(2,1)S(1)}, u32[]{:S(2)}, u32[]{:S(2)}) collective-permute-start(bf16[32,2048]{1,0:T(8,128)(2,1)S(1)} %get-tuple-element.33), channel_id=1, source_target_pairs={{0,12},{4,8},{8,4},{12,0},{1,13},{5,9},{9,5},{13,1},{2,14},{6,10},... | collective-permute-start | bytes 393224 | tf_op jit(solution)/shard_map/ppermute | solution.py:33

commit v6 on v5

--- a/solution.py
+++ b/solution.py
@@ -292,8 +292,8 @@
     crossed = swap(sum_b, "blk", n, 2)
     other = (first + dot(far_a, far_far)).astype(BF16)
     mine = dot(near_a, near_near)
+    mine = mine + dot(far_a, far_near)
     early = mine
-    mine = mine + dot(far_a, far_near)
     mine_a = add(mine, swap(other, "pair", 2, 1)).astype(BF16)
 
     crossed = after(crossed, other, early)

time: 88.1 us -> 88.1 us (level)
  transfers between devices with their start and end apart: 17 -> 17, of which waited for: 12 -> 13; matrix products, arithmetic and copies ran while one was open for 9% -> 9% of each run, Pallas kernels for 17% -> 17%
where the time goes in v6:
time: 88.1 us; the launch traced here: 88 us
  waiting for transfers between devices  31.6 us (36%)
  starting transfers between devices  23.2 us (26%)
  Pallas kernels  19.5 us (22%)
  matrix products  7.38 us (8%)
  blocking collectives  5.11 us (6%)
    ppermute x17, waiting for transfers between devices, swap(): return lax.ppermute(x, axis, [(i, i ^ flip) for i in range(size)])  31.6 us
    ppermute x17, starting transfers between devices, swap(): return lax.ppermute(x, axis, [(i, i ^ flip) for i in range(size)])  23.2 us
    dot_general x9, matrix products, dot(): return jnp.dot(x, w, preferred_element_type=F32)  7.38 us
    pallas_call x2, Pallas kernels, out_projection(): pl.pallas_call(functools.partial(out_kernel, pieces, near), out_shape=[ja...  6.52 us
    pallas_call x1, Pallas kernels, down_projection(): pl.pallas_call(functools.partial(down_kernel, pieces), out_shape=jax.Shap...  6.15 us
    pallas_call x1, Pallas kernels, fetch(): pl.pallas_call(fetch_kernel, out_shape=[part] * 4 + [jax.ShapeDtypeStruct...  5.28 us
    all_gather x1, blocking collectives, swapped(): hidden = lax.all_gather(hidden, 'pair', axis=0)  2.64 us
    all_gather x1, blocking collectives, swapped(): lax.all_gather(other, 'pair', axis=0)  2.46 us
  transfers between devices with their start and end apart: 17, of which 13 were waited for; matrix products, arithmetic and copies ran while one was open for 9% of the time, Pallas kernels for 17%

profile of v6, /device:TPU:0, one launch (start us, length us, event | category | flops | bytes accessed | tf_op | source)
XLA Modules:
  0.0 88.0 jit_solution(6440464351823899174)
XLA Ops:
  0.0 3.5 %shard_map.65 = (bf16[4,32,1024]{2,1,0:T(8,128)(2,1)S(1)}, bf16[4,32,1024]{2,1,0:T(8,128)(2,1)S(1)}, f32[1,128]{1,0:T(1,128)}, f32[1,2048]{1,0:T(1,128)}) custom-call(f32[3]{0:T(128)} %scales_hbm.3, bf16[256,2048]{1,0:T(8,128)(2,1)} %ctx_hbm.3, bf16[2048,2048]{1,0:T(8,128)(2,1)} %w_hbm.5, bf16[64,2048]{1,0:T(8,128)(2,1)} %res_hbm.3), custom_call_target="tpu_custom_call" | custom-call | flops 1073741824 | bytes 4194304 | tf_op jit(solution)/shard_map/pallas_call | solution.py:137
  3.5 3.1 %collective-permute-start = (bf16[128,1024]{1,0:T(8,128)(2,1)S(1)}, bf16[128,1024]{1,0:T(8,128)(2,1)S(1)}, u32[]{:S(2)}, u32[]{:S(2)}) collective-permute-start(bf16[128,1024]{1,0:T(8,128)(2,1)S(1)} %bitcast.48), channel_id=1, source_target_pairs={{0,4},{4,0},{8,12},{12,8},{1,5},{5,1},{9,13},{13,9},{2,6},{6,2},{1... | collective-permute-start | bytes 786440 | tf_op jit(solution)/shard_map/ppermute | solution.py:33
  6.6 3.0 %shard_map.64 = (bf16[4,32,1024]{2,1,0:T(8,128)(2,1)S(1)}, bf16[4,32,1024]{2,1,0:T(8,128)(2,1)S(1)}, f32[1,128]{1,0:T(1,128)S(1)}, f32[1,2048]{1,0:T(1,128)S(1)}) custom-call(f32[3]{0:T(128)} %scales_hbm.3, bf16[256,2048]{1,0:T(8,128)(2,1)} %ctx_hbm.3, bf16[2048,2048]{1,0:T(8,128)(2,1)} %w_hbm.5, bf16[64,2048]{1,0:T(8,128)(2,1)} %res_hbm.3), custom_call_target="tpu_custom_call" | custom-call | flops 1073741824 | bytes 4194304 | tf_op jit(solution)/shard_map/pallas_call | solution.py:137
  9.7 4.0 %collective-permute-done = bf16[128,1024]{1,0:T(8,128)(2,1)S(1)} collective-permute-done((bf16[128,1024]{1,0:T(8,128)(2,1)S(1)}, bf16[128,1024]{1,0:T(8,128)(2,1)S(1)}, u32[]{:S(2)}, u32[]{:S(2)}) %collective-permute-start) | collective-permute-done | bytes 262176 | tf_op jit(solution)/shard_map/ppermute | solution.py:33
  13.8 3.1 %collective-permute-start.1 = (bf16[128,1024]{1,0:T(8,128)(2,1)S(1)}, bf16[128,1024]{1,0:T(8,128)(2,1)S(1)}, u32[]{:S(2)}, u32[]{:S(2)}) collective-permute-start(bf16[128,1024]{1,0:T(8,128)(2,1)S(1)} %add_convert_fusion.3.done), channel_id=1, source_target_pairs={{0,8},{4,12},{8,0},{12,4},{1,9},{5,13},{9,1},{13,5},{2,10},{6,14},... | collective-permute-start | bytes 786440 | tf_op jit(solution)/shard_map/ppermute | solution.py:33
  17.0 5.3 %shard_map.66 = (bf16[1024,1792]{1,0:T(8,128)(2,1)S(1)}, bf16[1024,1792]{1,0:T(8,128)(2,1)S(1)}, bf16[1024,1792]{1,0:T(8,128)(2,1)S(1)}, bf16[1024,1792]{1,0:T(8,128)(2,1)S(1)}, f32[8,128]{1,0:T(8,128)S(1)}) custom-call(bf16[2048,3584]{1,0:T(8,128)(2,1)} %w_hbm.6, bf16[128,1024]{1,0:T(8,128)(2,1)S(1)} %add_convert_fusion.3.done), custom_call_target="tpu_custom_call" | custom-call | bytes 1024 | tf_op jit(solution)/shard_map/pallas_call | solution.py:176
  22.3 1.2 %collective-permute-done.2 = bf16[128,1024]{1,0:T(8,128)(2,1)S(1)} collective-permute-done((bf16[128,1024]{1,0:T(8,128)(2,1)S(1)}, bf16[128,1024]{1,0:T(8,128)(2,1)S(1)}, u32[]{:S(2)}, u32[]{:S(2)}) %collective-permute-start.2) | collective-permute-done | bytes 262176 | tf_op jit(solution)/shard_map/ppermute | solution.py:33
  23.6 3.6 %collective-permute-done.1.refs_0_ = bf16[128,1024]{1,0:T(8,128)(2,1)S(1)} collective-permute-done((bf16[128,1024]{1,0:T(8,128)(2,1)S(1)}, bf16[128,1024]{1,0:T(8,128)(2,1)S(1)}, u32[]{:S(2)}, u32[]{:S(2)}) %collective-permute-start.1) | collective-permute-done | bytes 262176 | tf_op jit(solution)/shard_map/ppermute | solution.py:33
  28.6 3.4 %collective-permute-start.7 = (bf16[128,1024]{1,0:T(8,128)(2,1)S(1)}, bf16[128,1024]{1,0:T(8,128)(2,1)S(1)}, u32[]{:S(2)}, u32[]{:S(2)}) collective-permute-start(bf16[128,1024]{1,0:T(8,128)(2,1)S(1)} %shard_map.69), channel_id=1, source_target_pairs={{0,8},{4,12},{8,0},{12,4},{1,9},{5,13},{9,1},{13,5},{2,10},{6,14},... | collective-permute-start | bytes 786440 | tf_op jit(solution)/shard_map/ppermute | solution.py:33
  32.0 5.4 %collective-permute-done.3 = bf16[128,1024]{1,0:T(8,128)(2,1)S(1)} collective-permute-done((bf16[128,1024]{1,0:T(8,128)(2,1)S(1)}, bf16[128,1024]{1,0:T(8,128)(2,1)S(1)}, u32[]{:S(2)}, u32[]{:S(2)}) %collective-permute-start.3) | collective-permute-done | bytes 262176 | tf_op jit(solution)/shard_map/ppermute | solution.py:33
  39.5 2.0 %collective-permute-done.7.refs_0_ = bf16[128,1024]{1,0:T(8,128)(2,1)S(1)} collective-permute-done((bf16[128,1024]{1,0:T(8,128)(2,1)S(1)}, bf16[128,1024]{1,0:T(8,128)(2,1)S(1)}, u32[]{:S(2)}, u32[]{:S(2)}) %collective-permute-start.7) | collective-permute-done | bytes 262176 | tf_op jit(solution)/shard_map/ppermute | solution.py:33
  42.5 1.6 %collective-permute-start.5 = (bf16[128,640]{1,0:T(8,128)(2,1)S(1)}, bf16[128,640]{1,0:T(8,128)(2,1)S(1)}, u32[]{:S(2)}, u32[]{:S(2)}) collective-permute-start(bf16[128,640]{1,0:T(8,128)(2,1)S(1)} %slice.18), channel_id=1, source_target_pairs={{0,2},{2,0},{1,3},{3,1},{4,6},{6,4},{5,7},{7,5},{8,10},{10,8},{9,1... | collective-permute-start | bytes 491528 | tf_op jit(solution)/shard_map/ppermute | solution.py:33
  45.3 3.1 %collective-permute-done.8.refs_0_ = bf16[128,1024]{1,0:T(8,128)(2,1)S(1)} collective-permute-done((bf16[128,1024]{1,0:T(8,128)(2,1)S(1)}, bf16[128,1024]{1,0:T(8,128)(2,1)S(1)}, u32[]{:S(2)}, u32[]{:S(2)}) %collective-permute-start.8) | collective-permute-done | bytes 262176 | tf_op jit(solution)/shard_map/ppermute | solution.py:33
  50.2 2.5 %all-gather = bf16[256,1792]{1,0:T(8,128)(2,1)S(1)} all-gather(bf16[128,1792]{1,0:T(8,128)(2,1)S(1)} %fusion.2), channel_id=2, replica_groups=mesh['groups'=2,'blk'=4,'sub'=2,'pair'=2] {'pair'}, dimensions={0}, use_global_device_ids=true | all-gather | bytes 1376256 | tf_op jit(solution)/shard_map/all_gather | solution.py:310
  54.2 1.5 %collective-permute-start.13 = (bf16[128,1792]{1,0:T(8,128)(2,1)S(1)}, bf16[128,1792]{1,0:T(8,128)(2,1)S(1)}, u32[]{:S(2)}, u32[]{:S(2)}) collective-permute-start(bf16[128,1792]{1,0:T(8,128)(2,1)S(1)} %shard_map.76.own), channel_id=1, source_target_pairs={{0,2},{2,0},{1,3},{3,1},{4,6},{6,4},{5,7},{7,5},{8,10},{10,8},{9,1... | collective-permute-start | bytes 1376264 | tf_op jit(solution)/shard_map/ppermute | solution.py:33
  56.1 6.2 %shard_map.75.refs_1_ = bf16[128,2048]{1,0:T(8,128)(2,1)S(1)} custom-call(bf16[128,3584]{1,0:T(8,128)(2,1)S(1)} %pad_maximum_fusion.hidden, bf16[3584,2048]{1,0:T(8,128)(2,1)} %w_hbm.7), custom_call_target="tpu_custom_call" | custom-call | flops 1879048192 | bytes 14680064 | tf_op jit(solution)/shard_map/pallas_call | solution.py:230
  62.3 2.6 %collective-permute-start.10 = (bf16[32,2048]{1,0:T(8,128)(2,1)S(1)}, bf16[32,2048]{1,0:T(8,128)(2,1)S(1)}, u32[]{:S(2)}, u32[]{:S(2)}) collective-permute-start(bf16[32,2048]{1,0:T(8,128)(2,1)S(1)} %get-tuple-element.36), channel_id=1, source_target_pairs={{0,12},{4,8},{8,4},{12,0},{1,13},{5,9},{9,5},{13,1},{2,14},{6,10},... | collective-permute-start | bytes 393224 | tf_op jit(solution)/shard_map/ppermute | solution.py:33
  67.5 2.6 %all-gather.1 = bf16[256,1792]{1,0:T(8,128)(2,1)S(1)} all-gather(bf16[128,1792]{1,0:T(8,128)(2,1)S(1)} %shard_map.78), channel_id=3, replica_groups=mesh['groups'=2,'blk'=4,'sub'=2,'pair'=2] {'pair'}, dimensions={0}, use_global_device_ids=true | all-gather | bytes 1376256 | tf_op jit(solution)/shard_map/all_gather | solution.py:330
  70.3 2.1 %convolution_convert_fusion.mlp = bf16[128,2048]{1,0:T(8,128)(2,1)S(1)} fusion(bf16[3584,2048]{1,0:T(8,128)(2,1)S(1)} %bitcast.50, bf16[128,1792]{1,0:T(8,128)(2,1)S(1)} %get-tuple-element.28, bf16[128,1792]{1,0:T(8,128)(2,1)S(1)} %get-tuple-element.27), kind=kOutput, calls=%fused_computation.7 | convolution fusion | flops 1881145344 | bytes 16121856 | tf_op jit(solution)/shard_map/dot_general | solution.py:41
  72.4 1.8 %collective-permute-start.16 = (bf16[32,2048]{1,0:T(8,128)(2,1)S(1)}, bf16[32,2048]{1,0:T(8,128)(2,1)S(1)}, u32[]{:S(2)}, u32[]{:S(2)}) collective-permute-start(bf16[32,2048]{1,0:T(8,128)(2,1)S(1)} %get-tuple-element.31), channel_id=1, source_target_pairs={{0,4},{4,0},{8,12},{12,8},{1,5},{5,1},{9,13},{13,9},{2,6},{6,2},{1... | collective-permute-start | bytes 393224 | tf_op jit(solution)/shard_map/ppermute | solution.py:33
  74.2 1.4 %collective-permute-start.15 = (bf16[32,2048]{1,0:T(8,128)(2,1)S(1)}, bf16[32,2048]{1,0:T(8,128)(2,1)S(1)}, u32[]{:S(2)}, u32[]{:S(2)}) collective-permute-start(bf16[32,2048]{1,0:T(8,128)(2,1)S(1)} %get-tuple-element.32), channel_id=1, source_target_pairs={{0,8},{4,12},{8,0},{12,4},{1,9},{5,13},{9,1},{13,5},{2,10},{6,14},... | collective-permute-start | bytes 393224 | tf_op jit(solution)/shard_map/ppermute | solution.py:33
  75.6 1.3 %collective-permute-start.14 = (bf16[32,2048]{1,0:T(8,128)(2,1)S(1)}, bf16[32,2048]{1,0:T(8,128)(2,1)S(1)}, u32[]{:S(2)}, u32[]{:S(2)}) collective-permute-start(bf16[32,2048]{1,0:T(8,128)(2,1)S(1)} %get-tuple-element.33), channel_id=1, source_target_pairs={{0,12},{4,8},{8,4},{12,0},{1,13},{5,9},{9,5},{13,1},{2,14},{6,10},... | collective-permute-start | bytes 393224 | tf_op jit(solution)/shard_map/ppermute | solution.py:33
  77.7 4.6 %collective-permute-done.16.third = bf16[32,2048]{1,0:T(8,128)(2,1)S(1)} collective-permute-done((bf16[32,2048]{1,0:T(8,128)(2,1)S(1)}, bf16[32,2048]{1,0:T(8,128)(2,1)S(1)}, u32[]{:S(2)}, u32[]{:S(2)}) %collective-permute-start.16) | collective-permute-done | bytes 131104 | tf_op jit(solution)/shard_map/ppermute | solution.py:33
  82.3 4.8 %collective-permute-done.15.second = bf16[32,2048]{1,0:T(8,128)(2,1)S(1)} collective-permute-done((bf16[32,2048]{1,0:T(8,128)(2,1)S(1)}, bf16[32,2048]{1,0:T(8,128)(2,1)S(1)}, u32[]{:S(2)}, u32[]{:S(2)}) %collective-permute-start.15) | collective-permute-done | bytes 131104 | tf_op jit(solution)/shard_map/ppermute | solution.py:33
  (61 shorter events, 13.9 us)
Async XLA Ops:
  3.5 10.2 %collective-permute-start = (bf16[128,1024]{1,0:T(8,128)(2,1)S(1)}, bf16[128,1024]{1,0:T(8,128)(2,1)S(1)}, u32[]{:S(2)}, u32[]{:S(2)}) collective-permute-start(bf16[128,1024]{1,0:T(8,128)(2,1)S(1)} %bitcast.48), channel_id=1, source_target_pairs={{0,4},{4,0},{8,12},{12,8},{1,5},{5,1},{9,13},{13,9},{2,6},{6,2},{1... | collective-permute-start | bytes 786440 | tf_op jit(solution)/shard_map/ppermute | solution.py:33
  9.6 13.8 %collective-permute-start.2 = (bf16[128,1024]{1,0:T(8,128)(2,1)S(1)}, bf16[128,1024]{1,0:T(8,128)(2,1)S(1)}, u32[]{:S(2)}, u32[]{:S(2)}) collective-permute-start(bf16[128,1024]{1,0:T(8,128)(2,1)S(1)} %shard_map.67), channel_id=1, source_target_pairs={{0,4},{4,0},{8,12},{12,8},{1,5},{5,1},{9,13},{13,9},{2,6},{6,2},{1... | collective-permute-start | bytes 786440 | tf_op jit(solution)/shard_map/ppermute | solution.py:33
  13.8 13.3 %collective-permute-start.1 = (bf16[128,1024]{1,0:T(8,128)(2,1)S(1)}, bf16[128,1024]{1,0:T(8,128)(2,1)S(1)}, u32[]{:S(2)}, u32[]{:S(2)}) collective-permute-start(bf16[128,1024]{1,0:T(8,128)(2,1)S(1)} %add_convert_fusion.3.done), channel_id=1, source_target_pairs={{0,8},{4,12},{8,0},{12,4},{1,9},{5,13},{9,1},{13,5},{2,10},{6,14},... | collective-permute-start | bytes 786440 | tf_op jit(solution)/shard_map/ppermute | solution.py:33
  27.2 10.2 %collective-permute-start.3 = (bf16[128,1024]{1,0:T(8,128)(2,1)S(1)}, bf16[128,1024]{1,0:T(8,128)(2,1)S(1)}, u32[]{:S(2)}, u32[]{:S(2)}) collective-permute-start(bf16[128,1024]{1,0:T(8,128)(2,1)S(1)} %add_convert_fusion.2), channel_id=1, source_target_pairs={{0,4},{4,0},{8,12},{12,8},{1,5},{5,1},{9,13},{13,9},{2,6},{6,2},{1... | collective-permute-start | bytes 786440 | tf_op jit(solution)/shard_map/ppermute | solution.py:33
  28.6 13.0 %collective-permute-start.7 = (bf16[128,1024]{1,0:T(8,128)(2,1)S(1)}, bf16[128,1024]{1,0:T(8,128)(2,1)S(1)}, u32[]{:S(2)}, u32[]{:S(2)}) collective-permute-start(bf16[128,1024]{1,0:T(8,128)(2,1)S(1)} %shard_map.69), channel_id=1, source_target_pairs={{0,8},{4,12},{8,0},{12,4},{1,9},{5,13},{9,1},{13,5},{2,10},{6,14},... | collective-permute-start | bytes 786440 | tf_op jit(solution)/shard_map/ppermute | solution.py:33
  38.1 4.2 %collective-permute-start.4 = (bf16[128,1792]{1,0:T(8,128)(2,1)S(1)}, bf16[128,1792]{1,0:T(8,128)(2,1)S(1)}, u32[]{:S(2)}, u32[]{:S(2)}) collective-permute-start(bf16[128,1792]{1,0:T(8,128)(2,1)S(1)} %fusion.1.refs_1_), channel_id=1, source_target_pairs={{0,1},{1,0},{2,3},{3,2},{4,5},{5,4},{6,7},{7,6},{8,9},{9,8},{10,11... | collective-permute-start | bytes 1376264 | tf_op jit(solution)/shard_map/ppermute | solution.py:33
  41.6 6.8 %collective-permute-start.8 = (bf16[128,1024]{1,0:T(8,128)(2,1)S(1)}, bf16[128,1024]{1,0:T(8,128)(2,1)S(1)}, u32[]{:S(2)}, u32[]{:S(2)}) collective-permute-start(bf16[128,1024]{1,0:T(8,128)(2,1)S(1)} %add_convert_fusion.1.near), channel_id=1, source_target_pairs={{0,4},{4,0},{8,12},{12,8},{1,5},{5,1},{9,13},{13,9},{2,6},{6,2},{1... | collective-permute-start | bytes 786440 | tf_op jit(solution)/shard_map/ppermute | solution.py:33
  42.5 7.1 %collective-permute-start.5 = (bf16[128,640]{1,0:T(8,128)(2,1)S(1)}, bf16[128,640]{1,0:T(8,128)(2,1)S(1)}, u32[]{:S(2)}, u32[]{:S(2)}) collective-permute-start(bf16[128,640]{1,0:T(8,128)(2,1)S(1)} %slice.18), channel_id=1, source_target_pairs={{0,2},{2,0},{1,3},{3,1},{4,6},{6,4},{5,7},{7,5},{8,10},{10,8},{9,1... | collective-permute-start | bytes 491528 | tf_op jit(solution)/shard_map/ppermute | solution.py:33
  44.7 9.0 %collective-permute-start.6 = (bf16[128,1152]{1,0:T(8,128)(2,1)S(1)}, bf16[128,1152]{1,0:T(8,128)(2,1)S(1)}, u32[]{:S(2)}, u32[]{:S(2)}) collective-permute-start(bf16[128,1152]{1,0:T(8,128)(2,1)S(1)} %slice.19), channel_id=1, source_target_pairs={{0,2},{2,0},{1,3},{3,1},{4,6},{6,4},{5,7},{7,5},{8,10},{10,8},{9,1... | collective-permute-start | bytes 884744 | tf_op jit(solution)/shard_map/ppermute | solution.py:33
  54.1 1.9 %collective-permute-start.9 = (bf16[128,1792]{1,0:T(8,128)(2,1)S(1)}, bf16[128,1792]{1,0:T(8,128)(2,1)S(1)}, u32[]{:S(2)}, u32[]{:S(2)}) collective-permute-start(bf16[128,1792]{1,0:T(8,128)(2,1)S(1)} %shard_map.74), channel_id=1, source_target_pairs={{0,1},{1,0},{2,3},{3,2},{4,5},{5,4},{6,7},{7,6},{8,9},{9,8},{10,11... | collective-permute-start | bytes 1376264 | tf_op jit(solution)/shard_map/ppermute | solution.py:33
  54.2 16.0 %slice-start = ((s8[14680064]{0:T(1024)(128)(4,1)}), s8[4194304]{0:T(1024)(128)(4,1)S(1)}, s32[]{:S(2)}) async-start(s8[14680064]{0:T(1024)(128)(4,1)} %bitcast.49), calls=%async_computation | async-start | bytes 8388608
  54.2 12.9 %collective-permute-start.13 = (bf16[128,1792]{1,0:T(8,128)(2,1)S(1)}, bf16[128,1792]{1,0:T(8,128)(2,1)S(1)}, u32[]{:S(2)}, u32[]{:S(2)}) collective-permute-start(bf16[128,1792]{1,0:T(8,128)(2,1)S(1)} %shard_map.76.own), channel_id=1, source_target_pairs={{0,2},{2,0},{1,3},{3,1},{4,6},{6,4},{5,7},{7,5},{8,10},{10,8},{9,1... | collective-permute-start | bytes 1376264 | tf_op jit(solution)/shard_map/ppermute | solution.py:33
  56.1 14.1 %slice-start.1 = ((s8[14680064]{0:T(1024)(128)(4,1)}), s8[4194304]{0:T(1024)(128)(4,1)S(1)}, s32[]{:S(2)}) async-start(s8[14680064]{0:T(1024)(128)(4,1)} %bitcast.49), calls=%async_computation.1 | async-start | bytes 8388608
  56.1 14.1 %slice-start.2 = ((s8[14680064]{0:T(1024)(128)(4,1)}), s8[4194304]{0:T(1024)(128)(4,1)S(1)}, s32[]{:S(2)}) async-start(s8[14680064]{0:T(1024)(128)(4,1)} %bitcast.49), calls=%async_computation.2 | async-start | bytes 8388608
  56.1 14.1 %slice-start.3 = ((s8[14680064]{0:T(1024)(128)(4,1)}), s8[2097152]{0:T(1024)(128)(4,1)S(1)}, s32[]{:S(2)}) async-start(s8[14680064]{0:T(1024)(128)(4,1)} %bitcast.49), calls=%async_computation.3 | async-start | bytes 4194304
  62.3 13.3 %collective-permute-start.10 = (bf16[32,2048]{1,0:T(8,128)(2,1)S(1)}, bf16[32,2048]{1,0:T(8,128)(2,1)S(1)}, u32[]{:S(2)}, u32[]{:S(2)}) collective-permute-start(bf16[32,2048]{1,0:T(8,128)(2,1)S(1)} %get-tuple-element.36), channel_id=1, source_target_pairs={{0,12},{4,8},{8,4},{12,0},{1,13},{5,9},{9,5},{13,1},{2,14},{6,10},... | collective-permute-start | bytes 393224 | tf_op jit(solution)/shard_map/ppermute | solution.py:33
  64.9 12.0 %collective-permute-start.12 = (bf16[32,2048]{1,0:T(8,128)(2,1)S(1)}, bf16[32,2048]{1,0:T(8,128)(2,1)S(1)}, u32[]{:S(2)}, u32[]{:S(2)}) collective-permute-start(bf16[32,2048]{1,0:T(8,128)(2,1)S(1)} %get-tuple-element.37), channel_id=1, source_target_pairs={{0,4},{4,0},{8,12},{12,8},{1,5},{5,1},{9,13},{13,9},{2,6},{6,2},{1... | collective-permute-start | bytes 393224 | tf_op jit(solution)/shard_map/ppermute | solution.py:33
  65.8 11.9 %collective-permute-start.11 = (bf16[32,2048]{1,0:T(8,128)(2,1)S(1)}, bf16[32,2048]{1,0:T(8,128)(2,1)S(1)}, u32[]{:S(2)}, u32[]{:S(2)}) collective-permute-start(bf16[32,2048]{1,0:T(8,128)(2,1)S(1)} %get-tuple-element.38), channel_id=1, source_target_pairs={{0,8},{4,12},{8,0},{12,4},{1,9},{5,13},{9,1},{13,5},{2,10},{6,14},... | collective-permute-start | bytes 393224 | tf_op jit(solution)/shard_map/ppermute | solution.py:33
  72.4 9.9 %collective-permute-start.16 = (bf16[32,2048]{1,0:T(8,128)(2,1)S(1)}, bf16[32,2048]{1,0:T(8,128)(2,1)S(1)}, u32[]{:S(2)}, u32[]{:S(2)}) collective-permute-start(bf16[32,2048]{1,0:T(8,128)(2,1)S(1)} %get-tuple-element.31), channel_id=1, source_target_pairs={{0,4},{4,0},{8,12},{12,8},{1,5},{5,1},{9,13},{13,9},{2,6},{6,2},{1... | collective-permute-start | bytes 393224 | tf_op jit(solution)/shard_map/ppermute | solution.py:33
  74.2 12.9 %collective-permute-start.15 = (bf16[32,2048]{1,0:T(8,128)(2,1)S(1)}, bf16[32,2048]{1,0:T(8,128)(2,1)S(1)}, u32[]{:S(2)}, u32[]{:S(2)}) collective-permute-start(bf16[32,2048]{1,0:T(8,128)(2,1)S(1)} %get-tuple-element.32), channel_id=1, source_target_pairs={{0,8},{4,12},{8,0},{12,4},{1,9},{5,13},{9,1},{13,5},{2,10},{6,14},... | collective-permute-start | bytes 393224 | tf_op jit(solution)/shard_map/ppermute | solution.py:33
  75.6 11.5 %collective-permute-start.14 = (bf16[32,2048]{1,0:T(8,128)(2,1)S(1)}, bf16[32,2048]{1,0:T(8,128)(2,1)S(1)}, u32[]{:S(2)}, u32[]{:S(2)}) collective-permute-start(bf16[32,2048]{1,0:T(8,128)(2,1)S(1)} %get-tuple-element.33), channel_id=1, source_target_pairs={{0,12},{4,8},{8,4},{12,0},{1,13},{5,9},{9,5},{13,1},{2,14},{6,10},... | collective-permute-start | bytes 393224 | tf_op jit(solution)/shard_map/ppermute | solution.py:33
